TPU v7x, 32 devices: a whole 2x2x4 slice. The times are simulated.
32 devices in a mesh: pipe: 2 (over x), ctx: 8 (over z, y), tp: 2 (over core).
Axes of the slice: x: 2, y: 2, z: 4, core: 2. Of those that a mesh axis runs over, the one named last changes fastest.
Arguments:
- qkv_proj: bfloat16 [2, 3, 1024, 8192], P('pipe', None, 'ctx', 'tp'), may hold values from -6 to 6
- cotangent: bfloat16 [2, 1024, 8192], P('pipe', 'ctx', 'tp'), may hold values from -6 to 6
- block_dest: int32 [2, 64], replicated, may hold values from 0 to 63, as said below
- doc_start: int32 [2, 1024], P('pipe', 'ctx'), may hold values 0 or 1
- mr_filter: bfloat16 [2, 512, 128], P('pipe', 'tp'), may hold values from -0.5 to 0.5
Outputs:
- input_grads: bfloat16 [2, 3, 1024, 8192], P('pipe', None, ('ctx', 'tp'))
Inputs may be any that keep to these rules, and one draw needn't show every extreme that they name: For each section p, block_dest[p] is a permutation of 0 .. 63. Entry d * 8 + b belongs to block b of ctx index d, and its value lies in b * 8 .. b * 8 + 7: every ctx index sends its block b to the part of the sequence held by ctx index b.
All inputs are finite; a program needn't handle non-finite values. No bound on the sum of `doc_start` on one device may be relied on, other than what follows from the above.
Results may differ from a plain program's by a relative error of at most 0.0049.
Values may be sent and summed in bfloat16 or wider, within the bound.
No kernel may reach another device: no remote copies, remote signals or barrier semaphores. Data moves between devices by JAX's collectives and lax.ppermute only.
A program may use at most 128 MiB of HBM per device.

v0:
```python
import functools
import math

import jax
import jax.numpy as jnp
from jax import lax
from jax.experimental import pallas as pl
from jax.experimental.pallas import tpu as pltpu
from jax.sharding import PartitionSpec as P

LANES = 128
CHUNKS = 2
MARK_ROWS = 16
VMEM_BYTES = 60 * 1024 * 1024
F32 = jnp.float32
BF16 = jnp.bfloat16


def params():
    return pltpu.CompilerParams(vmem_limit_bytes=VMEM_BYTES)


def whole_block(*shape):
    return pl.BlockSpec(shape, lambda _: (0,) * len(shape))


def smem():
    return pl.BlockSpec(memory_space=pltpu.SMEM)


def sending_order(peers):
    half = peers // 2
    return [k for i in range(half) for k in (half + i, i)]


def multiply_kernel(stacked, marked, sided, *refs):
    refs = list(refs)
    proj_ref, grad_ref = refs[:2]
    marks_ref = refs[2] if marked else None
    outs = refs[3 if marked else 2 :]
    if sided:
        side_ref = outs.pop()
        side_ref[0] = proj_ref[0, 1]
        side_ref[1] = proj_ref[0, 2]
        side_ref[2] = grad_ref[0]
    rows = grad_ref.shape[1]
    width = outs[0].shape[-1]
    me = lax.axis_index("ctx")
    if stacked:
        peers = outs[0].shape[0]
        places = [(peer, outs[0].at[peer]) for peer in range(peers)]
    else:
        peers = len(outs)
        places = [(me ^ k, out_ref) for k, out_ref in zip(sending_order(peers), outs)]
    span = peers * width
    begin = grad_ref.shape[2] - span
    for peer, out_ref in places:
        lanes = pl.ds(pl.multiple_of(begin + peer * width, LANES), width)
        query = proj_ref[0, 0, :, lanes].astype(F32)
        key_rows = proj_ref[0, 1, :, lanes].astype(F32)
        value = proj_ref[0, 2, :, lanes].astype(F32)
        grad_in = grad_ref[0, :, lanes].astype(F32)
        out_ref[:rows, :] = (key_rows * value).astype(BF16)
        out_ref[rows : 2 * rows, :] = (grad_in * query).astype(BF16)
        if marked:
            extra = out_ref.shape[0] - 2 * rows
            marks = marks_ref[...].astype(F32)
            out_ref[2 * rows :, :LANES] = jnp.broadcast_to(marks, (extra, LANES)).astype(BF16)
            if width > LANES:
                out_ref[2 * rows :, LANES:] = jnp.zeros((extra, width - LANES), BF16)


def multiply(index, width, peers, qkv_proj, cotangent, marks, stacked, sided):
    _, rows, channels = cotangent.shape
    span = peers * width
    taken = channels if sided else span
    block = 0 if sided else index
    marked = marks is not None
    in_specs = [
        pl.BlockSpec((1, 3, rows, taken), lambda _: (0, 0, 0, block)),
        pl.BlockSpec((1, rows, taken), lambda _: (0, 0, block)),
    ]
    args = [qkv_proj, cotangent]
    if marked:
        in_specs.append(whole_block(*marks.shape))
        args.append(marks)
    out = (2 * rows + (MARK_ROWS if marked else 0), width)
    shapes = [(peers,) + out] if stacked else [out] * peers
    if sided:
        shapes.append((3, rows, channels))
    return pl.pallas_call(
        functools.partial(multiply_kernel, stacked, marked, sided),
        out_shape=[jax.ShapeDtypeStruct(shape, BF16) for shape in shapes],
        in_specs=in_specs,
        out_specs=[whole_block(*shape) for shape in shapes],
        compiler_params=params(),
        cost_estimate=pl.CostEstimate(
            flops=2 * rows * span, bytes_accessed=14 * rows * taken, transcendentals=0
        ),
        grid=(1,),
        name="multiply",
    )(*args)


def first_row(meta_ref, peers, source, block):
    block_rows = LANES // peers
    row = meta_ref[source * peers + block] * block_rows
    return pl.multiple_of(row, block_rows)


def masks_kernel(me_at, meta_ref, *refs):
    marks_refs, (out_ref, seq, across) = refs[:-3], refs[-3:]
    peers = len(marks_refs)
    tile = LANES
    block_rows = tile // peers
    me = meta_ref[me_at]
    row_ids = lax.broadcasted_iota(jnp.int32, (tile, tile), 0)
    lane_ids = lax.broadcasted_iota(jnp.int32, (tile, tile), 1)
    eye = (row_ids == lane_ids).astype(BF16)
    lower = (row_ids >= lane_ids).astype(BF16)
    for k, marks_ref in zip(sending_order(peers), marks_refs):
        spread = lax.dot_general(
            eye, marks_ref[...], (((1,), (1,)), ((), ())), preferred_element_type=F32
        )
        column = jnp.broadcast_to(spread[:, :1], (tile, tile))
        for block in range(peers):
            first = first_row(meta_ref, peers, me ^ k, block)
            seq[pl.ds(first, block_rows), :] = column[
                block * block_rows : (block + 1) * block_rows
            ]
    carry = jnp.zeros((1, tile), F32)
    for b in range(peers):
        rows = slice(b * tile, (b + 1) * tile)
        count = (
            jnp.dot(lower, seq[rows, :].astype(BF16), preferred_element_type=F32) + carry
        )
        carry = count[tile - 1 :, :]
        seq[rows, :] = count
        across[rows, :] = count.T
    for b in range(peers):
        here = seq[b * tile : (b + 1) * tile, :]

        def same(other):
            return (here == across[other * tile : (other + 1) * tile, :]).astype(F32).astype(BF16)

        out_ref[b, 0, :, :tile] = same(max(b - 1, 0))
        out_ref[b, 0, :, tile:] = same(b)
        out_ref[b, 1, :, :tile] = same(b)
        out_ref[b, 1, :, tile:] = same(min(b + 1, peers - 1))


def document_masks(me_at, meta, received, mark_rows):
    peers = len(received)
    tile = LANES
    last = received[0].shape[0] // mark_rows - 1
    out = (peers, 2, tile, 2 * tile)
    return pl.pallas_call(
        functools.partial(masks_kernel, me_at),
        out_shape=jax.ShapeDtypeStruct(out, BF16),
        in_specs=[smem()] + [pl.BlockSpec((mark_rows, tile), lambda _: (last, 0))] * peers,
        out_specs=whole_block(*out),
        scratch_shapes=[
            pltpu.VMEM((peers * tile, tile), F32),
            pltpu.VMEM((peers * tile, tile), F32),
        ],
        compiler_params=params(),
        cost_estimate=pl.CostEstimate(
            flops=8 * peers * tile * tile, bytes_accessed=8 * peers * tile * tile, transcendentals=0
        ),
        grid=(1,),
        name="masks",
    )(meta, *received)


def conv_kernel(group_size, me_at, peers, meta_ref, mask_ref, base_ref, *refs):
    rows32, rows16, toep = refs[-3:]
    recv, outs = refs[: -3 - peers], refs[-3 - peers : -3]
    me = meta_ref[me_at]
    if len(recv) == 1:
        arrivals = [(source, recv[0].at[source]) for source in range(peers)]
    else:
        arrivals = [(me ^ k, recv_ref) for k, recv_ref in zip(sending_order(peers), recv)]
    tile = LANES
    width = outs[0].shape[1]
    groups = base_ref.shape[1]
    block_rows = tile // peers
    rows16[0, :tile, :] = jnp.zeros((tile, width), BF16)
    rows16[1, peers * tile :, :] = jnp.zeros((tile, width), BF16)

    for half in range(2):
        for group in range(groups):
            base = jnp.broadcast_to(base_ref[half, group : group + 1, :], (tile, 2 * tile))
            toep[half, group] = pltpu.roll(base, 0, 1, stride=1, stride_axis=0).astype(BF16)

    for source, recv_ref in arrivals:
        firsts = [first_row(meta_ref, peers, source, block) for block in range(peers)]
        for half in range(2):
            arrived = recv_ref[half * tile : (half + 1) * tile, :].astype(F32)
            for block in range(peers):
                rows32[half, pl.ds(firsts[block], block_rows), :] = arrived[
                    block * block_rows : (block + 1) * block_rows
                ]
    rows16[0, tile:, :] = rows32[0].astype(BF16)
    rows16[1, : peers * tile, :] = rows32[1].astype(BF16)

    tile_groups = tile // group_size
    lane_group = lax.broadcasted_iota(jnp.int32, (tile, tile), 1) // group_size

    def one_tile(b, carry):
        first = pl.multiple_of(b * tile, tile)
        for half in range(2):
            mask = mask_ref[b, half]
            for sub in range(width // tile):
                lanes = slice(sub * tile, (sub + 1) * tile)
                window = rows16[half, pl.ds(first, 2 * tile), lanes]
                total = jnp.zeros((tile, tile), F32)
                for group in range(tile_groups):
                    part = jnp.dot(
                        toep[half, sub * tile_groups + group] * mask,
                        window,
                        preferred_element_type=F32,
                    )
                    total = jnp.where(lane_group == group, part, total)
                rows32[half, pl.ds(first, tile), lanes] = total
        return carry

    lax.fori_loop(0, peers, one_tile, 0)

    for k, out_ref in zip(sending_order(peers), outs):
        firsts = [first_row(meta_ref, peers, me ^ k, block) for block in range(peers)]
        for half in range(2):
            pieces = [rows32[half, pl.ds(first, block_rows), :] for first in firsts]
            out_ref[half * tile : (half + 1) * tile, :] = jnp.concatenate(pieces, axis=0).astype(
                BF16
            )


def convolve(group_size, me_at, meta, received, masks, bases):
    peers = masks.shape[0]
    tile = LANES
    width = received[0].shape[-1]
    groups = bases.shape[1]
    out = (2 * tile, width)
    return pl.pallas_call(
        functools.partial(conv_kernel, group_size, me_at, peers),
        out_shape=[jax.ShapeDtypeStruct(out, BF16)] * peers,
        in_specs=[smem(), whole_block(*masks.shape), whole_block(*bases.shape)]
        + [whole_block(*r.shape) for r in received],
        out_specs=[whole_block(*out)] * peers,
        scratch_shapes=[
            pltpu.VMEM((2, peers * tile, width), F32),
            pltpu.VMEM((2, (peers + 1) * tile, width), BF16),
            pltpu.VMEM((2, groups, tile, 2 * tile), BF16),
        ],
        compiler_params=params(),
        cost_estimate=pl.CostEstimate(
            flops=8 * groups * peers * tile**3,
            bytes_accessed=8 * peers * tile * width + 4 * peers * tile**2,
            transcendentals=0,
        ),
        grid=(1,),
        name="convolve",
    )(meta, masks, bases, *received)


def gradients_kernel(me_at, tp_at, meta_ref, side_ref, *refs):
    result_ref, cross_ref = refs[-2:]
    peers = count_backs(refs)
    rows = side_ref.shape[1]
    width = side_ref.shape[2] // peers
    part = cross_ref.shape[1]
    me = meta_ref[me_at]
    mine = meta_ref[tp_at]
    for out_ref, index in ((cross_ref, 1 - mine), (result_ref.at[0], mine)):
        first = pl.multiple_of(index * part, part)
        at = pl.ds(first, part)
        later = pl.ds(pl.multiple_of(first + rows, part), part)
        for k, back_ref in zip(sending_order(peers), refs):
            lanes = pl.ds(pl.multiple_of((me ^ k) * width, LANES), width)
            medium = back_ref[at, :].astype(F32)
            mixed_grad = back_ref[later, :].astype(F32)
            key_rows = side_ref[0, at, lanes].astype(F32)
            value = side_ref[1, at, lanes].astype(F32)
            grad_in = side_ref[2, at, lanes].astype(F32)
            out_ref[0, :, lanes] = (grad_in * medium).astype(BF16)
            out_ref[1, :, lanes] = (mixed_grad * value).astype(BF16)
            out_ref[2, :, lanes] = (mixed_grad * key_rows).astype(BF16)


def count_backs(refs):
    return sum(1 for ref in refs if len(ref.shape) == 2)


def fixed(shape):
    return pl.BlockSpec(shape, lambda _, meta_ref: (0,) * len(shape))


def result_block(shape, chunk, chunks, tp_at, mine):
    def place(_, meta_ref):
        owner = meta_ref[tp_at] if mine else 1 - meta_ref[tp_at]
        return (0, 0, 0, owner * chunks + chunk)

    return pl.BlockSpec((1,) + shape, place)


def gradients(chunk, chunks, me_at, tp_at, tp_count, meta, backs, side, result):
    peers = len(backs)
    _, rows, channels = side.shape
    span = channels // chunks
    out = (3, rows // tp_count, span)
    whole = (1, 3, rows // tp_count, channels * tp_count)
    in_specs = [pl.BlockSpec((3, rows, span), lambda _, meta_ref: (0, 0, chunk))]
    in_specs += [fixed(backs[0].shape)] * peers
    args = [meta, side, *backs]
    aliases = {}
    if result is not None:
        aliases = {len(args): 0}
        args.append(result)
        in_specs.append(pl.BlockSpec(memory_space=pl.ANY))
    return pl.pallas_call(
        functools.partial(gradients_kernel, me_at, tp_at),
        out_shape=[jax.ShapeDtypeStruct(whole, BF16), jax.ShapeDtypeStruct(out, BF16)],
        grid_spec=pltpu.PrefetchScalarGridSpec(
            num_scalar_prefetch=1,
            grid=(1,),
            in_specs=in_specs,
            out_specs=[result_block(out, chunk, chunks, tp_at, True), fixed(out)],
        ),
        input_output_aliases=aliases,
        compiler_params=params(),
        cost_estimate=pl.CostEstimate(
            flops=3 * rows * span, bytes_accessed=16 * rows * span, transcendentals=0
        ),
        name="gradients",
    )(*args)


def place_kernel(meta_ref, cross_ref, held_ref, result_ref):
    result_ref[0] = cross_ref[...]


def place(chunk, chunks, tp_at, meta, cross, result):
    return pl.pallas_call(
        place_kernel,
        out_shape=jax.ShapeDtypeStruct(result.shape, BF16),
        grid_spec=pltpu.PrefetchScalarGridSpec(
            num_scalar_prefetch=1,
            grid=(1,),
            in_specs=[fixed(cross.shape), pl.BlockSpec(memory_space=pl.ANY)],
            out_specs=result_block(cross.shape, chunk, chunks, tp_at, False),
        ),
        input_output_aliases={2: 0},
        compiler_params=params(),
        cost_estimate=pl.CostEstimate(
            flops=0, bytes_accessed=4 * math.prod(cross.shape), transcendentals=0
        ),
        name="place",
    )(meta, cross, result)


def exchanged(arrays):
    peers = len(arrays)
    return [
        lax.ppermute(array, "ctx", [(i, i ^ k) for i in range(peers)]) if k else array
        for k, array in zip(sending_order(peers), arrays)
    ]


def back_to_previous(arrays):
    peers = len(arrays)
    pipes = lax.axis_size("pipe")
    return [
        lax.ppermute(
            array,
            ("pipe", "ctx"),
            [
                (pipe * peers + i, (pipe - 1) % pipes * peers + (i ^ k))
                for pipe in range(pipes)
                for i in range(peers)
            ],
        )
        for k, array in zip(sending_order(peers), arrays)
    ]


def shards(qkv_proj, cotangent, block_dest, doc_start, mr_filter):
    peers = lax.axis_size("ctx")
    pipes = lax.axis_size("pipe")
    tp_count = lax.axis_size("tp")
    channels = cotangent.shape[2]
    group_count, taps = mr_filter.shape[1:]
    group_size = channels // group_count
    units = channels // (peers * LANES)
    chunks = math.gcd(units, CHUNKS)
    width = channels // (peers * chunks)
    chunk_groups = width // group_size

    dest = lax.dynamic_index_in_dim(block_dest, lax.axis_index("pipe"), 0, keepdims=False)
    me_at = dest.shape[0]
    tp_at = me_at + 1
    here = [lax.axis_index("ctx"), lax.axis_index("tp")]
    meta = jnp.concatenate([dest, jnp.stack(here).astype(jnp.int32)])

    filt = lax.dynamic_index_in_dim(
        mr_filter[0].astype(F32).reshape(chunks, peers, chunk_groups, taps),
        lax.axis_index("ctx"),
        1,
        keepdims=False,
    )
    causal = jnp.pad(filt[:, :, ::-1], ((0, 0), (0, 0), (1, taps - 1)))
    anti = jnp.pad(filt, ((0, 0), (0, 0), (0, taps)))
    bases = jnp.stack([causal, anti], axis=1)

    to_previous = [(pipe, (pipe - 1) % pipes) for pipe in range(pipes)]
    received = []
    for chunk in range(chunks):
        stacked = chunk > 0
        products = multiply(
            chunk,
            width,
            peers,
            qkv_proj,
            cotangent,
            doc_start if chunk == 0 else None,
            stacked,
            chunk == chunks - 1,
        )
        products = list(products)
        if chunk == chunks - 1:
            side = lax.ppermute(products.pop(), "pipe", to_previous)
        if stacked:
            received.append([lax.all_to_all(products[0], "ctx", 0, 0, tiled=True)])
        else:
            received.append(exchanged(products))
    masks = document_masks(me_at, meta, received[0], MARK_ROWS)
    backs = []
    for chunk in range(chunks):
        convolved = convolve(group_size, me_at, meta, received[chunk], masks, bases[chunk])
        backs.append(back_to_previous(convolved))

    result, held = None, []
    for chunk in range(chunks):
        result, cross = gradients(
            chunk, chunks, me_at, tp_at, tp_count, meta, backs[chunk], side, result
        )
        held.append(lax.ppermute(cross, "tp", [(0, 1), (1, 0)]))
    for chunk in range(chunks):
        result = place(chunk, chunks, tp_at, meta, held[chunk], result)
    return result


def solution(mesh):
    placed = (
        P("pipe", None, "ctx", "tp"),
        P("pipe", "ctx", "tp"),
        P(),
        P("pipe", "ctx"),
        P("pipe", "tp", None),
    )
    return jax.shard_map(
        shards,
        mesh=mesh,
        in_specs=placed,
        out_specs=P("pipe", None, ("ctx", "tp"), None),
        check_vma=False,
    )
```

profile of v0, /device:TPU:21, one launch (start us, length us, event | category | flops | bytes accessed | tf_op | source)
XLA Modules:
  0.0 144.8 jit_solution(2642329010254520844)
XLA Ops:
  0.0 4.4 %multiply.2 = (bf16[8,256,256]{2,1,0:T(8,128)(2,1)}, bf16[3,128,4096]{2,1,0:T(8,128)(2,1)}) custom-call(bf16[1,3,128,4096]{3,2,1,0:T(8,128)(2,1)} %refs_0_.3, bf16[1,128,4096]{2,1,0:T(8,128)(2,1)} %refs_1_.3), custom_call_target="tpu_custom_call" | custom-call | flops 524288 | bytes 7340032 | tf_op jit(solution)/shard_map/multiply/pallas_call | solution.py:91
  4.4 1.2 collective-permute-start
  5.6 5.5 %all-to-all-start = ((bf16[8,256,256]{2,1,0:T(8,128)(2,1)}), bf16[8,256,256]{2,1,0:T(8,128)(2,1)}, u32[]{:S(2)}, u32[]{:S(2)}) async-start(bf16[8,256,256]{2,1,0:T(8,128)(2,1)} %get-tuple-element.44), calls=%async_computation | async-start | bytes 2097152 | tf_op jit(solution)/shard_map/all_to_all | solution.py:432
  11.2 2.8 %multiply.3 = (bf16[272,256]{1,0:T(8,128)(2,1)}, bf16[272,256]{1,0:T(8,128)(2,1)}, bf16[272,256]{1,0:T(8,128)(2,1)}, bf16[272,256]{1,0:T(8,128)(2,1)}, bf16[272,...) custom-call(bf16[1,3,128,4096]{3,2,1,0:T(8,128)(2,1)} %refs_0_.3, ...), custom_call_target="tpu_custom_call" | custom-call | flops 524288 | bytes 3670016 | tf_op jit(solution)/shard_map/multiply/pallas_call | solution.py:91
  13.9 0.3 collective-permute-start.1
  14.2 2.1 %collective-permute-start.2 = (bf16[272,256]{1,0:T(8,128)(2,1)}, bf16[272,256]{1,0:T(8,128)(2,1)S(1)}, u32[]{:S(2)}, u32[]{:S(2)}) collective-permute-start(bf16[272,256]{1,0:T(8,128)(2,1)} %get-tuple-element.38), channel_id=1, source_target_pairs={{0,10},{2,8},{4,14},{6,12},{8,2},{10,0},{12,6},{14,4},{1,11},{3,9}... | collective-permute-start | bytes 417800 | tf_op jit(solution)/shard_map/ppermute | solution.py:364
  16.3 1.2 collective-permute-start.3
  17.5 0.3 collective-permute-start.4
  17.8 0.7 convert_bitcast_fusion
  18.6 26.7 %collective-permute-done.1.refs_0_ = bf16[272,256]{1,0:T(8,128)(2,1)S(1)} collective-permute-done((bf16[272,256]{1,0:T(8,128)(2,1)}, bf16[272,256]{1,0:T(8,128)(2,1)S(1)}, u32[]{:S(2)}, u32[]{:S(2)}) %collective-permute-start.1) | collective-permute-done | bytes 139296 | tf_op jit(solution)/shard_map/ppermute | solution.py:364
  45.3 3.1 %collective-permute-start.5 = (bf16[272,256]{1,0:T(8,128)(2,1)}, bf16[272,256]{1,0:T(8,128)(2,1)S(1)}, u32[]{:S(2)}, u32[]{:S(2)}) collective-permute-start(bf16[272,256]{1,0:T(8,128)(2,1)} %get-tuple-element.41), channel_id=1, source_target_pairs={{0,4},{2,6},{4,0},{6,2},{8,12},{10,14},{12,8},{14,10},{1,5},{3,7},... | collective-permute-start | bytes 417800 | tf_op jit(solution)/shard_map/ppermute | solution.py:364
  48.4 0.7 collective-permute-start.6
  49.1 3.7 %collective-permute-start.7 = (bf16[272,256]{1,0:T(8,128)(2,1)}, bf16[272,256]{1,0:T(8,128)(2,1)S(1)}, u32[]{:S(2)}, u32[]{:S(2)}) collective-permute-start(bf16[272,256]{1,0:T(8,128)(2,1)} %get-tuple-element.43), channel_id=1, source_target_pairs={{0,6},{2,4},{4,2},{6,0},{8,14},{10,12},{12,10},{14,8},{1,7},{3,5},... | collective-permute-start | bytes 417800 | tf_op jit(solution)/shard_map/ppermute | solution.py:364
  52.8 0.6 pad_add_fusion.meta_ref
  53.4 0.6 fusion.2
  54.2 3.1 %collective-permute-done.7.refs_7_ = bf16[272,256]{1,0:T(8,128)(2,1)S(1)} collective-permute-done((bf16[272,256]{1,0:T(8,128)(2,1)}, bf16[272,256]{1,0:T(8,128)(2,1)S(1)}, u32[]{:S(2)}, u32[]{:S(2)}) %collective-permute-start.7) | collective-permute-done | bytes 139296 | tf_op jit(solution)/shard_map/ppermute | solution.py:364
  57.3 0.6 copy-done.8
  57.9 2.5 %masks.1.mask_ref = bf16[8,2,128,256]{3,2,1,0:T(8,128)(2,1)} custom-call(s32[66]{0:T(128)} %pad_add_fusion.meta_ref, bf16[272,256]{1,0:T(8,128)(2,1)} %copy-done.4, bf16[272,256]{1,0:T(8,128)(2,1)} %get-tuple-element.37.refs_1_, bf16[272,256]{1,0:T(8,128)(2,1)} %copy-done.5, bf16[272,256]{1,0:T(8,128)(2,1)} %collective-permute-done.3.refs_3_, ...), custom_call_target="tpu_custom_call" | custom-call | flops 1048576 | bytes 1048576 | tf_op jit(solution)/shard_map/masks/pallas_call | solution.py:157
  60.4 9.2 %convolve.3 = (bf16[256,256]{1,0:T(8,128)(2,1)}, bf16[256,256]{1,0:T(8,128)(2,1)}, bf16[256,256]{1,0:T(8,128)(2,1)}, bf16[256,256]{1,0:T(8,128)(2,1)}, bf16[256,...) custom-call(s32[66]{0:T(128)} %pad_add_fusion.meta_ref, ...), custom_call_target="tpu_custom_call" | custom-call | flops 2147483648 | bytes 2621440 | tf_op jit(solution)/shard_map/convolve/pallas_call | solution.py:244
  69.6 2.9 %collective-permute-start.16 = (bf16[256,256]{1,0:T(8,128)(2,1)}, bf16[256,256]{1,0:T(8,128)(2,1)S(1)}, u32[]{:S(2)}, u32[]{:S(2)}) collective-permute-start(bf16[256,256]{1,0:T(8,128)(2,1)} %get-tuple-element.53), channel_id=1, source_target_pairs={{0,24},{2,26},{4,28},{6,30},{8,16},{10,18},{12,20},{14,22},{16,8},... | collective-permute-start | bytes 393224 | tf_op jit(solution)/shard_map/ppermute | solution.py:373
  72.5 1.2 collective-permute-start.17
  73.7 3.3 %collective-permute-start.18 = (bf16[256,256]{1,0:T(8,128)(2,1)}, bf16[256,256]{1,0:T(8,128)(2,1)S(1)}, u32[]{:S(2)}, u32[]{:S(2)}) collective-permute-start(bf16[256,256]{1,0:T(8,128)(2,1)} %get-tuple-element.55), channel_id=1, source_target_pairs={{0,26},{2,24},{4,30},{6,28},{8,18},{10,16},{12,22},{14,20},{16,10}... | collective-permute-start | bytes 393224 | tf_op jit(solution)/shard_map/ppermute | solution.py:373
  77.0 0.2 collective-permute-start.19
  77.2 1.7 %collective-permute-start.20 = (bf16[256,256]{1,0:T(8,128)(2,1)}, bf16[256,256]{1,0:T(8,128)(2,1)}, u32[]{:S(2)}, u32[]{:S(2)}) collective-permute-start(bf16[256,256]{1,0:T(8,128)(2,1)} %get-tuple-element.57), channel_id=1, source_target_pairs={{0,28},{2,30},{4,24},{6,26},{8,20},{10,22},{12,16},{14,18},{16,12}... | collective-permute-start | bytes 393224 | tf_op jit(solution)/shard_map/ppermute | solution.py:373
  78.9 2.5 %collective-permute-start.21 = (bf16[256,256]{1,0:T(8,128)(2,1)}, bf16[256,256]{1,0:T(8,128)(2,1)}, u32[]{:S(2)}, u32[]{:S(2)}) collective-permute-start(bf16[256,256]{1,0:T(8,128)(2,1)} %get-tuple-element.58), channel_id=1, source_target_pairs={{0,20},{2,22},{4,16},{6,18},{8,28},{10,30},{12,24},{14,26},{16,4},... | collective-permute-start | bytes 393224 | tf_op jit(solution)/shard_map/ppermute | solution.py:373
  81.4 4.1 %collective-permute-done.18.refs_2_ = bf16[256,256]{1,0:T(8,128)(2,1)S(1)} collective-permute-done((bf16[256,256]{1,0:T(8,128)(2,1)}, bf16[256,256]{1,0:T(8,128)(2,1)S(1)}, u32[]{:S(2)}, u32[]{:S(2)}) %collective-permute-start.18) | collective-permute-done | bytes 131104 | tf_op jit(solution)/shard_map/ppermute | solution.py:373
  85.5 4.0 %collective-permute-start.22 = (bf16[256,256]{1,0:T(8,128)(2,1)}, bf16[256,256]{1,0:T(8,128)(2,1)}, u32[]{:S(2)}, u32[]{:S(2)}) collective-permute-start(bf16[256,256]{1,0:T(8,128)(2,1)} %get-tuple-element.59), channel_id=1, source_target_pairs={{0,30},{2,28},{4,26},{6,24},{8,22},{10,20},{12,18},{14,16},{16,14}... | collective-permute-start | bytes 393224 | tf_op jit(solution)/shard_map/ppermute | solution.py:373
  89.4 9.1 %convolve.2 = (bf16[256,256]{1,0:T(8,128)(2,1)}, bf16[256,256]{1,0:T(8,128)(2,1)}, bf16[256,256]{1,0:T(8,128)(2,1)}, bf16[256,256]{1,0:T(8,128)(2,1)}, bf16[256,...) custom-call(s32[66]{0:T(128)} %pad_add_fusion.meta_ref, ...), custom_call_target="tpu_custom_call" | custom-call | flops 2147483648 | bytes 2621440 | tf_op jit(solution)/shard_map/convolve/pallas_call | solution.py:244
  98.6 4.6 %collective-permute-start.23 = (bf16[256,256]{1,0:T(8,128)(2,1)}, bf16[256,256]{1,0:T(8,128)(2,1)S(1)}, u32[]{:S(2)}, u32[]{:S(2)}) collective-permute-start(bf16[256,256]{1,0:T(8,128)(2,1)} %get-tuple-element.60), channel_id=1, source_target_pairs={{0,22},{2,20},{4,18},{6,16},{8,30},{10,28},{12,26},{14,24},{16,6},... | collective-permute-start | bytes 393224 | tf_op jit(solution)/shard_map/ppermute | solution.py:373
  103.2 0.3 collective-permute-start.9
  103.5 2.5 %collective-permute-start.10 = (bf16[256,256]{1,0:T(8,128)(2,1)}, bf16[256,256]{1,0:T(8,128)(2,1)S(1)}, u32[]{:S(2)}, u32[]{:S(2)}) collective-permute-start(bf16[256,256]{1,0:T(8,128)(2,1)} %get-tuple-element.47), channel_id=1, source_target_pairs={{0,26},{2,24},{4,30},{6,28},{8,18},{10,16},{12,22},{14,20},{16,10}... | collective-permute-start | bytes 393224 | tf_op jit(solution)/shard_map/ppermute | solution.py:373
  106.0 1.3 collective-permute-done.23.refs_7_
  107.3 1.5 %collective-permute-start.11 = (bf16[256,256]{1,0:T(8,128)(2,1)}, bf16[256,256]{1,0:T(8,128)(2,1)S(1)}, u32[]{:S(2)}, u32[]{:S(2)}) collective-permute-start(bf16[256,256]{1,0:T(8,128)(2,1)} %get-tuple-element.48), channel_id=1, source_target_pairs={{0,18},{2,16},{4,22},{6,20},{8,26},{10,24},{12,30},{14,28},{16,2},... | collective-permute-start | bytes 393224 | tf_op jit(solution)/shard_map/ppermute | solution.py:373
  108.8 1.9 %collective-permute-done.8.refs_0_ = bf16[256,256]{1,0:T(8,128)(2,1)S(1)} collective-permute-done((bf16[256,256]{1,0:T(8,128)(2,1)}, bf16[256,256]{1,0:T(8,128)(2,1)S(1)}, u32[]{:S(2)}, u32[]{:S(2)}) %collective-permute-start.8) | collective-permute-done | bytes 131104 | tf_op jit(solution)/shard_map/ppermute | solution.py:373
  110.7 2.5 %collective-permute-start.13 = (bf16[256,256]{1,0:T(8,128)(2,1)}, bf16[256,256]{1,0:T(8,128)(2,1)S(1)}, u32[]{:S(2)}, u32[]{:S(2)}) collective-permute-start(bf16[256,256]{1,0:T(8,128)(2,1)} %get-tuple-element.50), channel_id=1, source_target_pairs={{0,20},{2,22},{4,16},{6,18},{8,28},{10,30},{12,24},{14,26},{16,4},... | collective-permute-start | bytes 393224 | tf_op jit(solution)/shard_map/ppermute | solution.py:373
  113.2 1.6 %collective-permute-done.10.refs_2_ = bf16[256,256]{1,0:T(8,128)(2,1)S(1)} collective-permute-done((bf16[256,256]{1,0:T(8,128)(2,1)}, bf16[256,256]{1,0:T(8,128)(2,1)S(1)}, u32[]{:S(2)}, u32[]{:S(2)}) %collective-permute-start.10) | collective-permute-done | bytes 131104 | tf_op jit(solution)/shard_map/ppermute | solution.py:373
  114.8 1.8 %collective-permute-start.14 = (bf16[256,256]{1,0:T(8,128)(2,1)}, bf16[256,256]{1,0:T(8,128)(2,1)}, u32[]{:S(2)}, u32[]{:S(2)}) collective-permute-start(bf16[256,256]{1,0:T(8,128)(2,1)} %get-tuple-element.51), channel_id=1, source_target_pairs={{0,30},{2,28},{4,26},{6,24},{8,22},{10,20},{12,18},{14,16},{16,14}... | collective-permute-start | bytes 393224 | tf_op jit(solution)/shard_map/ppermute | solution.py:373
  116.7 6.4 %collective-permute-start.15 = (bf16[256,256]{1,0:T(8,128)(2,1)}, bf16[256,256]{1,0:T(8,128)(2,1)}, u32[]{:S(2)}, u32[]{:S(2)}) collective-permute-start(bf16[256,256]{1,0:T(8,128)(2,1)} %get-tuple-element.52), channel_id=1, source_target_pairs={{0,22},{2,20},{4,18},{6,16},{8,30},{10,28},{12,26},{14,24},{16,6},... | collective-permute-start | bytes 393224 | tf_op jit(solution)/shard_map/ppermute | solution.py:373
  123.1 3.9 %gradients.2 = (bf16[1,3,64,8192]{3,2,1,0:T(8,128)(2,1)}, bf16[3,64,2048]{2,1,0:T(8,128)(2,1)}) custom-call(s32[66]{0:T(128)} %pad_add_fusion.meta_ref, bf16[3,128,4096]{2,1,0:T(8,128)(2,1)} %copy-done.1, bf16[256,256]{1,0:T(8,128)(2,1)} %copy-done.9, bf16[256,256]{1,0:T(8,128)(2,1)} %copy-done.10, bf16[256,256]{1,0:T(8,128)(2,1)} %copy-done.11, ...), custom_call_target="tpu_custom_call" | custom-call | flops 786432 | bytes 4194304 | tf_op jit(solution)/shard_map/gradients/pallas_call | solution.py:320
  127.0 3.4 %collective-permute-start.25 = (bf16[3,64,2048]{2,1,0:T(8,128)(2,1)}, bf16[3,64,2048]{2,1,0:T(8,128)(2,1)S(1)}, u32[]{:S(2)}, u32[]{:S(2)}) collective-permute-start(bf16[3,64,2048]{2,1,0:T(8,128)(2,1)} %get-tuple-element.63), channel_id=1, source_target_pairs={{0,1},{1,0},{2,3},{3,2},{4,5},{5,4},{6,7},{7,6},{8,9},{9,8},{10,11... | collective-permute-start | bytes 2359304 | tf_op jit(solution)/shard_map/ppermute | solution.py:446
  130.4 0.5 collective-permute-done.15.refs_7_
  130.9 0.1 copy-done.17
  131.1 3.9 %gradients.3 = (bf16[1,3,64,8192]{3,2,1,0:T(8,128)(2,1)}, bf16[3,64,2048]{2,1,0:T(8,128)(2,1)}) custom-call(s32[66]{0:T(128)} %pad_add_fusion.meta_ref, bf16[3,128,4096]{2,1,0:T(8,128)(2,1)} %copy-done.1, bf16[256,256]{1,0:T(8,128)(2,1)} %copy-done.13, bf16[256,256]{1,0:T(8,128)(2,1)} %copy-done.14, ...), custom_call_target="tpu_custom_call", output_to_operand_aliasing={{0}: (10, {})} | custom-call | flops 786432 | bytes 4194304 | tf_op jit(solution)/shard_map/gradients/pallas_call | solution.py:320
  135.0 2.5 %collective-permute-start.24 = (bf16[3,64,2048]{2,1,0:T(8,128)(2,1)}, bf16[3,64,2048]{2,1,0:T(8,128)(2,1)S(1)}, u32[]{:S(2)}, u32[]{:S(2)}) collective-permute-start(bf16[3,64,2048]{2,1,0:T(8,128)(2,1)} %get-tuple-element.62), channel_id=1, source_target_pairs={{0,1},{1,0},{2,3},{3,2},{4,5},{5,4},{6,7},{7,6},{8,9},{9,8},{10,11... | collective-permute-start | bytes 2359304 | tf_op jit(solution)/shard_map/ppermute | solution.py:446
  137.5 0.9 copy-done.2
  138.4 2.7 %place.2.held_ref = bf16[1,3,64,8192]{3,2,1,0:T(8,128)(2,1)} custom-call(s32[66]{0:T(128)} %pad_add_fusion.meta_ref, bf16[3,64,2048]{2,1,0:T(8,128)(2,1)} %copy-done.2, bf16[1,3,64,8192]{3,2,1,0:T(8,128)(2,1)} %get-tuple-element.64.held_ref), custom_call_target="tpu_custom_call", output_to_operand_aliasing={{}: (2, {})} | custom-call | bytes 1572864 | tf_op jit(solution)/shard_map/place/pallas_call | solution.py:343
  141.2 0.9 copy-done.3
  142.0 2.7 %place.3 = bf16[1,3,64,8192]{3,2,1,0:T(8,128)(2,1)} custom-call(s32[66]{0:T(128)} %pad_add_fusion.meta_ref, bf16[3,64,2048]{2,1,0:T(8,128)(2,1)} %copy-done.3, bf16[1,3,64,8192]{3,2,1,0:T(8,128)(2,1)} %place.2.held_ref), custom_call_target="tpu_custom_call", output_to_operand_aliasing={{}: (2, {})} | custom-call | bytes 1572864 | tf_op jit(solution)/shard_map/place/pallas_call | solution.py:343
  (59 shorter events, 0.5 us)
Async XLA Ops:
  0.0 18.5 %copy-start = (s32[2,64]{1,0:T(2,128)S(1)}, s32[2,64]{1,0:T(2,128)}, u32[]{:S(2)}) copy-start(s32[2,64]{1,0:T(2,128)} %param.7) | copy-start | bytes 1540
  4.4 112.3 %collective-permute-start = (bf16[3,128,4096]{2,1,0:T(8,128)(2,1)}, bf16[3,128,4096]{2,1,0:T(8,128)(2,1)S(1)}, u32[]{:S(2)}, u32[]{:S(2)}) collective-permute-start(bf16[3,128,4096]{2,1,0:T(8,128)(2,1)} %get-tuple-element.35), channel_id=1, source_target_pairs={{0,16},{16,0},{1,17},{17,1},{2,18},{18,2},{3,19},{19,3},{4,20},{20... | collective-permute-start | bytes 9437192 | tf_op jit(solution)/shard_map/ppermute | solution.py:430
  5.6 83.8 %all-to-all-start = ((bf16[8,256,256]{2,1,0:T(8,128)(2,1)}), bf16[8,256,256]{2,1,0:T(8,128)(2,1)}, u32[]{:S(2)}, u32[]{:S(2)}) async-start(bf16[8,256,256]{2,1,0:T(8,128)(2,1)} %get-tuple-element.44), calls=%async_computation | async-start | bytes 2097152 | tf_op jit(solution)/shard_map/all_to_all | solution.py:432
  13.9 31.4 %collective-permute-start.1 = (bf16[272,256]{1,0:T(8,128)(2,1)}, bf16[272,256]{1,0:T(8,128)(2,1)S(1)}, u32[]{:S(2)}, u32[]{:S(2)}) collective-permute-start(bf16[272,256]{1,0:T(8,128)(2,1)} %get-tuple-element.36), channel_id=1, source_target_pairs={{0,8},{2,10},{4,12},{6,14},{8,0},{10,2},{12,4},{14,6},{1,9},{3,11}... | collective-permute-start | bytes 417800 | tf_op jit(solution)/shard_map/ppermute | solution.py:364
  14.2 34.2 %collective-permute-start.2 = (bf16[272,256]{1,0:T(8,128)(2,1)}, bf16[272,256]{1,0:T(8,128)(2,1)S(1)}, u32[]{:S(2)}, u32[]{:S(2)}) collective-permute-start(bf16[272,256]{1,0:T(8,128)(2,1)} %get-tuple-element.38), channel_id=1, source_target_pairs={{0,10},{2,8},{4,14},{6,12},{8,2},{10,0},{12,6},{14,4},{1,11},{3,9}... | collective-permute-start | bytes 417800 | tf_op jit(solution)/shard_map/ppermute | solution.py:364
  16.3 32.7 %collective-permute-start.3 = (bf16[272,256]{1,0:T(8,128)(2,1)}, bf16[272,256]{1,0:T(8,128)(2,1)}, u32[]{:S(2)}, u32[]{:S(2)}) collective-permute-start(bf16[272,256]{1,0:T(8,128)(2,1)} %get-tuple-element.39), channel_id=1, source_target_pairs={{0,2},{2,0},{4,6},{6,4},{8,10},{10,8},{12,14},{14,12},{1,3},{3,1},... | collective-permute-start | bytes 417800 | tf_op jit(solution)/shard_map/ppermute | solution.py:364
  17.5 36.6 %collective-permute-start.4 = (bf16[272,256]{1,0:T(8,128)(2,1)}, bf16[272,256]{1,0:T(8,128)(2,1)}, u32[]{:S(2)}, u32[]{:S(2)}) collective-permute-start(bf16[272,256]{1,0:T(8,128)(2,1)} %get-tuple-element.40), channel_id=1, source_target_pairs={{0,12},{2,14},{4,8},{6,10},{8,4},{10,6},{12,0},{14,2},{1,13},{3,15... | collective-permute-start | bytes 417800 | tf_op jit(solution)/shard_map/ppermute | solution.py:364
  45.3 11.9 %copy-start.4 = (bf16[272,256]{1,0:T(8,128)(2,1)}, bf16[272,256]{1,0:T(8,128)(2,1)S(1)}, u32[]{:S(2)}) copy-start(bf16[272,256]{1,0:T(8,128)(2,1)S(1)} %collective-permute-done.1.refs_0_) | copy-start | bytes 417796
  45.3 8.7 %collective-permute-start.5 = (bf16[272,256]{1,0:T(8,128)(2,1)}, bf16[272,256]{1,0:T(8,128)(2,1)S(1)}, u32[]{:S(2)}, u32[]{:S(2)}) collective-permute-start(bf16[272,256]{1,0:T(8,128)(2,1)} %get-tuple-element.41), channel_id=1, source_target_pairs={{0,4},{2,6},{4,0},{6,2},{8,12},{10,14},{12,8},{14,10},{1,5},{3,7},... | collective-permute-start | bytes 417800 | tf_op jit(solution)/shard_map/ppermute | solution.py:364
  48.4 8.9 %copy-start.5 = (bf16[272,256]{1,0:T(8,128)(2,1)}, bf16[272,256]{1,0:T(8,128)(2,1)S(1)}, u32[]{:S(2)}) copy-start(bf16[272,256]{1,0:T(8,128)(2,1)S(1)} %collective-permute-done.2.refs_2_) | copy-start | bytes 417796
  48.4 5.8 %collective-permute-start.6 = (bf16[272,256]{1,0:T(8,128)(2,1)}, bf16[272,256]{1,0:T(8,128)(2,1)S(1)}, u32[]{:S(2)}, u32[]{:S(2)}) collective-permute-start(bf16[272,256]{1,0:T(8,128)(2,1)} %get-tuple-element.42), channel_id=1, source_target_pairs={{0,14},{2,12},{4,10},{6,8},{8,6},{10,4},{12,2},{14,0},{1,15},{3,13... | collective-permute-start | bytes 417800 | tf_op jit(solution)/shard_map/ppermute | solution.py:364
  49.1 8.2 %collective-permute-start.7 = (bf16[272,256]{1,0:T(8,128)(2,1)}, bf16[272,256]{1,0:T(8,128)(2,1)S(1)}, u32[]{:S(2)}, u32[]{:S(2)}) collective-permute-start(bf16[272,256]{1,0:T(8,128)(2,1)} %get-tuple-element.43), channel_id=1, source_target_pairs={{0,6},{2,4},{4,2},{6,0},{8,14},{10,12},{12,10},{14,8},{1,7},{3,5},... | collective-permute-start | bytes 417800 | tf_op jit(solution)/shard_map/ppermute | solution.py:364
  54.1 3.2 %copy-start.6 = (bf16[272,256]{1,0:T(8,128)(2,1)}, bf16[272,256]{1,0:T(8,128)(2,1)S(1)}, u32[]{:S(2)}) copy-start(bf16[272,256]{1,0:T(8,128)(2,1)S(1)} %collective-permute-done.5.refs_5_) | copy-start | bytes 417796
  54.2 3.1 %copy-start.7 = (bf16[272,256]{1,0:T(8,128)(2,1)}, bf16[272,256]{1,0:T(8,128)(2,1)S(1)}, u32[]{:S(2)}) copy-start(bf16[272,256]{1,0:T(8,128)(2,1)S(1)} %collective-permute-done.6.refs_6_) | copy-start | bytes 417796
  57.3 0.7 copy-start.8
  69.6 7.6 %collective-permute-start.16 = (bf16[256,256]{1,0:T(8,128)(2,1)}, bf16[256,256]{1,0:T(8,128)(2,1)S(1)}, u32[]{:S(2)}, u32[]{:S(2)}) collective-permute-start(bf16[256,256]{1,0:T(8,128)(2,1)} %get-tuple-element.53), channel_id=1, source_target_pairs={{0,24},{2,26},{4,28},{6,30},{8,16},{10,18},{12,20},{14,22},{16,8},... | collective-permute-start | bytes 393224 | tf_op jit(solution)/shard_map/ppermute | solution.py:373
  72.5 6.4 %collective-permute-start.17 = (bf16[256,256]{1,0:T(8,128)(2,1)}, bf16[256,256]{1,0:T(8,128)(2,1)S(1)}, u32[]{:S(2)}, u32[]{:S(2)}) collective-permute-start(bf16[256,256]{1,0:T(8,128)(2,1)} %get-tuple-element.54), channel_id=1, source_target_pairs={{0,16},{2,18},{4,20},{6,22},{8,24},{10,26},{12,28},{14,30},{16,0},... | collective-permute-start | bytes 393224 | tf_op jit(solution)/shard_map/ppermute | solution.py:373
  73.7 11.8 %collective-permute-start.18 = (bf16[256,256]{1,0:T(8,128)(2,1)}, bf16[256,256]{1,0:T(8,128)(2,1)S(1)}, u32[]{:S(2)}, u32[]{:S(2)}) collective-permute-start(bf16[256,256]{1,0:T(8,128)(2,1)} %get-tuple-element.55), channel_id=1, source_target_pairs={{0,26},{2,24},{4,30},{6,28},{8,18},{10,16},{12,22},{14,20},{16,10}... | collective-permute-start | bytes 393224 | tf_op jit(solution)/shard_map/ppermute | solution.py:373
  77.0 21.6 %collective-permute-start.19 = (bf16[256,256]{1,0:T(8,128)(2,1)}, bf16[256,256]{1,0:T(8,128)(2,1)}, u32[]{:S(2)}, u32[]{:S(2)}) collective-permute-start(bf16[256,256]{1,0:T(8,128)(2,1)} %get-tuple-element.56), channel_id=1, source_target_pairs={{0,18},{2,16},{4,22},{6,20},{8,26},{10,24},{12,30},{14,28},{16,2},... | collective-permute-start | bytes 393224 | tf_op jit(solution)/shard_map/ppermute | solution.py:373
  77.2 21.4 %copy-start.9 = (bf16[256,256]{1,0:T(8,128)(2,1)}, bf16[256,256]{1,0:T(8,128)(2,1)S(1)}, u32[]{:S(2)}) copy-start(bf16[256,256]{1,0:T(8,128)(2,1)S(1)} %collective-permute-done.16.refs_0_) | copy-start | bytes 393220
  77.2 26.0 %collective-permute-start.20 = (bf16[256,256]{1,0:T(8,128)(2,1)}, bf16[256,256]{1,0:T(8,128)(2,1)}, u32[]{:S(2)}, u32[]{:S(2)}) collective-permute-start(bf16[256,256]{1,0:T(8,128)(2,1)} %get-tuple-element.57), channel_id=1, source_target_pairs={{0,28},{2,30},{4,24},{6,26},{8,20},{10,22},{12,16},{14,18},{16,12}... | collective-permute-start | bytes 393224 | tf_op jit(solution)/shard_map/ppermute | solution.py:373
  78.9 19.6 %copy-start.10 = (bf16[256,256]{1,0:T(8,128)(2,1)}, bf16[256,256]{1,0:T(8,128)(2,1)S(1)}, u32[]{:S(2)}) copy-start(bf16[256,256]{1,0:T(8,128)(2,1)S(1)} %collective-permute-done.17.refs_1_) | copy-start | bytes 393220
  78.9 24.3 %collective-permute-start.21 = (bf16[256,256]{1,0:T(8,128)(2,1)}, bf16[256,256]{1,0:T(8,128)(2,1)}, u32[]{:S(2)}, u32[]{:S(2)}) collective-permute-start(bf16[256,256]{1,0:T(8,128)(2,1)} %get-tuple-element.58), channel_id=1, source_target_pairs={{0,20},{2,22},{4,16},{6,18},{8,28},{10,30},{12,24},{14,26},{16,4},... | collective-permute-start | bytes 393224 | tf_op jit(solution)/shard_map/ppermute | solution.py:373
  85.5 13.1 %copy-start.11 = (bf16[256,256]{1,0:T(8,128)(2,1)}, bf16[256,256]{1,0:T(8,128)(2,1)S(1)}, u32[]{:S(2)}) copy-start(bf16[256,256]{1,0:T(8,128)(2,1)S(1)} %collective-permute-done.18.refs_2_) | copy-start | bytes 393220
  85.5 18.0 %collective-permute-start.22 = (bf16[256,256]{1,0:T(8,128)(2,1)}, bf16[256,256]{1,0:T(8,128)(2,1)}, u32[]{:S(2)}, u32[]{:S(2)}) collective-permute-start(bf16[256,256]{1,0:T(8,128)(2,1)} %get-tuple-element.59), channel_id=1, source_target_pairs={{0,30},{2,28},{4,26},{6,24},{8,22},{10,20},{12,18},{14,16},{16,14}... | collective-permute-start | bytes 393224 | tf_op jit(solution)/shard_map/ppermute | solution.py:373
  98.6 8.8 %collective-permute-start.23 = (bf16[256,256]{1,0:T(8,128)(2,1)}, bf16[256,256]{1,0:T(8,128)(2,1)S(1)}, u32[]{:S(2)}, u32[]{:S(2)}) collective-permute-start(bf16[256,256]{1,0:T(8,128)(2,1)} %get-tuple-element.60), channel_id=1, source_target_pairs={{0,22},{2,20},{4,18},{6,16},{8,30},{10,28},{12,26},{14,24},{16,6},... | collective-permute-start | bytes 393224 | tf_op jit(solution)/shard_map/ppermute | solution.py:373
  103.1 7.5 %collective-permute-start.8 = (bf16[256,256]{1,0:T(8,128)(2,1)}, bf16[256,256]{1,0:T(8,128)(2,1)S(1)}, u32[]{:S(2)}, u32[]{:S(2)}) collective-permute-start(bf16[256,256]{1,0:T(8,128)(2,1)} %get-tuple-element.45), channel_id=1, source_target_pairs={{0,24},{2,26},{4,28},{6,30},{8,16},{10,18},{12,20},{14,22},{16,8},... | collective-permute-start | bytes 393224 | tf_op jit(solution)/shard_map/ppermute | solution.py:373
  103.2 7.5 %collective-permute-start.9 = (bf16[256,256]{1,0:T(8,128)(2,1)}, bf16[256,256]{1,0:T(8,128)(2,1)S(1)}, u32[]{:S(2)}, u32[]{:S(2)}) collective-permute-start(bf16[256,256]{1,0:T(8,128)(2,1)} %get-tuple-element.46), channel_id=1, source_target_pairs={{0,16},{2,18},{4,20},{6,22},{8,24},{10,26},{12,28},{14,30},{16,0},... | collective-permute-start | bytes 393224 | tf_op jit(solution)/shard_map/ppermute | solution.py:373
  103.5 11.3 %collective-permute-start.10 = (bf16[256,256]{1,0:T(8,128)(2,1)}, bf16[256,256]{1,0:T(8,128)(2,1)S(1)}, u32[]{:S(2)}, u32[]{:S(2)}) collective-permute-start(bf16[256,256]{1,0:T(8,128)(2,1)} %get-tuple-element.47), channel_id=1, source_target_pairs={{0,26},{2,24},{4,30},{6,28},{8,18},{10,16},{12,22},{14,20},{16,10}... | collective-permute-start | bytes 393224 | tf_op jit(solution)/shard_map/ppermute | solution.py:373
  107.3 15.8 %copy-start.12 = (bf16[256,256]{1,0:T(8,128)(2,1)}, bf16[256,256]{1,0:T(8,128)(2,1)S(1)}, u32[]{:S(2)}) copy-start(bf16[256,256]{1,0:T(8,128)(2,1)S(1)} %collective-permute-done.23.refs_7_) | copy-start | bytes 393220
  107.3 19.7 %collective-permute-start.11 = (bf16[256,256]{1,0:T(8,128)(2,1)}, bf16[256,256]{1,0:T(8,128)(2,1)S(1)}, u32[]{:S(2)}, u32[]{:S(2)}) collective-permute-start(bf16[256,256]{1,0:T(8,128)(2,1)} %get-tuple-element.48), channel_id=1, source_target_pairs={{0,18},{2,16},{4,22},{6,20},{8,26},{10,24},{12,30},{14,28},{16,2},... | collective-permute-start | bytes 393224 | tf_op jit(solution)/shard_map/ppermute | solution.py:373
  110.7 20.2 %copy-start.13 = (bf16[256,256]{1,0:T(8,128)(2,1)}, bf16[256,256]{1,0:T(8,128)(2,1)S(1)}, u32[]{:S(2)}) copy-start(bf16[256,256]{1,0:T(8,128)(2,1)S(1)} %collective-permute-done.8.refs_0_) | copy-start | bytes 393220
  110.7 19.7 %collective-permute-start.12 = (bf16[256,256]{1,0:T(8,128)(2,1)}, bf16[256,256]{1,0:T(8,128)(2,1)S(1)}, u32[]{:S(2)}, u32[]{:S(2)}) collective-permute-start(bf16[256,256]{1,0:T(8,128)(2,1)} %get-tuple-element.49), channel_id=1, source_target_pairs={{0,28},{2,30},{4,24},{6,26},{8,20},{10,22},{12,16},{14,18},{16,12}... | collective-permute-start | bytes 393224 | tf_op jit(solution)/shard_map/ppermute | solution.py:373
  110.7 20.2 %copy-start.14 = (bf16[256,256]{1,0:T(8,128)(2,1)}, bf16[256,256]{1,0:T(8,128)(2,1)S(1)}, u32[]{:S(2)}) copy-start(bf16[256,256]{1,0:T(8,128)(2,1)S(1)} %collective-permute-done.9.refs_1_) | copy-start | bytes 393220
  110.7 19.7 %collective-permute-start.13 = (bf16[256,256]{1,0:T(8,128)(2,1)}, bf16[256,256]{1,0:T(8,128)(2,1)S(1)}, u32[]{:S(2)}, u32[]{:S(2)}) collective-permute-start(bf16[256,256]{1,0:T(8,128)(2,1)} %get-tuple-element.50), channel_id=1, source_target_pairs={{0,20},{2,22},{4,16},{6,18},{8,28},{10,30},{12,24},{14,26},{16,4},... | collective-permute-start | bytes 393224 | tf_op jit(solution)/shard_map/ppermute | solution.py:373
  114.8 16.1 %copy-start.15 = (bf16[256,256]{1,0:T(8,128)(2,1)}, bf16[256,256]{1,0:T(8,128)(2,1)S(1)}, u32[]{:S(2)}) copy-start(bf16[256,256]{1,0:T(8,128)(2,1)S(1)} %collective-permute-done.10.refs_2_) | copy-start | bytes 393220
  114.8 15.6 %collective-permute-start.14 = (bf16[256,256]{1,0:T(8,128)(2,1)}, bf16[256,256]{1,0:T(8,128)(2,1)}, u32[]{:S(2)}, u32[]{:S(2)}) collective-permute-start(bf16[256,256]{1,0:T(8,128)(2,1)} %get-tuple-element.51), channel_id=1, source_target_pairs={{0,30},{2,28},{4,26},{6,24},{8,22},{10,20},{12,18},{14,16},{16,14}... | collective-permute-start | bytes 393224 | tf_op jit(solution)/shard_map/ppermute | solution.py:373
  116.7 6.4 %copy-start.1 = (bf16[3,128,4096]{2,1,0:T(8,128)(2,1)}, bf16[3,128,4096]{2,1,0:T(8,128)(2,1)S(1)}, u32[]{:S(2)}) copy-start(bf16[3,128,4096]{2,1,0:T(8,128)(2,1)S(1)} %collective-permute-done.side_ref) | copy-start | bytes 9437188
  116.7 14.2 %collective-permute-start.15 = (bf16[256,256]{1,0:T(8,128)(2,1)}, bf16[256,256]{1,0:T(8,128)(2,1)}, u32[]{:S(2)}, u32[]{:S(2)}) collective-permute-start(bf16[256,256]{1,0:T(8,128)(2,1)} %get-tuple-element.52), channel_id=1, source_target_pairs={{0,22},{2,20},{4,18},{6,16},{8,30},{10,28},{12,26},{14,24},{16,6},... | collective-permute-start | bytes 393224 | tf_op jit(solution)/shard_map/ppermute | solution.py:373
  127.0 3.9 %copy-start.16 = (bf16[256,256]{1,0:T(8,128)(2,1)}, bf16[256,256]{1,0:T(8,128)(2,1)S(1)}, u32[]{:S(2)}) copy-start(bf16[256,256]{1,0:T(8,128)(2,1)S(1)} %collective-permute-done.11.refs_3_) | copy-start | bytes 393220
  127.0 10.5 %collective-permute-start.25 = (bf16[3,64,2048]{2,1,0:T(8,128)(2,1)}, bf16[3,64,2048]{2,1,0:T(8,128)(2,1)S(1)}, u32[]{:S(2)}, u32[]{:S(2)}) collective-permute-start(bf16[3,64,2048]{2,1,0:T(8,128)(2,1)} %get-tuple-element.63), channel_id=1, source_target_pairs={{0,1},{1,0},{2,3},{3,2},{4,5},{5,4},{6,7},{7,6},{8,9},{9,8},{10,11... | collective-permute-start | bytes 2359304 | tf_op jit(solution)/shard_map/ppermute | solution.py:446
  130.4 0.7 copy-start.17
  130.4 0.7 copy-start.18
  135.0 6.1 %collective-permute-start.24 = (bf16[3,64,2048]{2,1,0:T(8,128)(2,1)}, bf16[3,64,2048]{2,1,0:T(8,128)(2,1)S(1)}, u32[]{:S(2)}, u32[]{:S(2)}) collective-permute-start(bf16[3,64,2048]{2,1,0:T(8,128)(2,1)} %get-tuple-element.62), channel_id=1, source_target_pairs={{0,1},{1,0},{2,3},{3,2},{4,5},{5,4},{6,7},{7,6},{8,9},{9,8},{10,11... | collective-permute-start | bytes 2359304 | tf_op jit(solution)/shard_map/ppermute | solution.py:446
  137.5 0.9 copy-start.2
  141.2 0.9 copy-start.3
where the time goes:
time: 147 us; the launch traced here: 145 us
  starting transfers between devices  59.3 us (40%)
  Pallas kernels  41.2 us (28%)
  waiting for transfers between devices  39.3 us (27%)
  local copies, waits for them, and re-layouts  2.83 us (2%)
  other arithmetic  1.97 us (1%)
    ppermute x16, starting transfers between devices, back_to_previous(): lax.ppermute(array, ('pipe', 'ctx'), [(pipe * peers + i, (pipe - 1) % pip...  35.4 us
    ppermute x7, waiting for transfers between devices, exchanged(): lax.ppermute(array, 'ctx', [(i, i ^ k) for i in range(peers)])  29.9 us
    pallas_call x2, Pallas kernels, convolve(): pl.pallas_call(functools.partial(conv_kernel, group_size, me_at, peers),...  18.3 us
    ppermute x7, starting transfers between devices, exchanged(): lax.ppermute(array, 'ctx', [(i, i ^ k) for i in range(peers)])  11.3 us
    ppermute x16, waiting for transfers between devices, back_to_previous(): lax.ppermute(array, ('pipe', 'ctx'), [(pipe * peers + i, (pipe - 1) % pip...  9.37 us
    pallas_call x2, Pallas kernels, gradients(): pl.pallas_call(functools.partial(gradients_kernel, me_at, tp_at), out_sha...  7.84 us
    pallas_call x2, Pallas kernels, multiply(): pl.pallas_call(functools.partial(multiply_kernel, stacked, marked, sided)...  7.18 us
    ppermute x2, starting transfers between devices, shards(): held.append(lax.ppermute(cross, 'tp', [(0, 1), (1, 0)]))  5.87 us
  transfers between devices with their start and end apart: 27, of which 8 were waited for; matrix products, arithmetic and copies ran while one was open for 1% of the time, Pallas kernels for 24%

commit v1 on v0

--- a/solution.py
+++ b/solution.py
@@ -11,13 +11,15 @@
 LANES = 128
 CHUNKS = 2
 MARK_ROWS = 16
-VMEM_BYTES = 60 * 1024 * 1024
+OUT_FIRST = 5
+BACK_FIRST = 4
+GRADIENTS_AFTER = 7
 F32 = jnp.float32
 BF16 = jnp.bfloat16
 
 
-def params():
-    return pltpu.CompilerParams(vmem_limit_bytes=VMEM_BYTES)
+def params(mebibytes):
+    return pltpu.CompilerParams(vmem_limit_bytes=mebibytes * 1024 * 1024)
 
 
 def whole_block(*shape):
@@ -33,73 +35,85 @@
     return [k for i in range(half) for k in (half + i, i)]
 
 
-def multiply_kernel(stacked, marked, sided, *refs):
-    refs = list(refs)
-    proj_ref, grad_ref = refs[:2]
-    marks_ref = refs[2] if marked else None
-    outs = refs[3 if marked else 2 :]
-    if sided:
-        side_ref = outs.pop()
-        side_ref[0] = proj_ref[0, 1]
-        side_ref[1] = proj_ref[0, 2]
-        side_ref[2] = grad_ref[0]
+def multiply_kernel(chunks, proj_ref, grad_ref, marks_ref, *refs):
+    arrived, made, in_sems, out_sems, side_sems = refs[-5:]
+    side_ref = refs[-6]
+    outs = refs[:-6]
+    peers = len(outs) // chunks
     rows = grad_ref.shape[1]
-    width = outs[0].shape[-1]
+    width = outs[0].shape[1]
+    span = peers * width
     me = lax.axis_index("ctx")
-    if stacked:
-        peers = outs[0].shape[0]
-        places = [(peer, outs[0].at[peer]) for peer in range(peers)]
-    else:
-        peers = len(outs)
-        places = [(me ^ k, out_ref) for k, out_ref in zip(sending_order(peers), outs)]
-    span = peers * width
-    begin = grad_ref.shape[2] - span
-    for peer, out_ref in places:
-        lanes = pl.ds(pl.multiple_of(begin + peer * width, LANES), width)
-        query = proj_ref[0, 0, :, lanes].astype(F32)
-        key_rows = proj_ref[0, 1, :, lanes].astype(F32)
-        value = proj_ref[0, 2, :, lanes].astype(F32)
-        grad_in = grad_ref[0, :, lanes].astype(F32)
-        out_ref[:rows, :] = (key_rows * value).astype(BF16)
-        out_ref[rows : 2 * rows, :] = (grad_in * query).astype(BF16)
-        if marked:
-            extra = out_ref.shape[0] - 2 * rows
-            marks = marks_ref[...].astype(F32)
-            out_ref[2 * rows :, :LANES] = jnp.broadcast_to(marks, (extra, LANES)).astype(BF16)
-            if width > LANES:
-                out_ref[2 * rows :, LANES:] = jnp.zeros((extra, width - LANES), BF16)
-
-
-def multiply(index, width, peers, qkv_proj, cotangent, marks, stacked, sided):
+    loads, stores = [], []
+    for chunk in range(chunks):
+        lanes = pl.ds(chunk * span, span)
+        for array in range(4):
+            source = grad_ref.at[0, :, lanes] if array == 3 else proj_ref.at[0, array, :, lanes]
+            loads.append(
+                pltpu.make_async_copy(
+                    source, arrived.at[array, :, lanes], in_sems.at[chunk, array]
+                )
+            )
+    for load in loads:
+        load.start()
+    marks = jnp.broadcast_to(marks_ref[...].astype(F32), (MARK_ROWS, LANES)).astype(BF16)
+    for chunk in range(chunks):
+        for load in loads[4 * chunk : 4 * chunk + 4]:
+            load.wait()
+        for j, k in enumerate(sending_order(peers)):
+            at = chunk * peers + j
+            first = pl.multiple_of(chunk * span + (me ^ k) * width, LANES)
+            query, key_rows, value, grad_in = [
+                arrived[array, :, pl.ds(first, width)].astype(F32) for array in range(4)
+            ]
+            made[at, :rows, :] = (key_rows * value).astype(BF16)
+            made[at, rows : 2 * rows, :] = (grad_in * query).astype(BF16)
+            if chunk == 0:
+                made[at, 2 * rows :, :LANES] = marks
+                if width > LANES:
+                    made[at, 2 * rows :, LANES:] = jnp.zeros((MARK_ROWS, width - LANES), BF16)
+            source = made.at[at] if chunk == 0 else made.at[at, : 2 * rows]
+            stores.append(pltpu.make_async_copy(source, outs[at], out_sems.at[at]))
+            stores[-1].start()
+        lanes = pl.ds(chunk * span, span)
+        for array in range(3):
+            stores.append(
+                pltpu.make_async_copy(
+                    arrived.at[array + 1, :, lanes],
+                    side_ref.at[array, :, lanes],
+                    side_sems.at[chunk, array],
+                )
+            )
+            stores[-1].start()
+    for store in stores:
+        store.wait()
+
+
+def multiply(chunks, width, peers, qkv_proj, cotangent, marks):
     _, rows, channels = cotangent.shape
-    span = peers * width
-    taken = channels if sided else span
-    block = 0 if sided else index
-    marked = marks is not None
-    in_specs = [
-        pl.BlockSpec((1, 3, rows, taken), lambda _: (0, 0, 0, block)),
-        pl.BlockSpec((1, rows, taken), lambda _: (0, 0, block)),
-    ]
-    args = [qkv_proj, cotangent]
-    if marked:
-        in_specs.append(whole_block(*marks.shape))
-        args.append(marks)
-    out = (2 * rows + (MARK_ROWS if marked else 0), width)
-    shapes = [(peers,) + out] if stacked else [out] * peers
-    if sided:
-        shapes.append((3, rows, channels))
-    return pl.pallas_call(
-        functools.partial(multiply_kernel, stacked, marked, sided),
+    anywhere = pl.BlockSpec(memory_space=pl.ANY)
+    tall = 2 * rows + MARK_ROWS
+    shapes = [(tall if chunk == 0 else 2 * rows, width) for chunk in range(chunks)]
+    shapes = [shape for shape in shapes for _ in range(peers)] + [(3, rows, channels)]
+    made = pl.pallas_call(
+        functools.partial(multiply_kernel, chunks),
         out_shape=[jax.ShapeDtypeStruct(shape, BF16) for shape in shapes],
-        in_specs=in_specs,
-        out_specs=[whole_block(*shape) for shape in shapes],
-        compiler_params=params(),
+        in_specs=[anywhere, anywhere, pl.BlockSpec(memory_space=pltpu.VMEM)],
+        out_specs=[anywhere] * len(shapes),
+        scratch_shapes=[
+            pltpu.VMEM((4, rows, channels), BF16),
+            pltpu.VMEM((chunks * peers, tall, width), BF16),
+            pltpu.SemaphoreType.DMA((chunks, 4)),
+            pltpu.SemaphoreType.DMA((chunks * peers,)),
+            pltpu.SemaphoreType.DMA((chunks, 3)),
+        ],
+        compiler_params=params(60),
         cost_estimate=pl.CostEstimate(
-            flops=2 * rows * span, bytes_accessed=14 * rows * taken, transcendentals=0
-        ),
-        grid=(1,),
+            flops=2 * rows * channels, bytes_accessed=18 * rows * channels, transcendentals=0
+        ),
         name="multiply",
-    )(*args)
+    )(qkv_proj, cotangent, marks)
+    return [list(made[c * peers : (c + 1) * peers]) for c in range(chunks)], made[-1]
 
 
 def first_row(meta_ref, peers, source, block):
@@ -163,7 +177,7 @@
             pltpu.VMEM((peers * tile, tile), F32),
             pltpu.VMEM((peers * tile, tile), F32),
         ],
-        compiler_params=params(),
+        compiler_params=params(24),
         cost_estimate=pl.CostEstimate(
             flops=8 * peers * tile * tile, bytes_accessed=8 * peers * tile * tile, transcendentals=0
         ),
@@ -172,14 +186,12 @@
     )(meta, *received)
 
 
-def conv_kernel(group_size, me_at, peers, meta_ref, mask_ref, base_ref, *refs):
+def conv_kernel(group_size, me_at, peers, passing, meta_ref, mask_ref, base_ref, *refs):
     rows32, rows16, toep = refs[-3:]
-    recv, outs = refs[: -3 - peers], refs[-3 - peers : -3]
+    recv = refs[:peers]
+    outs = refs[peers + passing : 2 * peers + passing]
     me = meta_ref[me_at]
-    if len(recv) == 1:
-        arrivals = [(source, recv[0].at[source]) for source in range(peers)]
-    else:
-        arrivals = [(me ^ k, recv_ref) for k, recv_ref in zip(sending_order(peers), recv)]
+    arrivals = [(me ^ k, recv_ref) for k, recv_ref in zip(sending_order(peers), recv)]
     tile = LANES
     width = outs[0].shape[1]
     groups = base_ref.shape[1]
@@ -235,24 +247,28 @@
             )
 
 
-def convolve(group_size, me_at, meta, received, masks, bases):
+def convolve(group_size, me_at, meta, received, masks, bases, passing):
     peers = masks.shape[0]
     tile = LANES
     width = received[0].shape[-1]
     groups = bases.shape[1]
     out = (2 * tile, width)
-    return pl.pallas_call(
-        functools.partial(conv_kernel, group_size, me_at, peers),
-        out_shape=[jax.ShapeDtypeStruct(out, BF16)] * peers,
+    anywhere = [pl.BlockSpec(memory_space=pl.ANY)] * len(passing)
+    outs = pl.pallas_call(
+        functools.partial(conv_kernel, group_size, me_at, peers, len(passing)),
+        out_shape=[jax.ShapeDtypeStruct(out, BF16)] * peers
+        + [jax.ShapeDtypeStruct(p.shape, BF16) for p in passing],
         in_specs=[smem(), whole_block(*masks.shape), whole_block(*bases.shape)]
-        + [whole_block(*r.shape) for r in received],
-        out_specs=[whole_block(*out)] * peers,
+        + [whole_block(*r.shape) for r in received]
+        + anywhere,
+        out_specs=[whole_block(*out)] * peers + anywhere,
+        input_output_aliases={3 + peers + i: peers + i for i in range(len(passing))},
         scratch_shapes=[
             pltpu.VMEM((2, peers * tile, width), F32),
             pltpu.VMEM((2, (peers + 1) * tile, width), BF16),
             pltpu.VMEM((2, groups, tile, 2 * tile), BF16),
         ],
-        compiler_params=params(),
+        compiler_params=params(24),
         cost_estimate=pl.CostEstimate(
             flops=8 * groups * peers * tile**3,
             bytes_accessed=8 * peers * tile * width + 4 * peers * tile**2,
@@ -260,12 +276,12 @@
         ),
         grid=(1,),
         name="convolve",
-    )(meta, masks, bases, *received)
-
-
-def gradients_kernel(me_at, tp_at, meta_ref, side_ref, *refs):
+    )(meta, masks, bases, *received, *passing)
+    return list(outs[:peers]), list(outs[peers:])
+
+
+def gradients_kernel(me_at, tp_at, peers, meta_ref, side_ref, *refs):
     result_ref, cross_ref = refs[-2:]
-    peers = count_backs(refs)
     rows = side_ref.shape[1]
     width = side_ref.shape[2] // peers
     part = cross_ref.shape[1]
@@ -287,10 +303,6 @@
             out_ref[2, :, lanes] = (mixed_grad * key_rows).astype(BF16)
 
 
-def count_backs(refs):
-    return sum(1 for ref in refs if len(ref.shape) == 2)
-
-
 def fixed(shape):
     return pl.BlockSpec(shape, lambda _, meta_ref: (0,) * len(shape))
 
@@ -303,7 +315,7 @@
     return pl.BlockSpec((1,) + shape, place)
 
 
-def gradients(chunk, chunks, me_at, tp_at, tp_count, meta, backs, side, result):
+def gradients(chunk, chunks, me_at, tp_at, tp_count, meta, backs, side, others):
     peers = len(backs)
     _, rows, channels = side.shape
     span = channels // chunks
@@ -312,13 +324,12 @@
     in_specs = [pl.BlockSpec((3, rows, span), lambda _, meta_ref: (0, 0, chunk))]
     in_specs += [fixed(backs[0].shape)] * peers
     args = [meta, side, *backs]
-    aliases = {}
-    if result is not None:
-        aliases = {len(args): 0}
-        args.append(result)
+    aliases = {} if chunk == 0 else {len(args): 0}
+    for other in others:
+        args.append(other)
         in_specs.append(pl.BlockSpec(memory_space=pl.ANY))
     return pl.pallas_call(
-        functools.partial(gradients_kernel, me_at, tp_at),
+        functools.partial(gradients_kernel, me_at, tp_at, peers),
         out_shape=[jax.ShapeDtypeStruct(whole, BF16), jax.ShapeDtypeStruct(out, BF16)],
         grid_spec=pltpu.PrefetchScalarGridSpec(
             num_scalar_prefetch=1,
@@ -327,7 +338,7 @@
             out_specs=[result_block(out, chunk, chunks, tp_at, True), fixed(out)],
         ),
         input_output_aliases=aliases,
-        compiler_params=params(),
+        compiler_params=params(24),
         cost_estimate=pl.CostEstimate(
             flops=3 * rows * span, bytes_accessed=16 * rows * span, transcendentals=0
         ),
@@ -350,7 +361,7 @@
             out_specs=result_block(cross.shape, chunk, chunks, tp_at, False),
         ),
         input_output_aliases={2: 0},
-        compiler_params=params(),
+        compiler_params=params(24),
         cost_estimate=pl.CostEstimate(
             flops=0, bytes_accessed=4 * math.prod(cross.shape), transcendentals=0
         ),
@@ -358,29 +369,20 @@
     )(meta, cross, result)
 
 
-def exchanged(arrays):
-    peers = len(arrays)
-    return [
-        lax.ppermute(array, "ctx", [(i, i ^ k) for i in range(peers)]) if k else array
-        for k, array in zip(sending_order(peers), arrays)
+def swap(array, k):
+    peers = lax.axis_size("ctx")
+    return lax.ppermute(array, "ctx", [(i, i ^ k) for i in range(peers)]) if k else array
+
+
+def swap_to_previous(array, k):
+    peers = lax.axis_size("ctx")
+    pipes = lax.axis_size("pipe")
+    pairs = [
+        (pipe * peers + i, (pipe - 1) % pipes * peers + (i ^ k))
+        for pipe in range(pipes)
+        for i in range(peers)
     ]
-
-
-def back_to_previous(arrays):
-    peers = len(arrays)
-    pipes = lax.axis_size("pipe")
-    return [
-        lax.ppermute(
-            array,
-            ("pipe", "ctx"),
-            [
-                (pipe * peers + i, (pipe - 1) % pipes * peers + (i ^ k))
-                for pipe in range(pipes)
-                for i in range(peers)
-            ],
-        )
-        for k, array in zip(sending_order(peers), arrays)
-    ]
+    return lax.ppermute(array, ("pipe", "ctx"), pairs)
 
 
 def shards(qkv_proj, cotangent, block_dest, doc_start, mr_filter):
@@ -412,40 +414,41 @@
     bases = jnp.stack([causal, anti], axis=1)
 
     to_previous = [(pipe, (pipe - 1) % pipes) for pipe in range(pipes)]
-    received = []
+    order = sending_order(peers)
+    products, side = multiply(chunks, width, peers, qkv_proj, cotangent, doc_start)
+    received = [swap(array, k) for array, k in zip(products[0], order)]
+    side = lax.ppermute(side, "pipe", to_previous)
+
+    first_out, first_back = OUT_FIRST * peers // 8, BACK_FIRST * peers // 8
+    masks = document_masks(me_at, meta, received, MARK_ROWS)
+    backs, late = [], []
     for chunk in range(chunks):
-        stacked = chunk > 0
-        products = multiply(
-            chunk,
-            width,
-            peers,
-            qkv_proj,
-            cotangent,
-            doc_start if chunk == 0 else None,
-            stacked,
-            chunk == chunks - 1,
+        coming = products[chunk + 1] if chunk + 1 < chunks else []
+        waiting = coming[first_out:]
+        convolved, passed = convolve(
+            group_size, me_at, meta, received, masks, bases[chunk], waiting + late
         )
-        products = list(products)
-        if chunk == chunks - 1:
-            side = lax.ppermute(products.pop(), "pipe", to_previous)
-        if stacked:
-            received.append([lax.all_to_all(products[0], "ctx", 0, 0, tiled=True)])
-        else:
-            received.append(exchanged(products))
-    masks = document_masks(me_at, meta, received[0], MARK_ROWS)
-    backs = []
+        received = [
+            swap(array, k)
+            for array, k in zip(coming[:first_out] + passed[: len(waiting)], order)
+        ]
+        if chunk:
+            backs[-1] += [
+                swap_to_previous(array, k)
+                for array, k in zip(passed[len(waiting) :], order[first_back:])
+            ]
+        now = first_back if coming else peers
+        backs.append([swap_to_previous(array, k) for array, k in zip(convolved[:now], order)])
+        late = convolved[now:]
+
+    result = None
     for chunk in range(chunks):
-        convolved = convolve(group_size, me_at, meta, received[chunk], masks, bases[chunk])
-        backs.append(back_to_previous(convolved))
-
-    result, held = None, []
-    for chunk in range(chunks):
+        others = [result] if chunk else backs[1][:GRADIENTS_AFTER] if chunks > 1 else []
         result, cross = gradients(
-            chunk, chunks, me_at, tp_at, tp_count, meta, backs[chunk], side, result
+            chunk, chunks, me_at, tp_at, tp_count, meta, backs[chunk], side, others
         )
-        held.append(lax.ppermute(cross, "tp", [(0, 1), (1, 0)]))
-    for chunk in range(chunks):
-        result = place(chunk, chunks, tp_at, meta, held[chunk], result)
+        cross = lax.ppermute(cross, "tp", [(0, 1), (1, 0)])
+        result = place(chunk, chunks, tp_at, meta, cross, result)
     return result
 
 

time: 147 us -> 141 us (0.959); the launches traced: 145 us -> 141 us
  Pallas kernels: 41.2 us -> 27.9 us
  waiting for transfers between devices: 39.3 us -> 46.5 us
  starting transfers between devices: 59.3 us -> 61.4 us
    pallas_call x6 -> x5, Pallas kernels: 33.3 us -> 23.6 us  [the longest x2 14.7 us: convolve(): pl.pallas_call(functools.partial(conv_kernel, group_size, me_at, peers, l...]
    ppermute x26 -> x33, starting transfers between devices: 53.8 us -> 61.4 us  [the longest x16 28.9 us: swap_to_previous(): return lax.ppermute(array, ('pipe', 'ctx'), pairs)]
    ppermute x26 -> x33, waiting for transfers between devices: 39.3 us -> 46.5 us  [the longest x16 30.8 us: swap_to_previous(): return lax.ppermute(array, ('pipe', 'ctx'), pairs)]
    all_to_all x1 -> x0, starting transfers between devices: 5.55 us -> none  [shards(): received.append([lax.all_to_all(products[0], 'ctx', 0, 0, tiled=True)])]
    pallas_call x2, Pallas kernels: 5.45 us -> 2.94 us  [place(): pl.pallas_call(place_kernel, out_shape=jax.ShapeDtypeStruct(result.shape,...]
    unnamed x38 -> x12, local copies, waits for them, and re-layouts: 2.68 us -> 3.62 us
  transfers between devices with their start and end apart: 27 -> 33, of which waited for: 8 -> 17; matrix products, arithmetic and copies ran while one was open for 1% -> 1% of each run, Pallas kernels for 24% -> 13%
where the time goes in v1:
time: 141 us
  starting transfers between devices  61.4 us (44%)
  waiting for transfers between devices  46.5 us (33%)
  Pallas kernels  27.9 us (20%)
  local copies, waits for them, and re-layouts  3.77 us (3%)
    ppermute x16, waiting for transfers between devices, swap_to_previous(): return lax.ppermute(array, ('pipe', 'ctx'), pairs)  30.8 us
    ppermute x16, starting transfers between devices, swap_to_previous(): return lax.ppermute(array, ('pipe', 'ctx'), pairs)  28.9 us
    ppermute x14, starting transfers between devices, swap(): lax.ppermute(array, 'ctx', [(i, i ^ k) for i in range(peers)])  25.1 us
    pallas_call x2, Pallas kernels, convolve(): pl.pallas_call(functools.partial(conv_kernel, group_size, me_at, peers, l...  14.7 us
    ppermute x14, waiting for transfers between devices, swap(): lax.ppermute(array, 'ctx', [(i, i ^ k) for i in range(peers)])  11.8 us
    ppermute x2, starting transfers between devices, shards(): cross = lax.ppermute(cross, 'tp', [(0, 1), (1, 0)])  6.16 us
    pallas_call x1, Pallas kernels, multiply(): pl.pallas_call(functools.partial(multiply_kernel, chunks), out_shape=[jax...  4.81 us
    pallas_call x2, Pallas kernels, gradients(): pl.pallas_call(functools.partial(gradients_kernel, me_at, tp_at, peers),...  4.01 us
  transfers between devices with their start and end apart: 33, of which 17 were waited for; matrix products, arithmetic and copies ran while one was open for 1% of the time, Pallas kernels for 13%

profile of v1, /device:TPU:21, one launch (start us, length us, event | category | flops | bytes accessed | tf_op | source)
XLA Modules:
  0.0 140.5 jit_solution(9345584698307008334)
XLA Ops:
  0.0 4.8 %multiply.1 = (bf16[272,256]{1,0:T(8,128)(2,1)}, bf16[272,256]{1,0:T(8,128)(2,1)}, bf16[272,256]{1,0:T(8,128)(2,1)}, bf16[272,256]{1,0:T(8,128)(2,1)}, bf16[272,...) custom-call(bf16[1,3,128,4096]{3,2,1,0:T(8,128)(2,1)} %proj_ref.1, ...), custom_call_target="tpu_custom_call" | custom-call | flops 1048576 | bytes 9437184 | tf_op jit(solution)/shard_map/multiply/pallas_call | solution.py:98
  4.8 1.3 collective-permute-start
  6.2 2.3 %collective-permute-start.2 = (bf16[272,256]{1,0:T(8,128)(2,1)}, bf16[272,256]{1,0:T(8,128)(2,1)S(1)}, u32[]{:S(2)}, u32[]{:S(2)}) collective-permute-start(bf16[272,256]{1,0:T(8,128)(2,1)} %get-tuple-element.52), channel_id=1, source_target_pairs={{0,10},{2,8},{4,14},{6,12},{8,2},{10,0},{12,6},{14,4},{1,11},{3,9}... | collective-permute-start | bytes 417800 | tf_op jit(solution)/shard_map/ppermute | solution.py:374
  8.4 1.2 collective-permute-start.3
  10.7 6.9 %collective-permute-done.1.refs_0_ = bf16[272,256]{1,0:T(8,128)(2,1)S(1)} collective-permute-done((bf16[272,256]{1,0:T(8,128)(2,1)}, bf16[272,256]{1,0:T(8,128)(2,1)S(1)}, u32[]{:S(2)}, u32[]{:S(2)}) %collective-permute-start.1) | collective-permute-done | bytes 139296 | tf_op jit(solution)/shard_map/ppermute | solution.py:374
  17.6 5.3 %collective-permute-start.5 = (bf16[272,256]{1,0:T(8,128)(2,1)}, bf16[272,256]{1,0:T(8,128)(2,1)S(1)}, u32[]{:S(2)}, u32[]{:S(2)}) collective-permute-start(bf16[272,256]{1,0:T(8,128)(2,1)} %get-tuple-element.55), channel_id=1, source_target_pairs={{0,4},{2,6},{4,0},{6,2},{8,12},{10,14},{12,8},{14,10},{1,5},{3,7},... | collective-permute-start | bytes 417800 | tf_op jit(solution)/shard_map/ppermute | solution.py:374
  22.9 1.1 collective-permute-start.6
  24.1 2.8 %collective-permute-start.7 = (bf16[272,256]{1,0:T(8,128)(2,1)}, bf16[272,256]{1,0:T(8,128)(2,1)S(1)}, u32[]{:S(2)}, u32[]{:S(2)}) collective-permute-start(bf16[272,256]{1,0:T(8,128)(2,1)} %get-tuple-element.57), channel_id=1, source_target_pairs={{0,6},{2,4},{4,2},{6,0},{8,14},{10,12},{12,10},{14,8},{1,7},{3,5},... | collective-permute-start | bytes 417800 | tf_op jit(solution)/shard_map/ppermute | solution.py:374
  26.9 0.9 collective-permute-done.4.refs_4_
  27.8 1.2 collective-permute-start.8
  29.1 1.1 collective-permute-start.9
  30.6 4.0 %collective-permute-start.10 = (bf16[256,256]{1,0:T(8,128)(2,1)}, bf16[256,256]{1,0:T(8,128)(2,1)S(1)}, u32[]{:S(2)}, u32[]{:S(2)}) collective-permute-start(bf16[256,256]{1,0:T(8,128)(2,1)} %get-tuple-element.61), channel_id=1, source_target_pairs={{0,2},{2,0},{4,6},{6,4},{8,10},{10,8},{12,14},{14,12},{1,3},{3,1},... | collective-permute-start | bytes 393224 | tf_op jit(solution)/shard_map/ppermute | solution.py:374
  34.6 1.0 collective-permute-start.11
  35.6 0.9 copy-done.1
  36.5 1.4 %masks.1.mask_ref = bf16[8,2,128,256]{3,2,1,0:T(8,128)(2,1)S(1)} custom-call(s32[66]{0:T(128)S(1)} %pad_add_fusion.meta_ref, bf16[272,256]{1,0:T(8,128)(2,1)S(1)} %collective-permute-done.1.refs_0_, bf16[272,256]{1,0:T(8,128)(2,1)S(1)} %copy-done.1, bf16[272,256]{1,0:T(8,128)(2,1)S(1)} %collective-permute-done.2.refs_2_, ...), custom_call_target="tpu_custom_call" | custom-call | flops 1048576 | bytes 1048576 | tf_op jit(solution)/shard_map/masks/pallas_call | solution.py:171
  37.9 0.9 copy-done.3
  38.8 0.9 copy-done.4
  39.7 0.9 copy-done.5
  40.6 7.6 %convolve.2 = (bf16[256,256]{1,0:T(8,128)(2,1)S(1)}, bf16[256,256]{1,0:T(8,128)(2,1)S(1)}, bf16[256,256]{1,0:T(8,128)(2,1)S(1)}, bf16[256,256]{1,0:T(8,128)(2,1)...) custom-call(s32[66]{0:T(128)S(1)} %pad_add_fusion.meta_ref, ...), custom_call_target="tpu_custom_call", output_to_operand_aliasing={{8}: (11, {}), {9}: (12, {}), {10}: (13, {})} | custom-call | flops 2147483648 | bytes 2621440 | tf_op jit(solution)/shard_map/convolve/pallas_call | solution.py:257
  48.3 3.9 %collective-permute-start.12 = (bf16[256,256]{1,0:T(8,128)(2,1)S(1)}, bf16[256,256]{1,0:T(8,128)(2,1)S(1)}, u32[]{:S(2)}, u32[]{:S(2)}) collective-permute-start(bf16[256,256]{1,0:T(8,128)(2,1)S(1)} %get-tuple-element.66), channel_id=1, source_target_pairs={{0,4},{2,6},{4,0},{6,2},{8,12},{10,14},{12,8},{14,10},{1,5},{3,7},... | collective-permute-start | bytes 393224 | tf_op jit(solution)/shard_map/ppermute | solution.py:374
  52.2 1.0 collective-permute-start.14
  53.2 2.5 %collective-permute-start.23 = (bf16[256,256]{1,0:T(8,128)(2,1)S(1)}, bf16[256,256]{1,0:T(8,128)(2,1)S(1)}, u32[]{:S(2)}, u32[]{:S(2)}) collective-permute-start(bf16[256,256]{1,0:T(8,128)(2,1)S(1)} %get-tuple-element.81), channel_id=1, source_target_pairs={{0,24},{2,26},{4,28},{6,30},{8,16},{10,18},{12,20},{14,22},{16,8},... | collective-permute-start | bytes 393224 | tf_op jit(solution)/shard_map/ppermute | solution.py:385
  56.9 1.0 collective-permute-done.13.refs_6_
  58.0 2.3 %collective-permute-start.25 = (bf16[256,256]{1,0:T(8,128)(2,1)S(1)}, bf16[256,256]{1,0:T(8,128)(2,1)S(1)}, u32[]{:S(2)}, u32[]{:S(2)}) collective-permute-start(bf16[256,256]{1,0:T(8,128)(2,1)S(1)} %get-tuple-element.83), channel_id=1, source_target_pairs={{0,26},{2,24},{4,30},{6,28},{8,18},{10,16},{12,22},{14,20},{16,10}... | collective-permute-start | bytes 393224 | tf_op jit(solution)/shard_map/ppermute | solution.py:385
  60.3 1.8 %collective-permute-done.14.refs_7_ = bf16[256,256]{1,0:T(8,128)(2,1)S(1)} collective-permute-done((bf16[256,256]{1,0:T(8,128)(2,1)S(1)}, bf16[256,256]{1,0:T(8,128)(2,1)S(1)}, u32[]{:S(2)}, u32[]{:S(2)}) %collective-permute-start.14) | collective-permute-done | bytes 131104 | tf_op jit(solution)/shard_map/ppermute | solution.py:374
  62.0 7.1 %convolve.3 = (bf16[256,256]{1,0:T(8,128)(2,1)S(1)}, bf16[256,256]{1,0:T(8,128)(2,1)S(1)}, bf16[256,256]{1,0:T(8,128)(2,1)S(1)}, bf16[256,256]{1,0:T(8,128)(2,1)...) custom-call(s32[66]{0:T(128)S(1)} %pad_add_fusion.meta_ref, ...), custom_call_target="tpu_custom_call", output_to_operand_aliasing={{8}: (11, {}), {9}: (12, {}), {10}: (13, {}), {11}: (14, {})} | custom-call | flops 2147483648 | bytes 2621440 | tf_op jit(solution)/shard_map/convolve/pallas_call | solution.py:257
  69.2 4.4 %collective-permute-start.15 = (bf16[256,256]{1,0:T(8,128)(2,1)S(1)}, bf16[256,256]{1,0:T(8,128)(2,1)S(1)}, u32[]{:S(2)}, u32[]{:S(2)}) collective-permute-start(bf16[256,256]{1,0:T(8,128)(2,1)S(1)} %get-tuple-element.73), channel_id=1, source_target_pairs={{0,24},{2,26},{4,28},{6,30},{8,16},{10,18},{12,20},{14,22},{16,8},... | collective-permute-start | bytes 393224 | tf_op jit(solution)/shard_map/ppermute | solution.py:385
  73.6 11.7 %collective-permute-done.24.refs_1_ = bf16[256,256]{1,0:T(8,128)(2,1)S(1)} collective-permute-done((bf16[256,256]{1,0:T(8,128)(2,1)S(1)}, bf16[256,256]{1,0:T(8,128)(2,1)S(1)}, u32[]{:S(2)}, u32[]{:S(2)}) %collective-permute-start.24) | collective-permute-done | bytes 131104 | tf_op jit(solution)/shard_map/ppermute | solution.py:385
  85.3 1.2 collective-permute-start.16
  86.6 1.5 %collective-permute-done.26.refs_3_ = bf16[256,256]{1,0:T(8,128)(2,1)S(1)} collective-permute-done((bf16[256,256]{1,0:T(8,128)(2,1)S(1)}, bf16[256,256]{1,0:T(8,128)(2,1)S(1)}, u32[]{:S(2)}, u32[]{:S(2)}) %collective-permute-start.26) | collective-permute-done | bytes 131104 | tf_op jit(solution)/shard_map/ppermute | solution.py:385
  88.1 2.2 %collective-permute-start.18 = (bf16[256,256]{1,0:T(8,128)(2,1)S(1)}, bf16[256,256]{1,0:T(8,128)(2,1)S(1)}, u32[]{:S(2)}, u32[]{:S(2)}) collective-permute-start(bf16[256,256]{1,0:T(8,128)(2,1)S(1)} %get-tuple-element.76), channel_id=1, source_target_pairs={{0,18},{2,16},{4,22},{6,20},{8,26},{10,24},{12,30},{14,28},{16,2},... | collective-permute-start | bytes 393224 | tf_op jit(solution)/shard_map/ppermute | solution.py:385
  91.3 1.7 %collective-permute-start.20 = (bf16[256,256]{1,0:T(8,128)(2,1)S(1)}, bf16[256,256]{1,0:T(8,128)(2,1)S(1)}, u32[]{:S(2)}, u32[]{:S(2)}) collective-permute-start(bf16[256,256]{1,0:T(8,128)(2,1)S(1)} %get-tuple-element.78), channel_id=1, source_target_pairs={{0,20},{2,22},{4,16},{6,18},{8,28},{10,30},{12,24},{14,26},{16,4},... | collective-permute-start | bytes 393224 | tf_op jit(solution)/shard_map/ppermute | solution.py:385
  93.1 1.6 %collective-permute-start.21 = (bf16[256,256]{1,0:T(8,128)(2,1)S(1)}, bf16[256,256]{1,0:T(8,128)(2,1)S(1)}, u32[]{:S(2)}, u32[]{:S(2)}) collective-permute-start(bf16[256,256]{1,0:T(8,128)(2,1)S(1)} %get-tuple-element.79), channel_id=1, source_target_pairs={{0,30},{2,28},{4,26},{6,24},{8,22},{10,20},{12,18},{14,16},{16,14}... | collective-permute-start | bytes 393224 | tf_op jit(solution)/shard_map/ppermute | solution.py:385
  94.7 5.2 %collective-permute-done.18.refs_11_.refs_3_ = bf16[256,256]{1,0:T(8,128)(2,1)S(1)} collective-permute-done((bf16[256,256]{1,0:T(8,128)(2,1)S(1)}, bf16[256,256]{1,0:T(8,128)(2,1)S(1)}, u32[]{:S(2)}, u32[]{:S(2)}) %collective-permute-start.18) | collective-permute-done | bytes 131104 | tf_op jit(solution)/shard_map/ppermute | solution.py:385
  99.9 6.5 %collective-permute-start.28 = (bf16[256,256]{1,0:T(8,128)(2,1)S(1)}, bf16[256,256]{1,0:T(8,128)(2,1)S(1)}, u32[]{:S(2)}, u32[]{:S(2)}) collective-permute-start(bf16[256,256]{1,0:T(8,128)(2,1)S(1)} %get-tuple-element.86), channel_id=1, source_target_pairs={{0,20},{2,22},{4,16},{6,18},{8,28},{10,30},{12,24},{14,26},{16,4},... | collective-permute-start | bytes 393224 | tf_op jit(solution)/shard_map/ppermute | solution.py:385
  106.4 2.6 %collective-permute-start.29 = (bf16[256,256]{1,0:T(8,128)(2,1)S(1)}, bf16[256,256]{1,0:T(8,128)(2,1)S(1)}, u32[]{:S(2)}, u32[]{:S(2)}) collective-permute-start(bf16[256,256]{1,0:T(8,128)(2,1)S(1)} %get-tuple-element.87), channel_id=1, source_target_pairs={{0,30},{2,28},{4,26},{6,24},{8,22},{10,20},{12,18},{14,16},{16,14}... | collective-permute-start | bytes 393224 | tf_op jit(solution)/shard_map/ppermute | solution.py:385
  109.0 2.5 %collective-permute-start.30 = (bf16[256,256]{1,0:T(8,128)(2,1)S(1)}, bf16[256,256]{1,0:T(8,128)(2,1)S(1)}, u32[]{:S(2)}, u32[]{:S(2)}) collective-permute-start(bf16[256,256]{1,0:T(8,128)(2,1)S(1)} %get-tuple-element.88), channel_id=1, source_target_pairs={{0,22},{2,20},{4,18},{6,16},{8,30},{10,28},{12,26},{14,24},{16,6},... | collective-permute-start | bytes 393224 | tf_op jit(solution)/shard_map/ppermute | solution.py:385
  111.5 0.9 collective-permute-done.28.refs_5_
  112.4 6.7 %collective-permute-done.29.refs_6_ = bf16[256,256]{1,0:T(8,128)(2,1)S(1)} collective-permute-done((bf16[256,256]{1,0:T(8,128)(2,1)S(1)}, bf16[256,256]{1,0:T(8,128)(2,1)S(1)}, u32[]{:S(2)}, u32[]{:S(2)}) %collective-permute-start.29) | collective-permute-done | bytes 131104 | tf_op jit(solution)/shard_map/ppermute | solution.py:385
  119.2 0.9 collective-permute-done.30.refs_7_
  120.0 2.0 %gradients.2 = (bf16[1,3,64,8192]{3,2,1,0:T(8,128)(2,1)}, bf16[3,64,2048]{2,1,0:T(8,128)(2,1)S(1)}) custom-call(s32[66]{0:T(128)S(1)} %pad_add_fusion.meta_ref, bf16[3,128,4096]{2,1,0:T(8,128)(2,1)S(1)} %collective-permute-done.side_ref, bf16[256,256]{1,0:T(8,128)(2,1)S(1)} %collective-permute-done.23.refs_0_, ...), custom_call_target="tpu_custom_call" | custom-call | flops 786432 | bytes 4194304 | tf_op jit(solution)/shard_map/gradients/pallas_call | solution.py:331
  122.1 5.4 %collective-permute-start.31 = (bf16[3,64,2048]{2,1,0:T(8,128)(2,1)S(1)}, bf16[3,64,2048]{2,1,0:T(8,128)(2,1)S(1)}, u32[]{:S(2)}, u32[]{:S(2)}) collective-permute-start(bf16[3,64,2048]{2,1,0:T(8,128)(2,1)S(1)} %get-tuple-element.89), channel_id=1, source_target_pairs={{0,1},{1,0},{2,3},{3,2},{4,5},{5,4},{6,7},{7,6},{8,9},{9,8},{10,11... | collective-permute-start | bytes 2359304 | tf_op jit(solution)/shard_map/ppermute | solution.py:450
  127.4 1.9 %collective-permute-done.31.cross_ref = bf16[3,64,2048]{2,1,0:T(8,128)(2,1)S(1)} collective-permute-done((bf16[3,64,2048]{2,1,0:T(8,128)(2,1)S(1)}, bf16[3,64,2048]{2,1,0:T(8,128)(2,1)S(1)}, u32[]{:S(2)}, u32[]{:S(2)}) %collective-permute-start.31) | collective-permute-done | bytes 786464 | tf_op jit(solution)/shard_map/ppermute | solution.py:450
  129.3 1.5 %place.2.refs_8_ = bf16[1,3,64,8192]{3,2,1,0:T(8,128)(2,1)} custom-call(s32[66]{0:T(128)S(1)} %pad_add_fusion.meta_ref, bf16[3,64,2048]{2,1,0:T(8,128)(2,1)S(1)} %collective-permute-done.31.cross_ref, bf16[1,3,64,8192]{3,2,1,0:T(8,128)(2,1)} %get-tuple-element.90.held_ref), custom_call_target="tpu_custom_call", output_to_operand_aliasing={{}: (2, {})} | custom-call | bytes 1572864 | tf_op jit(solution)/shard_map/place/pallas_call | solution.py:354
  130.8 3.5 %collective-permute-done.22.refs_7_ = bf16[256,256]{1,0:T(8,128)(2,1)S(1)} collective-permute-done((bf16[256,256]{1,0:T(8,128)(2,1)S(1)}, bf16[256,256]{1,0:T(8,128)(2,1)S(1)}, u32[]{:S(2)}, u32[]{:S(2)}) %collective-permute-start.22) | collective-permute-done | bytes 131104 | tf_op jit(solution)/shard_map/ppermute | solution.py:385
  134.4 2.0 %gradients.3 = (bf16[1,3,64,8192]{3,2,1,0:T(8,128)(2,1)}, bf16[3,64,2048]{2,1,0:T(8,128)(2,1)S(1)}) custom-call(s32[66]{0:T(128)S(1)} %pad_add_fusion.meta_ref, bf16[3,128,4096]{2,1,0:T(8,128)(2,1)S(1)} %collective-permute-done.side_ref, bf16[256,256]{1,0:T(8,128)(2,1)S(1)} %collective-permute-done.15.refs_8_.refs_0_, ...), custom_call_target="tpu_custom_call", output_to_operand_aliasing={{0}: (10, {})} | custom-call | flops 786432 | bytes 4194304 | tf_op jit(solution)/shard_map/gradients/pallas_call | solution.py:331
  137.1 1.9 %collective-permute-done.32.cross_ref = bf16[3,64,2048]{2,1,0:T(8,128)(2,1)S(1)} collective-permute-done((bf16[3,64,2048]{2,1,0:T(8,128)(2,1)S(1)}, bf16[3,64,2048]{2,1,0:T(8,128)(2,1)S(1)}, u32[]{:S(2)}, u32[]{:S(2)}) %collective-permute-start.32) | collective-permute-done | bytes 786464 | tf_op jit(solution)/shard_map/ppermute | solution.py:450
  139.1 1.5 %place.3 = bf16[1,3,64,8192]{3,2,1,0:T(8,128)(2,1)} custom-call(s32[66]{0:T(128)S(1)} %pad_add_fusion.meta_ref, bf16[3,64,2048]{2,1,0:T(8,128)(2,1)S(1)} %collective-permute-done.32.cross_ref, bf16[1,3,64,8192]{3,2,1,0:T(8,128)(2,1)} %get-tuple-element.92.held_ref), custom_call_target="tpu_custom_call", output_to_operand_aliasing={{}: (2, {})} | custom-call | bytes 1572864 | tf_op jit(solution)/shard_map/place/pallas_call | solution.py:354
  (44 shorter events, 5.0 us)
Async XLA Ops:
  0.0 10.5 %copy-start = (s32[2,64]{1,0:T(2,128)S(1)}, s32[2,64]{1,0:T(2,128)}, u32[]{:S(2)}) copy-start(s32[2,64]{1,0:T(2,128)} %param.7) | copy-start | bytes 1540
  4.8 115.2 %collective-permute-start = (bf16[3,128,4096]{2,1,0:T(8,128)(2,1)}, bf16[3,128,4096]{2,1,0:T(8,128)(2,1)S(1)}, u32[]{:S(2)}, u32[]{:S(2)}) collective-permute-start(bf16[3,128,4096]{2,1,0:T(8,128)(2,1)} %get-tuple-element.49), channel_id=1, source_target_pairs={{0,16},{16,0},{1,17},{17,1},{2,18},{18,2},{3,19},{19,3},{4,20},{20... | collective-permute-start | bytes 9437192 | tf_op jit(solution)/shard_map/ppermute | solution.py:420
  6.1 11.5 %collective-permute-start.1 = (bf16[272,256]{1,0:T(8,128)(2,1)}, bf16[272,256]{1,0:T(8,128)(2,1)S(1)}, u32[]{:S(2)}, u32[]{:S(2)}) collective-permute-start(bf16[272,256]{1,0:T(8,128)(2,1)} %get-tuple-element.50), channel_id=1, source_target_pairs={{0,8},{2,10},{4,12},{6,14},{8,0},{10,2},{12,4},{14,6},{1,9},{3,11}... | collective-permute-start | bytes 417800 | tf_op jit(solution)/shard_map/ppermute | solution.py:374
  6.2 16.8 %collective-permute-start.2 = (bf16[272,256]{1,0:T(8,128)(2,1)}, bf16[272,256]{1,0:T(8,128)(2,1)S(1)}, u32[]{:S(2)}, u32[]{:S(2)}) collective-permute-start(bf16[272,256]{1,0:T(8,128)(2,1)} %get-tuple-element.52), channel_id=1, source_target_pairs={{0,10},{2,8},{4,14},{6,12},{8,2},{10,0},{12,6},{14,4},{1,11},{3,9}... | collective-permute-start | bytes 417800 | tf_op jit(solution)/shard_map/ppermute | solution.py:374
  8.4 15.7 %collective-permute-start.3 = (bf16[272,256]{1,0:T(8,128)(2,1)}, bf16[272,256]{1,0:T(8,128)(2,1)}, u32[]{:S(2)}, u32[]{:S(2)}) collective-permute-start(bf16[272,256]{1,0:T(8,128)(2,1)} %get-tuple-element.53), channel_id=1, source_target_pairs={{0,2},{2,0},{4,6},{6,4},{8,10},{10,8},{12,14},{14,12},{1,3},{3,1},... | collective-permute-start | bytes 417800 | tf_op jit(solution)/shard_map/ppermute | solution.py:374
  9.7 18.2 %collective-permute-start.4 = (bf16[272,256]{1,0:T(8,128)(2,1)}, bf16[272,256]{1,0:T(8,128)(2,1)}, u32[]{:S(2)}, u32[]{:S(2)}) collective-permute-start(bf16[272,256]{1,0:T(8,128)(2,1)} %get-tuple-element.54), channel_id=1, source_target_pairs={{0,12},{2,14},{4,8},{6,10},{8,4},{10,6},{12,0},{14,2},{1,13},{3,15... | collective-permute-start | bytes 417800 | tf_op jit(solution)/shard_map/ppermute | solution.py:374
  17.6 11.5 %collective-permute-start.5 = (bf16[272,256]{1,0:T(8,128)(2,1)}, bf16[272,256]{1,0:T(8,128)(2,1)S(1)}, u32[]{:S(2)}, u32[]{:S(2)}) collective-permute-start(bf16[272,256]{1,0:T(8,128)(2,1)} %get-tuple-element.55), channel_id=1, source_target_pairs={{0,4},{2,6},{4,0},{6,2},{8,12},{10,14},{12,8},{14,10},{1,5},{3,7},... | collective-permute-start | bytes 417800 | tf_op jit(solution)/shard_map/ppermute | solution.py:374
  22.9 7.7 %collective-permute-start.6 = (bf16[272,256]{1,0:T(8,128)(2,1)}, bf16[272,256]{1,0:T(8,128)(2,1)S(1)}, u32[]{:S(2)}, u32[]{:S(2)}) collective-permute-start(bf16[272,256]{1,0:T(8,128)(2,1)} %get-tuple-element.56), channel_id=1, source_target_pairs={{0,14},{2,12},{4,10},{6,8},{8,6},{10,4},{12,2},{14,0},{1,15},{3,13... | collective-permute-start | bytes 417800 | tf_op jit(solution)/shard_map/ppermute | solution.py:374
  24.1 10.5 %collective-permute-start.7 = (bf16[272,256]{1,0:T(8,128)(2,1)}, bf16[272,256]{1,0:T(8,128)(2,1)S(1)}, u32[]{:S(2)}, u32[]{:S(2)}) collective-permute-start(bf16[272,256]{1,0:T(8,128)(2,1)} %get-tuple-element.57), channel_id=1, source_target_pairs={{0,6},{2,4},{4,2},{6,0},{8,14},{10,12},{12,10},{14,8},{1,7},{3,5},... | collective-permute-start | bytes 417800 | tf_op jit(solution)/shard_map/ppermute | solution.py:374
  27.8 20.4 %collective-permute-start.8 = (bf16[256,256]{1,0:T(8,128)(2,1)}, bf16[256,256]{1,0:T(8,128)(2,1)S(1)}, u32[]{:S(2)}, u32[]{:S(2)}) collective-permute-start(bf16[256,256]{1,0:T(8,128)(2,1)} %get-tuple-element.58), channel_id=1, source_target_pairs={{0,8},{2,10},{4,12},{6,14},{8,0},{10,2},{12,4},{14,6},{1,9},{3,11}... | collective-permute-start | bytes 393224 | tf_op jit(solution)/shard_map/ppermute | solution.py:374
  29.1 23.1 %collective-permute-start.9 = (bf16[256,256]{1,0:T(8,128)(2,1)}, bf16[256,256]{1,0:T(8,128)(2,1)S(1)}, u32[]{:S(2)}, u32[]{:S(2)}) collective-permute-start(bf16[256,256]{1,0:T(8,128)(2,1)} %get-tuple-element.60), channel_id=1, source_target_pairs={{0,10},{2,8},{4,14},{6,12},{8,2},{10,0},{12,6},{14,4},{1,11},{3,9}... | collective-permute-start | bytes 393224 | tf_op jit(solution)/shard_map/ppermute | solution.py:374
  30.6 21.6 %collective-permute-start.10 = (bf16[256,256]{1,0:T(8,128)(2,1)}, bf16[256,256]{1,0:T(8,128)(2,1)S(1)}, u32[]{:S(2)}, u32[]{:S(2)}) collective-permute-start(bf16[256,256]{1,0:T(8,128)(2,1)} %get-tuple-element.61), channel_id=1, source_target_pairs={{0,2},{2,0},{4,6},{6,4},{8,10},{10,8},{12,14},{14,12},{1,3},{3,1},... | collective-permute-start | bytes 393224 | tf_op jit(solution)/shard_map/ppermute | solution.py:374
  34.6 18.6 %collective-permute-start.11 = (bf16[256,256]{1,0:T(8,128)(2,1)}, bf16[256,256]{1,0:T(8,128)(2,1)S(1)}, u32[]{:S(2)}, u32[]{:S(2)}) collective-permute-start(bf16[256,256]{1,0:T(8,128)(2,1)} %get-tuple-element.62), channel_id=1, source_target_pairs={{0,12},{2,14},{4,8},{6,10},{8,4},{10,6},{12,0},{14,2},{1,13},{3,15... | collective-permute-start | bytes 393224 | tf_op jit(solution)/shard_map/ppermute | solution.py:374
  35.6 0.9 copy-start.1
  37.9 0.9 copy-start.3
  38.8 0.9 copy-start.4
  39.7 0.9 copy-start.5
  40.6 21.4 %copy-start.2 = (bf16[256,256]{1,0:T(8,128)(2,1)S(1)}, bf16[256,256]{1,0:T(8,128)(2,1)}, u32[]{:S(2)}) copy-start(bf16[256,256]{1,0:T(8,128)(2,1)} %get-tuple-element.59.refs_1_) | copy-start | bytes 393220
  48.3 8.1 %collective-permute-start.12 = (bf16[256,256]{1,0:T(8,128)(2,1)S(1)}, bf16[256,256]{1,0:T(8,128)(2,1)S(1)}, u32[]{:S(2)}, u32[]{:S(2)}) collective-permute-start(bf16[256,256]{1,0:T(8,128)(2,1)S(1)} %get-tuple-element.66), channel_id=1, source_target_pairs={{0,4},{2,6},{4,0},{6,2},{8,12},{10,14},{12,8},{14,10},{1,5},{3,7},... | collective-permute-start | bytes 393224 | tf_op jit(solution)/shard_map/ppermute | solution.py:374
  52.2 5.8 %collective-permute-start.13 = (bf16[256,256]{1,0:T(8,128)(2,1)S(1)}, bf16[256,256]{1,0:T(8,128)(2,1)S(1)}, u32[]{:S(2)}, u32[]{:S(2)}) collective-permute-start(bf16[256,256]{1,0:T(8,128)(2,1)S(1)} %get-tuple-element.67), channel_id=1, source_target_pairs={{0,14},{2,12},{4,10},{6,8},{8,6},{10,4},{12,2},{14,0},{1,15},{3,13... | collective-permute-start | bytes 393224 | tf_op jit(solution)/shard_map/ppermute | solution.py:374
  52.2 9.8 %collective-permute-start.14 = (bf16[256,256]{1,0:T(8,128)(2,1)S(1)}, bf16[256,256]{1,0:T(8,128)(2,1)S(1)}, u32[]{:S(2)}, u32[]{:S(2)}) collective-permute-start(bf16[256,256]{1,0:T(8,128)(2,1)S(1)} %get-tuple-element.68), channel_id=1, source_target_pairs={{0,6},{2,4},{4,2},{6,0},{8,14},{10,12},{12,10},{14,8},{1,7},{3,5},... | collective-permute-start | bytes 393224 | tf_op jit(solution)/shard_map/ppermute | solution.py:374
  53.2 16.0 %collective-permute-start.23 = (bf16[256,256]{1,0:T(8,128)(2,1)S(1)}, bf16[256,256]{1,0:T(8,128)(2,1)S(1)}, u32[]{:S(2)}, u32[]{:S(2)}) collective-permute-start(bf16[256,256]{1,0:T(8,128)(2,1)S(1)} %get-tuple-element.81), channel_id=1, source_target_pairs={{0,24},{2,26},{4,28},{6,30},{8,16},{10,18},{12,20},{14,22},{16,8},... | collective-permute-start | bytes 393224 | tf_op jit(solution)/shard_map/ppermute | solution.py:385
  56.4 28.9 %collective-permute-start.24 = (bf16[256,256]{1,0:T(8,128)(2,1)S(1)}, bf16[256,256]{1,0:T(8,128)(2,1)S(1)}, u32[]{:S(2)}, u32[]{:S(2)}) collective-permute-start(bf16[256,256]{1,0:T(8,128)(2,1)S(1)} %get-tuple-element.82), channel_id=1, source_target_pairs={{0,16},{2,18},{4,20},{6,22},{8,24},{10,26},{12,28},{14,30},{16,0},... | collective-permute-start | bytes 393224 | tf_op jit(solution)/shard_map/ppermute | solution.py:385
  58.0 28.6 %collective-permute-start.25 = (bf16[256,256]{1,0:T(8,128)(2,1)S(1)}, bf16[256,256]{1,0:T(8,128)(2,1)S(1)}, u32[]{:S(2)}, u32[]{:S(2)}) collective-permute-start(bf16[256,256]{1,0:T(8,128)(2,1)S(1)} %get-tuple-element.83), channel_id=1, source_target_pairs={{0,26},{2,24},{4,30},{6,28},{8,18},{10,16},{12,22},{14,20},{16,10}... | collective-permute-start | bytes 393224 | tf_op jit(solution)/shard_map/ppermute | solution.py:385
  62.0 26.0 %collective-permute-start.26 = (bf16[256,256]{1,0:T(8,128)(2,1)S(1)}, bf16[256,256]{1,0:T(8,128)(2,1)S(1)}, u32[]{:S(2)}, u32[]{:S(2)}) collective-permute-start(bf16[256,256]{1,0:T(8,128)(2,1)S(1)} %get-tuple-element.84), channel_id=1, source_target_pairs={{0,18},{2,16},{4,22},{6,20},{8,26},{10,24},{12,30},{14,28},{16,2},... | collective-permute-start | bytes 393224 | tf_op jit(solution)/shard_map/ppermute | solution.py:385
  69.2 21.1 %collective-permute-start.15 = (bf16[256,256]{1,0:T(8,128)(2,1)S(1)}, bf16[256,256]{1,0:T(8,128)(2,1)S(1)}, u32[]{:S(2)}, u32[]{:S(2)}) collective-permute-start(bf16[256,256]{1,0:T(8,128)(2,1)S(1)} %get-tuple-element.73), channel_id=1, source_target_pairs={{0,24},{2,26},{4,28},{6,30},{8,16},{10,18},{12,20},{14,22},{16,8},... | collective-permute-start | bytes 393224 | tf_op jit(solution)/shard_map/ppermute | solution.py:385
  85.3 6.0 %collective-permute-start.16 = (bf16[256,256]{1,0:T(8,128)(2,1)S(1)}, bf16[256,256]{1,0:T(8,128)(2,1)S(1)}, u32[]{:S(2)}, u32[]{:S(2)}) collective-permute-start(bf16[256,256]{1,0:T(8,128)(2,1)S(1)} %get-tuple-element.74), channel_id=1, source_target_pairs={{0,16},{2,18},{4,20},{6,22},{8,24},{10,26},{12,28},{14,30},{16,0},... | collective-permute-start | bytes 393224 | tf_op jit(solution)/shard_map/ppermute | solution.py:385
  86.5 6.6 %collective-permute-start.17 = (bf16[256,256]{1,0:T(8,128)(2,1)S(1)}, bf16[256,256]{1,0:T(8,128)(2,1)S(1)}, u32[]{:S(2)}, u32[]{:S(2)}) collective-permute-start(bf16[256,256]{1,0:T(8,128)(2,1)S(1)} %get-tuple-element.75), channel_id=1, source_target_pairs={{0,26},{2,24},{4,30},{6,28},{8,18},{10,16},{12,22},{14,20},{16,10}... | collective-permute-start | bytes 393224 | tf_op jit(solution)/shard_map/ppermute | solution.py:385
  88.1 11.9 %collective-permute-start.18 = (bf16[256,256]{1,0:T(8,128)(2,1)S(1)}, bf16[256,256]{1,0:T(8,128)(2,1)S(1)}, u32[]{:S(2)}, u32[]{:S(2)}) collective-permute-start(bf16[256,256]{1,0:T(8,128)(2,1)S(1)} %get-tuple-element.76), channel_id=1, source_target_pairs={{0,18},{2,16},{4,22},{6,20},{8,26},{10,24},{12,30},{14,28},{16,2},... | collective-permute-start | bytes 393224 | tf_op jit(solution)/shard_map/ppermute | solution.py:385
  90.2 9.7 %collective-permute-start.19 = (bf16[256,256]{1,0:T(8,128)(2,1)S(1)}, bf16[256,256]{1,0:T(8,128)(2,1)S(1)}, u32[]{:S(2)}, u32[]{:S(2)}) collective-permute-start(bf16[256,256]{1,0:T(8,128)(2,1)S(1)} %get-tuple-element.77), channel_id=1, source_target_pairs={{0,28},{2,30},{4,24},{6,26},{8,20},{10,22},{12,16},{14,18},{16,12}... | collective-permute-start | bytes 393224 | tf_op jit(solution)/shard_map/ppermute | solution.py:385
  91.3 15.1 %collective-permute-start.20 = (bf16[256,256]{1,0:T(8,128)(2,1)S(1)}, bf16[256,256]{1,0:T(8,128)(2,1)S(1)}, u32[]{:S(2)}, u32[]{:S(2)}) collective-permute-start(bf16[256,256]{1,0:T(8,128)(2,1)S(1)} %get-tuple-element.78), channel_id=1, source_target_pairs={{0,20},{2,22},{4,16},{6,18},{8,28},{10,30},{12,24},{14,26},{16,4},... | collective-permute-start | bytes 393224 | tf_op jit(solution)/shard_map/ppermute | solution.py:385
  93.1 15.9 %collective-permute-start.21 = (bf16[256,256]{1,0:T(8,128)(2,1)S(1)}, bf16[256,256]{1,0:T(8,128)(2,1)S(1)}, u32[]{:S(2)}, u32[]{:S(2)}) collective-permute-start(bf16[256,256]{1,0:T(8,128)(2,1)S(1)} %get-tuple-element.79), channel_id=1, source_target_pairs={{0,30},{2,28},{4,26},{6,24},{8,22},{10,20},{12,18},{14,16},{16,14}... | collective-permute-start | bytes 393224 | tf_op jit(solution)/shard_map/ppermute | solution.py:385
  99.9 11.6 %collective-permute-start.27 = (bf16[256,256]{1,0:T(8,128)(2,1)S(1)}, bf16[256,256]{1,0:T(8,128)(2,1)S(1)}, u32[]{:S(2)}, u32[]{:S(2)}) collective-permute-start(bf16[256,256]{1,0:T(8,128)(2,1)S(1)} %get-tuple-element.85), channel_id=1, source_target_pairs={{0,28},{2,30},{4,24},{6,26},{8,20},{10,22},{12,16},{14,18},{16,12}... | collective-permute-start | bytes 393224 | tf_op jit(solution)/shard_map/ppermute | solution.py:385
  99.9 12.5 %collective-permute-start.28 = (bf16[256,256]{1,0:T(8,128)(2,1)S(1)}, bf16[256,256]{1,0:T(8,128)(2,1)S(1)}, u32[]{:S(2)}, u32[]{:S(2)}) collective-permute-start(bf16[256,256]{1,0:T(8,128)(2,1)S(1)} %get-tuple-element.86), channel_id=1, source_target_pairs={{0,20},{2,22},{4,16},{6,18},{8,28},{10,30},{12,24},{14,26},{16,4},... | collective-permute-start | bytes 393224 | tf_op jit(solution)/shard_map/ppermute | solution.py:385
  106.4 12.8 %collective-permute-start.29 = (bf16[256,256]{1,0:T(8,128)(2,1)S(1)}, bf16[256,256]{1,0:T(8,128)(2,1)S(1)}, u32[]{:S(2)}, u32[]{:S(2)}) collective-permute-start(bf16[256,256]{1,0:T(8,128)(2,1)S(1)} %get-tuple-element.87), channel_id=1, source_target_pairs={{0,30},{2,28},{4,26},{6,24},{8,22},{10,20},{12,18},{14,16},{16,14}... | collective-permute-start | bytes 393224 | tf_op jit(solution)/shard_map/ppermute | solution.py:385
  109.0 11.0 %collective-permute-start.30 = (bf16[256,256]{1,0:T(8,128)(2,1)S(1)}, bf16[256,256]{1,0:T(8,128)(2,1)S(1)}, u32[]{:S(2)}, u32[]{:S(2)}) collective-permute-start(bf16[256,256]{1,0:T(8,128)(2,1)S(1)} %get-tuple-element.88), channel_id=1, source_target_pairs={{0,22},{2,20},{4,18},{6,16},{8,30},{10,28},{12,26},{14,24},{16,6},... | collective-permute-start | bytes 393224 | tf_op jit(solution)/shard_map/ppermute | solution.py:385
  122.1 7.3 %collective-permute-start.31 = (bf16[3,64,2048]{2,1,0:T(8,128)(2,1)S(1)}, bf16[3,64,2048]{2,1,0:T(8,128)(2,1)S(1)}, u32[]{:S(2)}, u32[]{:S(2)}) collective-permute-start(bf16[3,64,2048]{2,1,0:T(8,128)(2,1)S(1)} %get-tuple-element.89), channel_id=1, source_target_pairs={{0,1},{1,0},{2,3},{3,2},{4,5},{5,4},{6,7},{7,6},{8,9},{9,8},{10,11... | collective-permute-start | bytes 2359304 | tf_op jit(solution)/shard_map/ppermute | solution.py:450
  127.4 6.9 %collective-permute-start.22 = (bf16[256,256]{1,0:T(8,128)(2,1)S(1)}, bf16[256,256]{1,0:T(8,128)(2,1)S(1)}, u32[]{:S(2)}, u32[]{:S(2)}) collective-permute-start(bf16[256,256]{1,0:T(8,128)(2,1)S(1)} %get-tuple-element.80), channel_id=1, source_target_pairs={{0,22},{2,20},{4,18},{6,16},{8,30},{10,28},{12,26},{14,24},{16,6},... | collective-permute-start | bytes 393224 | tf_op jit(solution)/shard_map/ppermute | solution.py:385
  136.4 2.7 %collective-permute-start.32 = (bf16[3,64,2048]{2,1,0:T(8,128)(2,1)S(1)}, bf16[3,64,2048]{2,1,0:T(8,128)(2,1)S(1)}, u32[]{:S(2)}, u32[]{:S(2)}) collective-permute-start(bf16[3,64,2048]{2,1,0:T(8,128)(2,1)S(1)} %get-tuple-element.91), channel_id=1, source_target_pairs={{0,1},{1,0},{2,3},{3,2},{4,5},{5,4},{6,7},{7,6},{8,9},{9,8},{10,11... | collective-permute-start | bytes 2359304 | tf_op jit(solution)/shard_map/ppermute | solution.py:450

commit v2 on v1

--- a/solution.py
+++ b/solution.py
@@ -12,8 +12,7 @@
 CHUNKS = 2
 MARK_ROWS = 16
 OUT_FIRST = 5
-BACK_FIRST = 4
-GRADIENTS_AFTER = 7
+BACK_FIRST = 5
 F32 = jnp.float32
 BF16 = jnp.bfloat16
 
@@ -32,7 +31,7 @@
 
 def sending_order(peers):
     half = peers // 2
-    return [k for i in range(half) for k in (half + i, i)]
+    return [k for i in range(half) for k in (i, half + i)]
 
 
 def multiply_kernel(chunks, proj_ref, grad_ref, marks_ref, *refs):
@@ -186,10 +185,10 @@
     )(meta, *received)
 
 
-def conv_kernel(group_size, me_at, peers, passing, meta_ref, mask_ref, base_ref, *refs):
+def conv_kernel(group_size, me_at, peers, meta_ref, mask_ref, base_ref, *refs):
     rows32, rows16, toep = refs[-3:]
     recv = refs[:peers]
-    outs = refs[peers + passing : 2 * peers + passing]
+    outs = refs[peers : 2 * peers]
     me = meta_ref[me_at]
     arrivals = [(me ^ k, recv_ref) for k, recv_ref in zip(sending_order(peers), recv)]
     tile = LANES
@@ -247,22 +246,18 @@
             )
 
 
-def convolve(group_size, me_at, meta, received, masks, bases, passing):
+def convolve(group_size, me_at, meta, received, masks, bases):
     peers = masks.shape[0]
     tile = LANES
     width = received[0].shape[-1]
     groups = bases.shape[1]
     out = (2 * tile, width)
-    anywhere = [pl.BlockSpec(memory_space=pl.ANY)] * len(passing)
     outs = pl.pallas_call(
-        functools.partial(conv_kernel, group_size, me_at, peers, len(passing)),
-        out_shape=[jax.ShapeDtypeStruct(out, BF16)] * peers
-        + [jax.ShapeDtypeStruct(p.shape, BF16) for p in passing],
+        functools.partial(conv_kernel, group_size, me_at, peers),
+        out_shape=[jax.ShapeDtypeStruct(out, BF16)] * peers,
         in_specs=[smem(), whole_block(*masks.shape), whole_block(*bases.shape)]
-        + [whole_block(*r.shape) for r in received]
-        + anywhere,
-        out_specs=[whole_block(*out)] * peers + anywhere,
-        input_output_aliases={3 + peers + i: peers + i for i in range(len(passing))},
+        + [whole_block(*r.shape) for r in received],
+        out_specs=[whole_block(*out)] * peers,
         scratch_shapes=[
             pltpu.VMEM((2, peers * tile, width), F32),
             pltpu.VMEM((2, (peers + 1) * tile, width), BF16),
@@ -276,8 +271,8 @@
         ),
         grid=(1,),
         name="convolve",
-    )(meta, masks, bases, *received, *passing)
-    return list(outs[:peers]), list(outs[peers:])
+    )(meta, masks, bases, *received)
+    return list(outs)
 
 
 def gradients_kernel(me_at, tp_at, peers, meta_ref, side_ref, *refs):
@@ -424,31 +419,30 @@
     backs, late = [], []
     for chunk in range(chunks):
         coming = products[chunk + 1] if chunk + 1 < chunks else []
-        waiting = coming[first_out:]
-        convolved, passed = convolve(
-            group_size, me_at, meta, received, masks, bases[chunk], waiting + late
-        )
-        received = [
-            swap(array, k)
-            for array, k in zip(coming[:first_out] + passed[: len(waiting)], order)
-        ]
+        convolved = convolve(group_size, me_at, meta, received, masks, bases[chunk])
+        convolved, waited, late = lax.optimization_barrier((convolved, coming[first_out:], late))
+        received = [swap(array, k) for array, k in zip(coming[:first_out] + waited, order)]
         if chunk:
             backs[-1] += [
-                swap_to_previous(array, k)
-                for array, k in zip(passed[len(waiting) :], order[first_back:])
+                swap_to_previous(array, k) for array, k in zip(late, order[first_back:])
             ]
+        if coming:
+            late = convolved[first_back:]
+        else:
+            last, side = lax.optimization_barrier((convolved[first_back:], side))
+            convolved = convolved[:first_back] + last
         now = first_back if coming else peers
         backs.append([swap_to_previous(array, k) for array, k in zip(convolved[:now], order)])
-        late = convolved[now:]
-
-    result = None
+
+    result, held = None, []
     for chunk in range(chunks):
-        others = [result] if chunk else backs[1][:GRADIENTS_AFTER] if chunks > 1 else []
+        others = [result] if chunk else [array for back in backs[1:] for array in back]
         result, cross = gradients(
             chunk, chunks, me_at, tp_at, tp_count, meta, backs[chunk], side, others
         )
-        cross = lax.ppermute(cross, "tp", [(0, 1), (1, 0)])
-        result = place(chunk, chunks, tp_at, meta, cross, result)
+        held.append(lax.ppermute(cross, "tp", [(0, 1), (1, 0)]))
+    for chunk in range(chunks):
+        result = place(chunk, chunks, tp_at, meta, held[chunk], result)
     return result
 
 

time: 141 us -> 139 us (0.986)
  the two profiles are of different devices: /device:TPU:21 before, /device:TPU:0 now
where the time goes in v2:
time: 139 us
  starting transfers between devices  76.6 us (55%)
  waiting for transfers between devices  32.7 us (24%)
  Pallas kernels  27.9 us (20%)
    ppermute x16, starting transfers between devices, swap_to_previous(): return lax.ppermute(array, ('pipe', 'ctx'), pairs)  47.1 us
    ppermute x14, starting transfers between devices, swap(): lax.ppermute(array, 'ctx', [(i, i ^ k) for i in range(peers)])  25.9 us
    ppermute x14, waiting for transfers between devices, swap(): lax.ppermute(array, 'ctx', [(i, i ^ k) for i in range(peers)])  17.7 us
    pallas_call x2, Pallas kernels, convolve(): pl.pallas_call(functools.partial(conv_kernel, group_size, me_at, peers),...  14.7 us
    ppermute x16, waiting for transfers between devices, swap_to_previous(): return lax.ppermute(array, ('pipe', 'ctx'), pairs)  14.5 us
    pallas_call x1, Pallas kernels, multiply(): pl.pallas_call(functools.partial(multiply_kernel, chunks), out_shape=[jax...  4.81 us
    pallas_call x2, Pallas kernels, gradients(): pl.pallas_call(functools.partial(gradients_kernel, me_at, tp_at, peers),...  4.01 us
    ppermute x1, starting transfers between devices, shards(): side = lax.ppermute(side, 'pipe', to_previous)  3 us
  transfers between devices with their start and end apart: 33, of which 14 were waited for; matrix products, arithmetic and copies ran while one was open for 1% of the time, Pallas kernels for 14%

profile of v2, /device:TPU:0, one launch (start us, length us, event | category | flops | bytes accessed | tf_op | source)
XLA Modules:
  0.0 139.1 jit_solution(17240287052544625007)
XLA Ops:
  0.0 4.8 %multiply.1 = (bf16[272,256]{1,0:T(8,128)(2,1)}, bf16[272,256]{1,0:T(8,128)(2,1)}, bf16[272,256]{1,0:T(8,128)(2,1)}, bf16[272,256]{1,0:T(8,128)(2,1)}, bf16[272,...) custom-call(bf16[1,3,128,4096]{3,2,1,0:T(8,128)(2,1)} %proj_ref.1, ...), custom_call_target="tpu_custom_call" | custom-call | flops 1048576 | bytes 9437184 | tf_op jit(solution)/shard_map/multiply/pallas_call | solution.py:97
  4.8 3.0 %collective-permute-start.14 = (bf16[3,128,4096]{2,1,0:T(8,128)(2,1)}, bf16[3,128,4096]{2,1,0:T(8,128)(2,1)S(1)}, u32[]{:S(2)}, u32[]{:S(2)}) collective-permute-start(bf16[3,128,4096]{2,1,0:T(8,128)(2,1)} %get-tuple-element.109), channel_id=1, source_target_pairs={{0,16},{16,0},{1,17},{17,1},{2,18},{18,2},{3,19},{19,3},{4,20},{20... | collective-permute-start | bytes 9437192 | tf_op jit(solution)/shard_map/ppermute | solution.py:415
  7.8 2.6 %collective-permute-start = (bf16[272,256]{1,0:T(8,128)(2,1)}, bf16[272,256]{1,0:T(8,128)(2,1)S(1)}, u32[]{:S(2)}, u32[]{:S(2)}) collective-permute-start(bf16[272,256]{1,0:T(8,128)(2,1)} %get-tuple-element.69), channel_id=1, source_target_pairs={{0,8},{2,10},{4,12},{6,14},{8,0},{10,2},{12,4},{14,6},{1,9},{3,11}... | collective-permute-start | bytes 417800 | tf_op jit(solution)/shard_map/ppermute | solution.py:369
  10.4 1.5 %collective-permute-start.1 = (bf16[272,256]{1,0:T(8,128)(2,1)}, bf16[272,256]{1,0:T(8,128)(2,1)S(1)}, u32[]{:S(2)}, u32[]{:S(2)}) collective-permute-start(bf16[272,256]{1,0:T(8,128)(2,1)} %get-tuple-element.70), channel_id=1, source_target_pairs={{0,2},{2,0},{4,6},{6,4},{8,10},{10,8},{12,14},{14,12},{1,3},{3,1},... | collective-permute-start | bytes 417800 | tf_op jit(solution)/shard_map/ppermute | solution.py:369
  12.2 1.6 %collective-permute-start.3 = (bf16[272,256]{1,0:T(8,128)(2,1)}, bf16[272,256]{1,0:T(8,128)(2,1)}, u32[]{:S(2)}, u32[]{:S(2)}) collective-permute-start(bf16[272,256]{1,0:T(8,128)(2,1)} %get-tuple-element.72), channel_id=1, source_target_pairs={{0,4},{2,6},{4,0},{6,2},{8,12},{10,14},{12,8},{14,10},{1,5},{3,7},... | collective-permute-start | bytes 417800 | tf_op jit(solution)/shard_map/ppermute | solution.py:369
  13.8 0.7 convert_bitcast_fusion
  14.7 6.5 %collective-permute-done.refs_1_ = bf16[272,256]{1,0:T(8,128)(2,1)S(1)} collective-permute-done((bf16[272,256]{1,0:T(8,128)(2,1)}, bf16[272,256]{1,0:T(8,128)(2,1)S(1)}, u32[]{:S(2)}, u32[]{:S(2)}) %collective-permute-start) | collective-permute-done | bytes 139296 | tf_op jit(solution)/shard_map/ppermute | solution.py:369
  21.2 2.5 %collective-permute-start.4 = (bf16[272,256]{1,0:T(8,128)(2,1)}, bf16[272,256]{1,0:T(8,128)(2,1)S(1)}, u32[]{:S(2)}, u32[]{:S(2)}) collective-permute-start(bf16[272,256]{1,0:T(8,128)(2,1)} %get-tuple-element.73), channel_id=1, source_target_pairs={{0,12},{2,14},{4,8},{6,10},{8,4},{10,6},{12,0},{14,2},{1,13},{3,15... | collective-permute-start | bytes 417800 | tf_op jit(solution)/shard_map/ppermute | solution.py:369
  24.1 3.6 %collective-permute-start.6 = (bf16[272,256]{1,0:T(8,128)(2,1)}, bf16[272,256]{1,0:T(8,128)(2,1)S(1)}, u32[]{:S(2)}, u32[]{:S(2)}) collective-permute-start(bf16[272,256]{1,0:T(8,128)(2,1)} %get-tuple-element.75), channel_id=1, source_target_pairs={{0,14},{2,12},{4,10},{6,8},{8,6},{10,4},{12,2},{14,0},{1,15},{3,13... | collective-permute-start | bytes 417800 | tf_op jit(solution)/shard_map/ppermute | solution.py:369
  27.7 0.5 collective-permute-start.7
  28.3 1.2 collective-permute-done.4.refs_5_
  29.4 2.0 %collective-permute-start.8 = (bf16[256,256]{1,0:T(8,128)(2,1)}, bf16[256,256]{1,0:T(8,128)(2,1)S(1)}, u32[]{:S(2)}, u32[]{:S(2)}) collective-permute-start(bf16[256,256]{1,0:T(8,128)(2,1)} %get-tuple-element.78), channel_id=1, source_target_pairs={{0,2},{2,0},{4,6},{6,4},{8,10},{10,8},{12,14},{14,12},{1,3},{3,1},... | collective-permute-start | bytes 393224 | tf_op jit(solution)/shard_map/ppermute | solution.py:369
  31.4 1.8 %collective-permute-done.5.refs_6_ = bf16[272,256]{1,0:T(8,128)(2,1)S(1)} collective-permute-done((bf16[272,256]{1,0:T(8,128)(2,1)}, bf16[272,256]{1,0:T(8,128)(2,1)S(1)}, u32[]{:S(2)}, u32[]{:S(2)}) %collective-permute-start.5) | collective-permute-done | bytes 139296 | tf_op jit(solution)/shard_map/ppermute | solution.py:369
  33.3 0.8 collective-permute-start.9
  34.0 2.1 %collective-permute-done.6.refs_7_ = bf16[272,256]{1,0:T(8,128)(2,1)S(1)} collective-permute-done((bf16[272,256]{1,0:T(8,128)(2,1)}, bf16[272,256]{1,0:T(8,128)(2,1)S(1)}, u32[]{:S(2)}, u32[]{:S(2)}) %collective-permute-start.6) | collective-permute-done | bytes 139296 | tf_op jit(solution)/shard_map/ppermute | solution.py:369
  36.2 6.2 %collective-permute-start.10 = (bf16[256,256]{1,0:T(8,128)(2,1)}, bf16[256,256]{1,0:T(8,128)(2,1)S(1)}, u32[]{:S(2)}, u32[]{:S(2)}) collective-permute-start(bf16[256,256]{1,0:T(8,128)(2,1)} %get-tuple-element.80), channel_id=1, source_target_pairs={{0,4},{2,6},{4,0},{6,2},{8,12},{10,14},{12,8},{14,10},{1,5},{3,7},... | collective-permute-start | bytes 393224 | tf_op jit(solution)/shard_map/ppermute | solution.py:369
  42.4 0.9 copy-done.1
  43.3 1.4 %masks.1.mask_ref = bf16[8,2,128,256]{3,2,1,0:T(8,128)(2,1)S(1)} custom-call(s32[66]{0:T(128)S(1)} %pad_add_fusion.meta_ref, bf16[272,256]{1,0:T(8,128)(2,1)S(1)} %copy-done.1, bf16[272,256]{1,0:T(8,128)(2,1)S(1)} %collective-permute-done.refs_1_, bf16[272,256]{1,0:T(8,128)(2,1)S(1)} %collective-permute-done.1.refs_2_, ...), custom_call_target="tpu_custom_call" | custom-call | flops 1048576 | bytes 1048576 | tf_op jit(solution)/shard_map/masks/pallas_call | solution.py:170
  44.8 7.6 %convolve.2 = (bf16[256,256]{1,0:T(8,128)(2,1)S(1)}, bf16[256,256]{1,0:T(8,128)(2,1)S(1)}, bf16[256,256]{1,0:T(8,128)(2,1)S(1)}, bf16[256,256]{1,0:T(8,128)(2,1)...) custom-call(s32[66]{0:T(128)S(1)} %pad_add_fusion.meta_ref, ...), custom_call_target="tpu_custom_call" | custom-call | flops 2147483648 | bytes 2621440 | tf_op jit(solution)/shard_map/convolve/pallas_call | solution.py:255
  52.4 3.4 %collective-permute-start.11 = (bf16[256,256]{1,0:T(8,128)(2,1)S(1)}, bf16[256,256]{1,0:T(8,128)(2,1)S(1)}, u32[]{:S(2)}, u32[]{:S(2)}) collective-permute-start(bf16[256,256]{1,0:T(8,128)(2,1)S(1)} %copy-done.5), channel_id=1, source_target_pairs={{0,12},{2,14},{4,8},{6,10},{8,4},{10,6},{12,0},{14,2},{1,13},{3,15... | collective-permute-start | bytes 393224 | tf_op jit(solution)/shard_map/ppermute | solution.py:369
  55.9 1.0 collective-permute-start.13
  56.8 0.5 collective-permute-start.23
  57.4 3.3 %collective-permute-done.11.refs_5_ = bf16[256,256]{1,0:T(8,128)(2,1)S(1)} collective-permute-done((bf16[256,256]{1,0:T(8,128)(2,1)S(1)}, bf16[256,256]{1,0:T(8,128)(2,1)S(1)}, u32[]{:S(2)}, u32[]{:S(2)}) %collective-permute-start.11) | collective-permute-done | bytes 131104 | tf_op jit(solution)/shard_map/ppermute | solution.py:369
  60.7 2.3 %collective-permute-start.24 = (bf16[256,256]{1,0:T(8,128)(2,1)S(1)}, bf16[256,256]{1,0:T(8,128)(2,1)S(1)}, u32[]{:S(2)}, u32[]{:S(2)}) collective-permute-start(bf16[256,256]{1,0:T(8,128)(2,1)S(1)} %get-tuple-element.120), channel_id=1, source_target_pairs={{0,24},{2,26},{4,28},{6,30},{8,16},{10,18},{12,20},{14,22},{16,8},... | collective-permute-start | bytes 393224 | tf_op jit(solution)/shard_map/ppermute | solution.py:380
  63.0 1.3 collective-permute-done.12.refs_6_
  64.3 1.2 collective-permute-start.25
  65.5 1.0 collective-permute-done.13.refs_7_
  66.5 5.9 %collective-permute-start.26 = (bf16[256,256]{1,0:T(8,128)(2,1)S(1)}, bf16[256,256]{1,0:T(8,128)(2,1)S(1)}, u32[]{:S(2)}, u32[]{:S(2)}) collective-permute-start(bf16[256,256]{1,0:T(8,128)(2,1)S(1)} %get-tuple-element.122), channel_id=1, source_target_pairs={{0,26},{2,24},{4,30},{6,28},{8,18},{10,16},{12,22},{14,20},{16,10}... | collective-permute-start | bytes 393224 | tf_op jit(solution)/shard_map/ppermute | solution.py:380
  72.4 7.1 %convolve.3 = (bf16[256,256]{1,0:T(8,128)(2,1)S(1)}, bf16[256,256]{1,0:T(8,128)(2,1)S(1)}, bf16[256,256]{1,0:T(8,128)(2,1)S(1)}, bf16[256,256]{1,0:T(8,128)(2,1)...) custom-call(s32[66]{0:T(128)S(1)} %pad_add_fusion.meta_ref, ...), custom_call_target="tpu_custom_call" | custom-call | flops 2147483648 | bytes 2621440 | tf_op jit(solution)/shard_map/convolve/pallas_call | solution.py:255
  79.5 5.9 %collective-permute-done.23.refs_0_ = bf16[256,256]{1,0:T(8,128)(2,1)S(1)} collective-permute-done((bf16[256,256]{1,0:T(8,128)(2,1)S(1)}, bf16[256,256]{1,0:T(8,128)(2,1)S(1)}, u32[]{:S(2)}, u32[]{:S(2)}) %collective-permute-start.23) | collective-permute-done | bytes 131104 | tf_op jit(solution)/shard_map/ppermute | solution.py:380
  85.4 3.1 %collective-permute-start.27 = (bf16[256,256]{1,0:T(8,128)(2,1)S(1)}, bf16[256,256]{1,0:T(8,128)(2,1)S(1)}, u32[]{:S(2)}, u32[]{:S(2)}) collective-permute-start(bf16[256,256]{1,0:T(8,128)(2,1)S(1)} %get-tuple-element.123), channel_id=1, source_target_pairs={{0,20},{2,22},{4,16},{6,18},{8,28},{10,30},{12,24},{14,26},{16,4},... | collective-permute-start | bytes 393224 | tf_op jit(solution)/shard_map/ppermute | solution.py:380
  88.5 0.5 collective-permute-start.15
  89.0 1.2 collective-permute-done.25.refs_2_
  90.2 3.5 %collective-permute-start.16 = (bf16[256,256]{1,0:T(8,128)(2,1)S(1)}, bf16[256,256]{1,0:T(8,128)(2,1)S(1)}, u32[]{:S(2)}, u32[]{:S(2)}) collective-permute-start(bf16[256,256]{1,0:T(8,128)(2,1)S(1)} %get-tuple-element.112), channel_id=1, source_target_pairs={{0,24},{2,26},{4,28},{6,30},{8,16},{10,18},{12,20},{14,22},{16,8},... | collective-permute-start | bytes 393224 | tf_op jit(solution)/shard_map/ppermute | solution.py:380
  94.2 3.3 %collective-permute-start.18 = (bf16[256,256]{1,0:T(8,128)(2,1)S(1)}, bf16[256,256]{1,0:T(8,128)(2,1)S(1)}, u32[]{:S(2)}, u32[]{:S(2)}) collective-permute-start(bf16[256,256]{1,0:T(8,128)(2,1)S(1)} %get-tuple-element.114), channel_id=1, source_target_pairs={{0,26},{2,24},{4,30},{6,28},{8,18},{10,16},{12,22},{14,20},{16,10}... | collective-permute-start | bytes 393224 | tf_op jit(solution)/shard_map/ppermute | solution.py:380
  97.5 1.7 %collective-permute-done.15.refs_8_.refs_0_ = bf16[256,256]{1,0:T(8,128)(2,1)S(1)} collective-permute-done((bf16[256,256]{1,0:T(8,128)(2,1)S(1)}, bf16[256,256]{1,0:T(8,128)(2,1)S(1)}, u32[]{:S(2)}, u32[]{:S(2)}) %collective-permute-start.15) | collective-permute-done | bytes 131104 | tf_op jit(solution)/shard_map/ppermute | solution.py:380
  99.2 7.0 %collective-permute-start.28 = (bf16[256,256]{1,0:T(8,128)(2,1)S(1)}, bf16[256,256]{1,0:T(8,128)(2,1)S(1)}, u32[]{:S(2)}, u32[]{:S(2)}) collective-permute-start(bf16[256,256]{1,0:T(8,128)(2,1)S(1)} %get-tuple-element.124), channel_id=1, source_target_pairs={{0,28},{2,30},{4,24},{6,26},{8,20},{10,22},{12,16},{14,18},{16,12}... | collective-permute-start | bytes 393224 | tf_op jit(solution)/shard_map/ppermute | solution.py:380
  106.2 3.0 %collective-permute-start.29 = (bf16[256,256]{1,0:T(8,128)(2,1)S(1)}, bf16[256,256]{1,0:T(8,128)(2,1)S(1)}, u32[]{:S(2)}, u32[]{:S(2)}) collective-permute-start(bf16[256,256]{1,0:T(8,128)(2,1)S(1)} %get-tuple-element.125), channel_id=1, source_target_pairs={{0,22},{2,20},{4,18},{6,16},{8,30},{10,28},{12,26},{14,24},{16,6},... | collective-permute-start | bytes 393224 | tf_op jit(solution)/shard_map/ppermute | solution.py:380
  109.2 1.0 collective-permute-start.30
  110.2 9.6 %collective-permute-start.20 = (bf16[256,256]{1,0:T(8,128)(2,1)S(1)}, bf16[256,256]{1,0:T(8,128)(2,1)S(1)}, u32[]{:S(2)}, u32[]{:S(2)}) collective-permute-start(bf16[256,256]{1,0:T(8,128)(2,1)S(1)} %get-tuple-element.116), channel_id=1, source_target_pairs={{0,28},{2,30},{4,24},{6,26},{8,20},{10,22},{12,16},{14,18},{16,12}... | collective-permute-start | bytes 393224 | tf_op jit(solution)/shard_map/ppermute | solution.py:380
  119.8 5.7 %collective-permute-start.22 = (bf16[256,256]{1,0:T(8,128)(2,1)S(1)}, bf16[256,256]{1,0:T(8,128)(2,1)S(1)}, u32[]{:S(2)}, u32[]{:S(2)}) collective-permute-start(bf16[256,256]{1,0:T(8,128)(2,1)S(1)} %get-tuple-element.118), channel_id=1, source_target_pairs={{0,30},{2,28},{4,26},{6,24},{8,22},{10,20},{12,18},{14,16},{16,14}... | collective-permute-start | bytes 393224 | tf_op jit(solution)/shard_map/ppermute | solution.py:380
  125.5 1.1 collective-permute-done.21.refs_14_.refs_6_
  126.6 4.6 %collective-permute-done.22.refs_15_.refs_7_ = bf16[256,256]{1,0:T(8,128)(2,1)S(1)} collective-permute-done((bf16[256,256]{1,0:T(8,128)(2,1)S(1)}, bf16[256,256]{1,0:T(8,128)(2,1)S(1)}, u32[]{:S(2)}, u32[]{:S(2)}) %collective-permute-start.22) | collective-permute-done | bytes 131104 | tf_op jit(solution)/shard_map/ppermute | solution.py:380
  131.2 2.0 %gradients.2 = (bf16[1,3,64,8192]{3,2,1,0:T(8,128)(2,1)}, bf16[3,64,2048]{2,1,0:T(8,128)(2,1)S(1)}) custom-call(s32[66]{0:T(128)S(1)} %pad_add_fusion.meta_ref, bf16[3,128,4096]{2,1,0:T(8,128)(2,1)S(1)} %collective-permute-done.14.side_ref, bf16[256,256]{1,0:T(8,128)(2,1)S(1)} %collective-permute-done.23.refs_0_, ...), custom_call_target="tpu_custom_call" | custom-call | flops 786432 | bytes 4194304 | tf_op jit(solution)/shard_map/gradients/pallas_call | solution.py:326
  133.2 2.0 %gradients.3 = (bf16[1,3,64,8192]{3,2,1,0:T(8,128)(2,1)}, bf16[3,64,2048]{2,1,0:T(8,128)(2,1)S(1)}) custom-call(s32[66]{0:T(128)S(1)} %pad_add_fusion.meta_ref, bf16[3,128,4096]{2,1,0:T(8,128)(2,1)S(1)} %collective-permute-done.14.side_ref, bf16[256,256]{1,0:T(8,128)(2,1)S(1)} %collective-permute-done.15.refs_8_.refs_0_, ...), custom_call_target="tpu_custom_call", output_to_operand_aliasing={{0}: (10, {})} | custom-call | flops 786432 | bytes 4194304 | tf_op jit(solution)/shard_map/gradients/pallas_call | solution.py:326
  135.2 0.5 collective-permute-start.31
  135.7 1.5 %place.2.held_ref = bf16[1,3,64,8192]{3,2,1,0:T(8,128)(2,1)} custom-call(s32[66]{0:T(128)S(1)} %pad_add_fusion.meta_ref, bf16[3,64,2048]{2,1,0:T(8,128)(2,1)S(1)} %collective-permute-done.32.cross_ref, bf16[1,3,64,8192]{3,2,1,0:T(8,128)(2,1)} %get-tuple-element.130.held_ref), custom_call_target="tpu_custom_call", output_to_operand_aliasing={{}: (2, {})} | custom-call | bytes 1572864 | tf_op jit(solution)/shard_map/place/pallas_call | solution.py:349
  137.7 1.5 %place.3 = bf16[1,3,64,8192]{3,2,1,0:T(8,128)(2,1)} custom-call(s32[66]{0:T(128)S(1)} %pad_add_fusion.meta_ref, bf16[3,64,2048]{2,1,0:T(8,128)(2,1)S(1)} %collective-permute-done.31.cross_ref, bf16[1,3,64,8192]{3,2,1,0:T(8,128)(2,1)} %place.2.held_ref), custom_call_target="tpu_custom_call", output_to_operand_aliasing={{}: (2, {})} | custom-call | bytes 1572864 | tf_op jit(solution)/shard_map/place/pallas_call | solution.py:349
  (44 shorter events, 1.9 us)
Async XLA Ops:
  0.0 14.5 %copy-start = (s32[2,64]{1,0:T(2,128)S(1)}, s32[2,64]{1,0:T(2,128)}, u32[]{:S(2)}) copy-start(s32[2,64]{1,0:T(2,128)} %param.7) | copy-start | bytes 1540
  4.8 94.3 %collective-permute-start.14 = (bf16[3,128,4096]{2,1,0:T(8,128)(2,1)}, bf16[3,128,4096]{2,1,0:T(8,128)(2,1)S(1)}, u32[]{:S(2)}, u32[]{:S(2)}) collective-permute-start(bf16[3,128,4096]{2,1,0:T(8,128)(2,1)} %get-tuple-element.109), channel_id=1, source_target_pairs={{0,16},{16,0},{1,17},{17,1},{2,18},{18,2},{3,19},{19,3},{4,20},{20... | collective-permute-start | bytes 9437192 | tf_op jit(solution)/shard_map/ppermute | solution.py:415
  7.8 13.4 %collective-permute-start = (bf16[272,256]{1,0:T(8,128)(2,1)}, bf16[272,256]{1,0:T(8,128)(2,1)S(1)}, u32[]{:S(2)}, u32[]{:S(2)}) collective-permute-start(bf16[272,256]{1,0:T(8,128)(2,1)} %get-tuple-element.69), channel_id=1, source_target_pairs={{0,8},{2,10},{4,12},{6,14},{8,0},{10,2},{12,4},{14,6},{1,9},{3,11}... | collective-permute-start | bytes 417800 | tf_op jit(solution)/shard_map/ppermute | solution.py:369
  10.4 13.3 %collective-permute-start.1 = (bf16[272,256]{1,0:T(8,128)(2,1)}, bf16[272,256]{1,0:T(8,128)(2,1)S(1)}, u32[]{:S(2)}, u32[]{:S(2)}) collective-permute-start(bf16[272,256]{1,0:T(8,128)(2,1)} %get-tuple-element.70), channel_id=1, source_target_pairs={{0,2},{2,0},{4,6},{6,4},{8,10},{10,8},{12,14},{14,12},{1,3},{3,1},... | collective-permute-start | bytes 417800 | tf_op jit(solution)/shard_map/ppermute | solution.py:369
  11.9 12.1 %collective-permute-start.2 = (bf16[272,256]{1,0:T(8,128)(2,1)}, bf16[272,256]{1,0:T(8,128)(2,1)}, u32[]{:S(2)}, u32[]{:S(2)}) collective-permute-start(bf16[272,256]{1,0:T(8,128)(2,1)} %get-tuple-element.71), channel_id=1, source_target_pairs={{0,10},{2,8},{4,14},{6,12},{8,2},{10,0},{12,6},{14,4},{1,11},{3,9}... | collective-permute-start | bytes 417800 | tf_op jit(solution)/shard_map/ppermute | solution.py:369
  12.2 15.5 %collective-permute-start.3 = (bf16[272,256]{1,0:T(8,128)(2,1)}, bf16[272,256]{1,0:T(8,128)(2,1)}, u32[]{:S(2)}, u32[]{:S(2)}) collective-permute-start(bf16[272,256]{1,0:T(8,128)(2,1)} %get-tuple-element.72), channel_id=1, source_target_pairs={{0,4},{2,6},{4,0},{6,2},{8,12},{10,14},{12,8},{14,10},{1,5},{3,7},... | collective-permute-start | bytes 417800 | tf_op jit(solution)/shard_map/ppermute | solution.py:369
  21.2 8.2 %collective-permute-start.4 = (bf16[272,256]{1,0:T(8,128)(2,1)}, bf16[272,256]{1,0:T(8,128)(2,1)S(1)}, u32[]{:S(2)}, u32[]{:S(2)}) collective-permute-start(bf16[272,256]{1,0:T(8,128)(2,1)} %get-tuple-element.73), channel_id=1, source_target_pairs={{0,12},{2,14},{4,8},{6,10},{8,4},{10,6},{12,0},{14,2},{1,13},{3,15... | collective-permute-start | bytes 417800 | tf_op jit(solution)/shard_map/ppermute | solution.py:369
  23.7 9.6 %collective-permute-start.5 = (bf16[272,256]{1,0:T(8,128)(2,1)}, bf16[272,256]{1,0:T(8,128)(2,1)S(1)}, u32[]{:S(2)}, u32[]{:S(2)}) collective-permute-start(bf16[272,256]{1,0:T(8,128)(2,1)} %get-tuple-element.74), channel_id=1, source_target_pairs={{0,6},{2,4},{4,2},{6,0},{8,14},{10,12},{12,10},{14,8},{1,7},{3,5},... | collective-permute-start | bytes 417800 | tf_op jit(solution)/shard_map/ppermute | solution.py:369
  24.1 12.1 %collective-permute-start.6 = (bf16[272,256]{1,0:T(8,128)(2,1)}, bf16[272,256]{1,0:T(8,128)(2,1)S(1)}, u32[]{:S(2)}, u32[]{:S(2)}) collective-permute-start(bf16[272,256]{1,0:T(8,128)(2,1)} %get-tuple-element.75), channel_id=1, source_target_pairs={{0,14},{2,12},{4,10},{6,8},{8,6},{10,4},{12,2},{14,0},{1,15},{3,13... | collective-permute-start | bytes 417800 | tf_op jit(solution)/shard_map/ppermute | solution.py:369
  27.7 24.6 %collective-permute-start.7 = (bf16[256,256]{1,0:T(8,128)(2,1)}, bf16[256,256]{1,0:T(8,128)(2,1)S(1)}, u32[]{:S(2)}, u32[]{:S(2)}) collective-permute-start(bf16[256,256]{1,0:T(8,128)(2,1)} %get-tuple-element.77), channel_id=1, source_target_pairs={{0,8},{2,10},{4,12},{6,14},{8,0},{10,2},{12,4},{14,6},{1,9},{3,11}... | collective-permute-start | bytes 393224 | tf_op jit(solution)/shard_map/ppermute | solution.py:369
  29.4 26.4 %collective-permute-start.8 = (bf16[256,256]{1,0:T(8,128)(2,1)}, bf16[256,256]{1,0:T(8,128)(2,1)S(1)}, u32[]{:S(2)}, u32[]{:S(2)}) collective-permute-start(bf16[256,256]{1,0:T(8,128)(2,1)} %get-tuple-element.78), channel_id=1, source_target_pairs={{0,2},{2,0},{4,6},{6,4},{8,10},{10,8},{12,14},{14,12},{1,3},{3,1},... | collective-permute-start | bytes 393224 | tf_op jit(solution)/shard_map/ppermute | solution.py:369
  33.3 22.5 %collective-permute-start.9 = (bf16[256,256]{1,0:T(8,128)(2,1)}, bf16[256,256]{1,0:T(8,128)(2,1)S(1)}, u32[]{:S(2)}, u32[]{:S(2)}) collective-permute-start(bf16[256,256]{1,0:T(8,128)(2,1)} %get-tuple-element.79), channel_id=1, source_target_pairs={{0,10},{2,8},{4,14},{6,12},{8,2},{10,0},{12,6},{14,4},{1,11},{3,9}... | collective-permute-start | bytes 393224 | tf_op jit(solution)/shard_map/ppermute | solution.py:369
  36.2 20.7 %collective-permute-start.10 = (bf16[256,256]{1,0:T(8,128)(2,1)}, bf16[256,256]{1,0:T(8,128)(2,1)S(1)}, u32[]{:S(2)}, u32[]{:S(2)}) collective-permute-start(bf16[256,256]{1,0:T(8,128)(2,1)} %get-tuple-element.80), channel_id=1, source_target_pairs={{0,4},{2,6},{4,0},{6,2},{8,12},{10,14},{12,8},{14,10},{1,5},{3,7},... | collective-permute-start | bytes 393224 | tf_op jit(solution)/shard_map/ppermute | solution.py:369
  42.4 0.9 copy-start.1
  44.7 7.7 %copy-start.5 = (bf16[256,256]{1,0:T(8,128)(2,1)S(1)}, bf16[256,256]{1,0:T(8,128)(2,1)}, u32[]{:S(2)}) copy-start(bf16[256,256]{1,0:T(8,128)(2,1)} %get-tuple-element.92) | copy-start | bytes 393220
  44.7 11.1 %copy-start.4 = (bf16[256,256]{1,0:T(8,128)(2,1)S(1)}, bf16[256,256]{1,0:T(8,128)(2,1)}, u32[]{:S(2)}) copy-start(bf16[256,256]{1,0:T(8,128)(2,1)} %get-tuple-element.93) | copy-start | bytes 393220
  44.7 11.1 %copy-start.3 = (bf16[256,256]{1,0:T(8,128)(2,1)S(1)}, bf16[256,256]{1,0:T(8,128)(2,1)}, u32[]{:S(2)}) copy-start(bf16[256,256]{1,0:T(8,128)(2,1)} %get-tuple-element.94) | copy-start | bytes 393220
  44.7 27.6 %copy-start.2 = (bf16[256,256]{1,0:T(8,128)(2,1)S(1)}, bf16[256,256]{1,0:T(8,128)(2,1)}, u32[]{:S(2)}) copy-start(bf16[256,256]{1,0:T(8,128)(2,1)} %get-tuple-element.76.refs_0_) | copy-start | bytes 393220
  52.4 8.3 %collective-permute-start.11 = (bf16[256,256]{1,0:T(8,128)(2,1)S(1)}, bf16[256,256]{1,0:T(8,128)(2,1)S(1)}, u32[]{:S(2)}, u32[]{:S(2)}) collective-permute-start(bf16[256,256]{1,0:T(8,128)(2,1)S(1)} %copy-done.5), channel_id=1, source_target_pairs={{0,12},{2,14},{4,8},{6,10},{8,4},{10,6},{12,0},{14,2},{1,13},{3,15... | collective-permute-start | bytes 393224 | tf_op jit(solution)/shard_map/ppermute | solution.py:369
  55.8 8.5 %collective-permute-start.12 = (bf16[256,256]{1,0:T(8,128)(2,1)S(1)}, bf16[256,256]{1,0:T(8,128)(2,1)S(1)}, u32[]{:S(2)}, u32[]{:S(2)}) collective-permute-start(bf16[256,256]{1,0:T(8,128)(2,1)S(1)} %copy-done.4), channel_id=1, source_target_pairs={{0,6},{2,4},{4,2},{6,0},{8,14},{10,12},{12,10},{14,8},{1,7},{3,5},... | collective-permute-start | bytes 393224 | tf_op jit(solution)/shard_map/ppermute | solution.py:369
  55.9 10.6 %collective-permute-start.13 = (bf16[256,256]{1,0:T(8,128)(2,1)S(1)}, bf16[256,256]{1,0:T(8,128)(2,1)S(1)}, u32[]{:S(2)}, u32[]{:S(2)}) collective-permute-start(bf16[256,256]{1,0:T(8,128)(2,1)S(1)} %copy-done.3), channel_id=1, source_target_pairs={{0,14},{2,12},{4,10},{6,8},{8,6},{10,4},{12,2},{14,0},{1,15},{3,13... | collective-permute-start | bytes 393224 | tf_op jit(solution)/shard_map/ppermute | solution.py:369
  56.8 28.6 %collective-permute-start.23 = (bf16[256,256]{1,0:T(8,128)(2,1)S(1)}, bf16[256,256]{1,0:T(8,128)(2,1)S(1)}, u32[]{:S(2)}, u32[]{:S(2)}) collective-permute-start(bf16[256,256]{1,0:T(8,128)(2,1)S(1)} %get-tuple-element.119), channel_id=1, source_target_pairs={{0,16},{2,18},{4,20},{6,22},{8,24},{10,26},{12,28},{14,30},{16,0},... | collective-permute-start | bytes 393224 | tf_op jit(solution)/shard_map/ppermute | solution.py:380
  60.7 27.8 %collective-permute-start.24 = (bf16[256,256]{1,0:T(8,128)(2,1)S(1)}, bf16[256,256]{1,0:T(8,128)(2,1)S(1)}, u32[]{:S(2)}, u32[]{:S(2)}) collective-permute-start(bf16[256,256]{1,0:T(8,128)(2,1)S(1)} %get-tuple-element.120), channel_id=1, source_target_pairs={{0,24},{2,26},{4,28},{6,30},{8,16},{10,18},{12,20},{14,22},{16,8},... | collective-permute-start | bytes 393224 | tf_op jit(solution)/shard_map/ppermute | solution.py:380
  64.3 25.9 %collective-permute-start.25 = (bf16[256,256]{1,0:T(8,128)(2,1)S(1)}, bf16[256,256]{1,0:T(8,128)(2,1)S(1)}, u32[]{:S(2)}, u32[]{:S(2)}) collective-permute-start(bf16[256,256]{1,0:T(8,128)(2,1)S(1)} %get-tuple-element.121), channel_id=1, source_target_pairs={{0,18},{2,16},{4,22},{6,20},{8,26},{10,24},{12,30},{14,28},{16,2},... | collective-permute-start | bytes 393224 | tf_op jit(solution)/shard_map/ppermute | solution.py:380
  66.5 27.2 %collective-permute-start.26 = (bf16[256,256]{1,0:T(8,128)(2,1)S(1)}, bf16[256,256]{1,0:T(8,128)(2,1)S(1)}, u32[]{:S(2)}, u32[]{:S(2)}) collective-permute-start(bf16[256,256]{1,0:T(8,128)(2,1)S(1)} %get-tuple-element.122), channel_id=1, source_target_pairs={{0,26},{2,24},{4,30},{6,28},{8,18},{10,16},{12,22},{14,20},{16,10}... | collective-permute-start | bytes 393224 | tf_op jit(solution)/shard_map/ppermute | solution.py:380
  85.4 8.8 %collective-permute-start.27 = (bf16[256,256]{1,0:T(8,128)(2,1)S(1)}, bf16[256,256]{1,0:T(8,128)(2,1)S(1)}, u32[]{:S(2)}, u32[]{:S(2)}) collective-permute-start(bf16[256,256]{1,0:T(8,128)(2,1)S(1)} %get-tuple-element.123), channel_id=1, source_target_pairs={{0,20},{2,22},{4,16},{6,18},{8,28},{10,30},{12,24},{14,26},{16,4},... | collective-permute-start | bytes 393224 | tf_op jit(solution)/shard_map/ppermute | solution.py:380
  88.5 10.7 %collective-permute-start.15 = (bf16[256,256]{1,0:T(8,128)(2,1)S(1)}, bf16[256,256]{1,0:T(8,128)(2,1)S(1)}, u32[]{:S(2)}, u32[]{:S(2)}) collective-permute-start(bf16[256,256]{1,0:T(8,128)(2,1)S(1)} %get-tuple-element.111), channel_id=1, source_target_pairs={{0,16},{2,18},{4,20},{6,22},{8,24},{10,26},{12,28},{14,30},{16,0},... | collective-permute-start | bytes 393224 | tf_op jit(solution)/shard_map/ppermute | solution.py:380
  90.2 16.0 %collective-permute-start.16 = (bf16[256,256]{1,0:T(8,128)(2,1)S(1)}, bf16[256,256]{1,0:T(8,128)(2,1)S(1)}, u32[]{:S(2)}, u32[]{:S(2)}) collective-permute-start(bf16[256,256]{1,0:T(8,128)(2,1)S(1)} %get-tuple-element.112), channel_id=1, source_target_pairs={{0,24},{2,26},{4,28},{6,30},{8,16},{10,18},{12,20},{14,22},{16,8},... | collective-permute-start | bytes 393224 | tf_op jit(solution)/shard_map/ppermute | solution.py:380
  93.7 15.5 %collective-permute-start.17 = (bf16[256,256]{1,0:T(8,128)(2,1)S(1)}, bf16[256,256]{1,0:T(8,128)(2,1)S(1)}, u32[]{:S(2)}, u32[]{:S(2)}) collective-permute-start(bf16[256,256]{1,0:T(8,128)(2,1)S(1)} %get-tuple-element.113), channel_id=1, source_target_pairs={{0,18},{2,16},{4,22},{6,20},{8,26},{10,24},{12,30},{14,28},{16,2},... | collective-permute-start | bytes 393224 | tf_op jit(solution)/shard_map/ppermute | solution.py:380
  94.2 16.0 %collective-permute-start.18 = (bf16[256,256]{1,0:T(8,128)(2,1)S(1)}, bf16[256,256]{1,0:T(8,128)(2,1)S(1)}, u32[]{:S(2)}, u32[]{:S(2)}) collective-permute-start(bf16[256,256]{1,0:T(8,128)(2,1)S(1)} %get-tuple-element.114), channel_id=1, source_target_pairs={{0,26},{2,24},{4,30},{6,28},{8,18},{10,16},{12,22},{14,20},{16,10}... | collective-permute-start | bytes 393224 | tf_op jit(solution)/shard_map/ppermute | solution.py:380
  99.2 20.6 %collective-permute-start.19 = (bf16[256,256]{1,0:T(8,128)(2,1)S(1)}, bf16[256,256]{1,0:T(8,128)(2,1)S(1)}, u32[]{:S(2)}, u32[]{:S(2)}) collective-permute-start(bf16[256,256]{1,0:T(8,128)(2,1)S(1)} %get-tuple-element.115), channel_id=1, source_target_pairs={{0,20},{2,22},{4,16},{6,18},{8,28},{10,30},{12,24},{14,26},{16,4},... | collective-permute-start | bytes 393224 | tf_op jit(solution)/shard_map/ppermute | solution.py:380
  99.2 20.6 %collective-permute-start.28 = (bf16[256,256]{1,0:T(8,128)(2,1)S(1)}, bf16[256,256]{1,0:T(8,128)(2,1)S(1)}, u32[]{:S(2)}, u32[]{:S(2)}) collective-permute-start(bf16[256,256]{1,0:T(8,128)(2,1)S(1)} %get-tuple-element.124), channel_id=1, source_target_pairs={{0,28},{2,30},{4,24},{6,26},{8,20},{10,22},{12,16},{14,18},{16,12}... | collective-permute-start | bytes 393224 | tf_op jit(solution)/shard_map/ppermute | solution.py:380
  106.2 19.3 %collective-permute-start.29 = (bf16[256,256]{1,0:T(8,128)(2,1)S(1)}, bf16[256,256]{1,0:T(8,128)(2,1)S(1)}, u32[]{:S(2)}, u32[]{:S(2)}) collective-permute-start(bf16[256,256]{1,0:T(8,128)(2,1)S(1)} %get-tuple-element.125), channel_id=1, source_target_pairs={{0,22},{2,20},{4,18},{6,16},{8,30},{10,28},{12,26},{14,24},{16,6},... | collective-permute-start | bytes 393224 | tf_op jit(solution)/shard_map/ppermute | solution.py:380
  109.2 16.3 %collective-permute-start.30 = (bf16[256,256]{1,0:T(8,128)(2,1)S(1)}, bf16[256,256]{1,0:T(8,128)(2,1)S(1)}, u32[]{:S(2)}, u32[]{:S(2)}) collective-permute-start(bf16[256,256]{1,0:T(8,128)(2,1)S(1)} %get-tuple-element.126), channel_id=1, source_target_pairs={{0,30},{2,28},{4,26},{6,24},{8,22},{10,20},{12,18},{14,16},{16,14}... | collective-permute-start | bytes 393224 | tf_op jit(solution)/shard_map/ppermute | solution.py:380
  110.2 15.3 %collective-permute-start.20 = (bf16[256,256]{1,0:T(8,128)(2,1)S(1)}, bf16[256,256]{1,0:T(8,128)(2,1)S(1)}, u32[]{:S(2)}, u32[]{:S(2)}) collective-permute-start(bf16[256,256]{1,0:T(8,128)(2,1)S(1)} %get-tuple-element.116), channel_id=1, source_target_pairs={{0,28},{2,30},{4,24},{6,26},{8,20},{10,22},{12,16},{14,18},{16,12}... | collective-permute-start | bytes 393224 | tf_op jit(solution)/shard_map/ppermute | solution.py:380
  119.8 6.8 %collective-permute-start.21 = (bf16[256,256]{1,0:T(8,128)(2,1)S(1)}, bf16[256,256]{1,0:T(8,128)(2,1)S(1)}, u32[]{:S(2)}, u32[]{:S(2)}) collective-permute-start(bf16[256,256]{1,0:T(8,128)(2,1)S(1)} %get-tuple-element.117), channel_id=1, source_target_pairs={{0,22},{2,20},{4,18},{6,16},{8,30},{10,28},{12,26},{14,24},{16,6},... | collective-permute-start | bytes 393224 | tf_op jit(solution)/shard_map/ppermute | solution.py:380
  119.8 11.4 %collective-permute-start.22 = (bf16[256,256]{1,0:T(8,128)(2,1)S(1)}, bf16[256,256]{1,0:T(8,128)(2,1)S(1)}, u32[]{:S(2)}, u32[]{:S(2)}) collective-permute-start(bf16[256,256]{1,0:T(8,128)(2,1)S(1)} %get-tuple-element.118), channel_id=1, source_target_pairs={{0,30},{2,28},{4,26},{6,24},{8,22},{10,20},{12,18},{14,16},{16,14}... | collective-permute-start | bytes 393224 | tf_op jit(solution)/shard_map/ppermute | solution.py:380
  133.2 2.5 %collective-permute-start.32 = (bf16[3,64,2048]{2,1,0:T(8,128)(2,1)S(1)}, bf16[3,64,2048]{2,1,0:T(8,128)(2,1)S(1)}, u32[]{:S(2)}, u32[]{:S(2)}) collective-permute-start(bf16[3,64,2048]{2,1,0:T(8,128)(2,1)S(1)} %get-tuple-element.129), channel_id=1, source_target_pairs={{0,1},{1,0},{2,3},{3,2},{4,5},{5,4},{6,7},{7,6},{8,9},{9,8},{10,11... | collective-permute-start | bytes 2359304 | tf_op jit(solution)/shard_map/ppermute | solution.py:443
  135.2 2.4 %collective-permute-start.31 = (bf16[3,64,2048]{2,1,0:T(8,128)(2,1)S(1)}, bf16[3,64,2048]{2,1,0:T(8,128)(2,1)S(1)}, u32[]{:S(2)}, u32[]{:S(2)}) collective-permute-start(bf16[3,64,2048]{2,1,0:T(8,128)(2,1)S(1)} %get-tuple-element.128), channel_id=1, source_target_pairs={{0,1},{1,0},{2,3},{3,2},{4,5},{5,4},{6,7},{7,6},{8,9},{9,8},{10,11... | collective-permute-start | bytes 2359304 | tf_op jit(solution)/shard_map/ppermute | solution.py:443

commit v3 on v2

--- a/solution.py
+++ b/solution.py
@@ -9,7 +9,7 @@
 from jax.sharding import PartitionSpec as P
 
 LANES = 128
-CHUNKS = 2
+CHUNKS = 1
 MARK_ROWS = 16
 OUT_FIRST = 5
 BACK_FIRST = 5
@@ -263,7 +263,7 @@
             pltpu.VMEM((2, (peers + 1) * tile, width), BF16),
             pltpu.VMEM((2, groups, tile, 2 * tile), BF16),
         ],
-        compiler_params=params(24),
+        compiler_params=params(40),
         cost_estimate=pl.CostEstimate(
             flops=8 * groups * peers * tile**3,
             bytes_accessed=8 * peers * tile * width + 4 * peers * tile**2,

time: 139 us -> 137 us (0.986)
  the two profiles are of different devices: /device:TPU:0 before, /device:TPU:21 now
where the time goes in v3:
time: 137 us; the launch traced here: 136 us
  waiting for transfers between devices  82.7 us (60%)
  starting transfers between devices  26.7 us (19%)
  Pallas kernels  24.3 us (18%)
    ppermute x8, waiting for transfers between devices, swap_to_previous(): return lax.ppermute(array, ('pipe', 'ctx'), pairs)  48 us
    ppermute x7, waiting for transfers between devices, swap(): lax.ppermute(array, 'ctx', [(i, i ^ k) for i in range(peers)])  31.7 us
    ppermute x7, starting transfers between devices, swap(): lax.ppermute(array, 'ctx', [(i, i ^ k) for i in range(peers)])  18.9 us
    pallas_call x1, Pallas kernels, convolve(): pl.pallas_call(functools.partial(conv_kernel, group_size, me_at, peers),...  13.4 us
    ppermute x8, starting transfers between devices, swap_to_previous(): return lax.ppermute(array, ('pipe', 'ctx'), pairs)  5.99 us
    pallas_call x1, Pallas kernels, multiply(): pl.pallas_call(functools.partial(multiply_kernel, chunks), out_shape=[jax...  5.34 us
    ppermute x1, waiting for transfers between devices, shards(): held.append(lax.ppermute(cross, 'tp', [(0, 1), (1, 0)]))  3.04 us
  transfers between devices with their start and end apart: 17, of which 8 were waited for; matrix products, arithmetic and copies ran while one was open for 1% of the time, Pallas kernels for 11%

profile of v3, /device:TPU:21, one launch (start us, length us, event | category | flops | bytes accessed | tf_op | source)
XLA Modules:
  0.0 135.7 jit_solution(15520681424021540426)
XLA Ops:
  0.0 0.0 copy-start
  0.0 5.3 %multiply.1 = (bf16[272,512]{1,0:T(8,128)(2,1)}, bf16[272,512]{1,0:T(8,128)(2,1)}, bf16[272,512]{1,0:T(8,128)(2,1)}, bf16[272,512]{1,0:T(8,128)(2,1)}, bf16[272,...) custom-call(bf16[1,3,128,4096]{3,2,1,0:T(8,128)(2,1)} %proj_ref.1, ...), custom_call_target="tpu_custom_call" | custom-call | flops 1048576 | bytes 9437184 | tf_op jit(solution)/shard_map/multiply/pallas_call | solution.py:97
  5.3 0.0 copy-start.2
  5.4 1.3 collective-permute-start.7
  6.6 0.1 collective-permute-start
  6.7 0.2 collective-permute-start.1
  6.9 3.3 %collective-permute-start.2 = (bf16[272,512]{1,0:T(8,128)(2,1)}, bf16[272,512]{1,0:T(8,128)(2,1)}, u32[]{:S(2)}, u32[]{:S(2)}) collective-permute-start(bf16[272,512]{1,0:T(8,128)(2,1)} %get-tuple-element.31), channel_id=1, source_target_pairs={{0,10},{2,8},{4,14},{6,12},{8,2},{10,0},{12,6},{14,4},{1,11},{3,9}... | collective-permute-start | bytes 835592 | tf_op jit(solution)/shard_map/ppermute | solution.py:369
  10.2 1.3 collective-permute-start.3
  11.5 0.0 copy-done
  11.5 0.7 convert_bitcast_fusion
  12.2 12.1 %collective-permute-done.refs_1_ = bf16[272,512]{1,0:T(8,128)(2,1)} collective-permute-done((bf16[272,512]{1,0:T(8,128)(2,1)}, bf16[272,512]{1,0:T(8,128)(2,1)}, u32[]{:S(2)}, u32[]{:S(2)}) %collective-permute-start) | collective-permute-done | bytes 278560 | tf_op jit(solution)/shard_map/ppermute | solution.py:369
  24.3 3.4 %collective-permute-start.4 = (bf16[272,512]{1,0:T(8,128)(2,1)}, bf16[272,512]{1,0:T(8,128)(2,1)}, u32[]{:S(2)}, u32[]{:S(2)}) collective-permute-start(bf16[272,512]{1,0:T(8,128)(2,1)} %get-tuple-element.33), channel_id=1, source_target_pairs={{0,12},{2,14},{4,8},{6,10},{8,4},{10,6},{12,0},{14,2},{1,13},{3,15... | collective-permute-start | bytes 835592 | tf_op jit(solution)/shard_map/ppermute | solution.py:369
  27.6 0.0 collective-permute-done.1.refs_2_
  27.6 1.9 %collective-permute-start.5 = (bf16[272,512]{1,0:T(8,128)(2,1)}, bf16[272,512]{1,0:T(8,128)(2,1)}, u32[]{:S(2)}, u32[]{:S(2)}) collective-permute-start(bf16[272,512]{1,0:T(8,128)(2,1)} %get-tuple-element.34), channel_id=1, source_target_pairs={{0,6},{2,4},{4,2},{6,0},{8,14},{10,12},{12,10},{14,8},{1,7},{3,5},... | collective-permute-start | bytes 835592 | tf_op jit(solution)/shard_map/ppermute | solution.py:369
  29.5 0.8 collective-permute-done.2.refs_3_
  30.3 8.8 %collective-permute-start.6 = (bf16[272,512]{1,0:T(8,128)(2,1)}, bf16[272,512]{1,0:T(8,128)(2,1)}, u32[]{:S(2)}, u32[]{:S(2)}) collective-permute-start(bf16[272,512]{1,0:T(8,128)(2,1)} %get-tuple-element.35), channel_id=1, source_target_pairs={{0,14},{2,12},{4,10},{6,8},{8,6},{10,4},{12,2},{14,0},{1,15},{3,13... | collective-permute-start | bytes 835592 | tf_op jit(solution)/shard_map/ppermute | solution.py:369
  39.1 0.1 pad_add_fusion.meta_ref
  39.2 0.1 rev.3
  39.3 0.1 pad_bitcast_fusion
  39.4 0.0 collective-permute-done.3.refs_4_
  39.4 12.9 %collective-permute-done.4.refs_5_ = bf16[272,512]{1,0:T(8,128)(2,1)} collective-permute-done((bf16[272,512]{1,0:T(8,128)(2,1)}, bf16[272,512]{1,0:T(8,128)(2,1)}, u32[]{:S(2)}, u32[]{:S(2)}) %collective-permute-start.4) | collective-permute-done | bytes 278560 | tf_op jit(solution)/shard_map/ppermute | solution.py:369
  52.3 0.0 collective-permute-done.5.refs_6_
  52.3 5.9 %collective-permute-done.6.refs_7_ = bf16[272,512]{1,0:T(8,128)(2,1)} collective-permute-done((bf16[272,512]{1,0:T(8,128)(2,1)}, bf16[272,512]{1,0:T(8,128)(2,1)}, u32[]{:S(2)}, u32[]{:S(2)}) %collective-permute-start.6) | collective-permute-done | bytes 278560 | tf_op jit(solution)/shard_map/ppermute | solution.py:369
  58.2 1.0 copy-done.1
  59.2 1.4 %masks.1.mask_ref = bf16[8,2,128,256]{3,2,1,0:T(8,128)(2,1)S(1)} custom-call(s32[66]{0:T(128)S(1)} %pad_add_fusion.meta_ref, bf16[272,512]{1,0:T(8,128)(2,1)S(1)} %copy-done.1, bf16[272,512]{1,0:T(8,128)(2,1)} %collective-permute-done.refs_1_, bf16[272,512]{1,0:T(8,128)(2,1)} %collective-permute-done.1.refs_2_, ...), custom_call_target="tpu_custom_call" | custom-call | flops 1048576 | bytes 1048576 | tf_op jit(solution)/shard_map/masks/pallas_call | solution.py:170
  60.6 0.0 copy-done.2
  60.6 13.4 %convolve.1 = (bf16[256,512]{1,0:T(8,128)(2,1)S(1)}, bf16[256,512]{1,0:T(8,128)(2,1)S(1)}, bf16[256,512]{1,0:T(8,128)(2,1)S(1)}, bf16[256,512]{1,0:T(8,128)(2,1)...) custom-call(s32[66]{0:T(128)S(1)} %pad_add_fusion.meta_ref, ...), custom_call_target="tpu_custom_call" | custom-call | flops 4294967296 | bytes 4718592 | tf_op jit(solution)/shard_map/convolve/pallas_call | solution.py:255
  74.0 0.3 collective-permute-start.8
  74.4 0.0 collective-permute-start.9
  74.4 2.2 %collective-permute-start.10 = (bf16[256,512]{1,0:T(8,128)(2,1)S(1)}, bf16[256,512]{1,0:T(8,128)(2,1)S(1)}, u32[]{:S(2)}, u32[]{:S(2)}) collective-permute-start(bf16[256,512]{1,0:T(8,128)(2,1)S(1)} %get-tuple-element.43), channel_id=1, source_target_pairs={{0,18},{2,16},{4,22},{6,20},{8,26},{10,24},{12,30},{14,28},{16,2},... | collective-permute-start | bytes 786440 | tf_op jit(solution)/shard_map/ppermute | solution.py:380
  76.5 3.2 %collective-permute-start.11 = (bf16[256,512]{1,0:T(8,128)(2,1)S(1)}, bf16[256,512]{1,0:T(8,128)(2,1)S(1)}, u32[]{:S(2)}, u32[]{:S(2)}) collective-permute-start(bf16[256,512]{1,0:T(8,128)(2,1)S(1)} %get-tuple-element.44), channel_id=1, source_target_pairs={{0,26},{2,24},{4,30},{6,28},{8,18},{10,16},{12,22},{14,20},{16,10}... | collective-permute-start | bytes 786440 | tf_op jit(solution)/shard_map/ppermute | solution.py:380
  79.7 0.0 collective-permute-done.7.side_ref
  79.7 0.0 collective-permute-start.12
  79.7 18.6 %collective-permute-done.8.refs_0_ = bf16[256,512]{1,0:T(8,128)(2,1)S(1)} collective-permute-done((bf16[256,512]{1,0:T(8,128)(2,1)S(1)}, bf16[256,512]{1,0:T(8,128)(2,1)S(1)}, u32[]{:S(2)}, u32[]{:S(2)}) %collective-permute-start.8) | collective-permute-done | bytes 262176 | tf_op jit(solution)/shard_map/ppermute | solution.py:380
  98.3 0.3 collective-permute-start.13
  98.6 0.0 collective-permute-done.9.refs_1_
  98.6 0.0 collective-permute-start.14
  98.6 17.1 %collective-permute-done.10.refs_2_ = bf16[256,512]{1,0:T(8,128)(2,1)S(1)} collective-permute-done((bf16[256,512]{1,0:T(8,128)(2,1)S(1)}, bf16[256,512]{1,0:T(8,128)(2,1)S(1)}, u32[]{:S(2)}, u32[]{:S(2)}) %collective-permute-start.10) | collective-permute-done | bytes 262176 | tf_op jit(solution)/shard_map/ppermute | solution.py:380
  115.8 0.0 collective-permute-start.15
  115.8 0.0 collective-permute-done.11.refs_3_
  115.8 0.0 collective-permute-done.12.refs_4_
  115.8 0.0 collective-permute-done.13.refs_5_
  115.8 0.0 collective-permute-done.14.refs_6_
  115.8 12.3 %collective-permute-done.15.refs_7_ = bf16[256,512]{1,0:T(8,128)(2,1)S(1)} collective-permute-done((bf16[256,512]{1,0:T(8,128)(2,1)S(1)}, bf16[256,512]{1,0:T(8,128)(2,1)S(1)}, u32[]{:S(2)}, u32[]{:S(2)}) %collective-permute-start.15) | collective-permute-done | bytes 262176 | tf_op jit(solution)/shard_map/ppermute | solution.py:380
  128.1 2.3 %gradients.1 = (bf16[1,3,64,8192]{3,2,1,0:T(8,128)(2,1)}, bf16[3,64,4096]{2,1,0:T(8,128)(2,1)S(1)}) custom-call(s32[66]{0:T(128)S(1)} %pad_add_fusion.meta_ref, bf16[3,128,4096]{2,1,0:T(8,128)(2,1)S(1)} %collective-permute-done.7.side_ref, bf16[256,512]{1,0:T(8,128)(2,1)S(1)} %collective-permute-done.8.refs_0_, ...), custom_call_target="tpu_custom_call" | custom-call | flops 1572864 | bytes 8388608 | tf_op jit(solution)/shard_map/gradients/pallas_call | solution.py:326
  130.4 0.5 collective-permute-start.16
  130.9 3.0 %collective-permute-done.16.cross_ref = bf16[3,64,4096]{2,1,0:T(8,128)(2,1)S(1)} collective-permute-done((bf16[3,64,4096]{2,1,0:T(8,128)(2,1)S(1)}, bf16[3,64,4096]{2,1,0:T(8,128)(2,1)S(1)}, u32[]{:S(2)}, u32[]{:S(2)}) %collective-permute-start.16) | collective-permute-done | bytes 1572896 | tf_op jit(solution)/shard_map/ppermute | solution.py:443
  133.9 1.8 %place.1 = bf16[1,3,64,8192]{3,2,1,0:T(8,128)(2,1)} custom-call(s32[66]{0:T(128)S(1)} %pad_add_fusion.meta_ref, bf16[3,64,4096]{2,1,0:T(8,128)(2,1)S(1)} %collective-permute-done.16.cross_ref, bf16[1,3,64,8192]{3,2,1,0:T(8,128)(2,1)} %get-tuple-element.50.held_ref), custom_call_target="tpu_custom_call", output_to_operand_aliasing={{}: (2, {})} | custom-call | bytes 3145728 | tf_op jit(solution)/shard_map/place/pallas_call | solution.py:349
  (3 shorter events, 0.0 us)
Async XLA Ops:
  0.0 11.5 %copy-start = (s32[2,64]{1,0:T(2,128)S(1)}, s32[2,64]{1,0:T(2,128)}, u32[]{:S(2)}) copy-start(s32[2,64]{1,0:T(2,128)} %param.7) | copy-start | bytes 1540
  5.3 55.2 %copy-start.2 = (bf16[272,512]{1,0:T(8,128)(2,1)S(1)}, bf16[272,512]{1,0:T(8,128)(2,1)}, u32[]{:S(2)}) copy-start(bf16[272,512]{1,0:T(8,128)(2,1)} %get-tuple-element.28.refs_0_) | copy-start | bytes 835588
  5.4 74.4 %collective-permute-start.7 = (bf16[3,128,4096]{2,1,0:T(8,128)(2,1)}, bf16[3,128,4096]{2,1,0:T(8,128)(2,1)S(1)}, u32[]{:S(2)}, u32[]{:S(2)}) collective-permute-start(bf16[3,128,4096]{2,1,0:T(8,128)(2,1)} %get-tuple-element.39), channel_id=1, source_target_pairs={{0,16},{16,0},{1,17},{17,1},{2,18},{18,2},{3,19},{19,3},{4,20},{20... | collective-permute-start | bytes 9437192 | tf_op jit(solution)/shard_map/ppermute | solution.py:415
  6.6 17.6 %collective-permute-start = (bf16[272,512]{1,0:T(8,128)(2,1)}, bf16[272,512]{1,0:T(8,128)(2,1)}, u32[]{:S(2)}, u32[]{:S(2)}) collective-permute-start(bf16[272,512]{1,0:T(8,128)(2,1)} %get-tuple-element.29), channel_id=1, source_target_pairs={{0,8},{2,10},{4,12},{6,14},{8,0},{10,2},{12,4},{14,6},{1,9},{3,11}... | collective-permute-start | bytes 835592 | tf_op jit(solution)/shard_map/ppermute | solution.py:369
  6.7 20.9 %collective-permute-start.1 = (bf16[272,512]{1,0:T(8,128)(2,1)}, bf16[272,512]{1,0:T(8,128)(2,1)}, u32[]{:S(2)}, u32[]{:S(2)}) collective-permute-start(bf16[272,512]{1,0:T(8,128)(2,1)} %get-tuple-element.30), channel_id=1, source_target_pairs={{0,2},{2,0},{4,6},{6,4},{8,10},{10,8},{12,14},{14,12},{1,3},{3,1},... | collective-permute-start | bytes 835592 | tf_op jit(solution)/shard_map/ppermute | solution.py:369
  6.9 23.4 %collective-permute-start.2 = (bf16[272,512]{1,0:T(8,128)(2,1)}, bf16[272,512]{1,0:T(8,128)(2,1)}, u32[]{:S(2)}, u32[]{:S(2)}) collective-permute-start(bf16[272,512]{1,0:T(8,128)(2,1)} %get-tuple-element.31), channel_id=1, source_target_pairs={{0,10},{2,8},{4,14},{6,12},{8,2},{10,0},{12,6},{14,4},{1,11},{3,9}... | collective-permute-start | bytes 835592 | tf_op jit(solution)/shard_map/ppermute | solution.py:369
  10.2 29.2 %collective-permute-start.3 = (bf16[272,512]{1,0:T(8,128)(2,1)}, bf16[272,512]{1,0:T(8,128)(2,1)}, u32[]{:S(2)}, u32[]{:S(2)}) collective-permute-start(bf16[272,512]{1,0:T(8,128)(2,1)} %get-tuple-element.32), channel_id=1, source_target_pairs={{0,4},{2,6},{4,0},{6,2},{8,12},{10,14},{12,8},{14,10},{1,5},{3,7},... | collective-permute-start | bytes 835592 | tf_op jit(solution)/shard_map/ppermute | solution.py:369
  24.3 28.0 %collective-permute-start.4 = (bf16[272,512]{1,0:T(8,128)(2,1)}, bf16[272,512]{1,0:T(8,128)(2,1)}, u32[]{:S(2)}, u32[]{:S(2)}) collective-permute-start(bf16[272,512]{1,0:T(8,128)(2,1)} %get-tuple-element.33), channel_id=1, source_target_pairs={{0,12},{2,14},{4,8},{6,10},{8,4},{10,6},{12,0},{14,2},{1,13},{3,15... | collective-permute-start | bytes 835592 | tf_op jit(solution)/shard_map/ppermute | solution.py:369
  27.6 24.7 %collective-permute-start.5 = (bf16[272,512]{1,0:T(8,128)(2,1)}, bf16[272,512]{1,0:T(8,128)(2,1)}, u32[]{:S(2)}, u32[]{:S(2)}) collective-permute-start(bf16[272,512]{1,0:T(8,128)(2,1)} %get-tuple-element.34), channel_id=1, source_target_pairs={{0,6},{2,4},{4,2},{6,0},{8,14},{10,12},{12,10},{14,8},{1,7},{3,5},... | collective-permute-start | bytes 835592 | tf_op jit(solution)/shard_map/ppermute | solution.py:369
  30.3 27.9 %collective-permute-start.6 = (bf16[272,512]{1,0:T(8,128)(2,1)}, bf16[272,512]{1,0:T(8,128)(2,1)}, u32[]{:S(2)}, u32[]{:S(2)}) collective-permute-start(bf16[272,512]{1,0:T(8,128)(2,1)} %get-tuple-element.35), channel_id=1, source_target_pairs={{0,14},{2,12},{4,10},{6,8},{8,6},{10,4},{12,2},{14,0},{1,15},{3,13... | collective-permute-start | bytes 835592 | tf_op jit(solution)/shard_map/ppermute | solution.py:369
  58.2 1.0 copy-start.1
  74.0 24.3 %collective-permute-start.8 = (bf16[256,512]{1,0:T(8,128)(2,1)S(1)}, bf16[256,512]{1,0:T(8,128)(2,1)S(1)}, u32[]{:S(2)}, u32[]{:S(2)}) collective-permute-start(bf16[256,512]{1,0:T(8,128)(2,1)S(1)} %get-tuple-element.41), channel_id=1, source_target_pairs={{0,16},{2,18},{4,20},{6,22},{8,24},{10,26},{12,28},{14,30},{16,0},... | collective-permute-start | bytes 786440 | tf_op jit(solution)/shard_map/ppermute | solution.py:380
  74.4 24.3 %collective-permute-start.9 = (bf16[256,512]{1,0:T(8,128)(2,1)S(1)}, bf16[256,512]{1,0:T(8,128)(2,1)S(1)}, u32[]{:S(2)}, u32[]{:S(2)}) collective-permute-start(bf16[256,512]{1,0:T(8,128)(2,1)S(1)} %get-tuple-element.42), channel_id=1, source_target_pairs={{0,24},{2,26},{4,28},{6,30},{8,16},{10,18},{12,20},{14,22},{16,8},... | collective-permute-start | bytes 786440 | tf_op jit(solution)/shard_map/ppermute | solution.py:380
  74.4 41.4 %collective-permute-start.10 = (bf16[256,512]{1,0:T(8,128)(2,1)S(1)}, bf16[256,512]{1,0:T(8,128)(2,1)S(1)}, u32[]{:S(2)}, u32[]{:S(2)}) collective-permute-start(bf16[256,512]{1,0:T(8,128)(2,1)S(1)} %get-tuple-element.43), channel_id=1, source_target_pairs={{0,18},{2,16},{4,22},{6,20},{8,26},{10,24},{12,30},{14,28},{16,2},... | collective-permute-start | bytes 786440 | tf_op jit(solution)/shard_map/ppermute | solution.py:380
  76.5 39.2 %collective-permute-start.11 = (bf16[256,512]{1,0:T(8,128)(2,1)S(1)}, bf16[256,512]{1,0:T(8,128)(2,1)S(1)}, u32[]{:S(2)}, u32[]{:S(2)}) collective-permute-start(bf16[256,512]{1,0:T(8,128)(2,1)S(1)} %get-tuple-element.44), channel_id=1, source_target_pairs={{0,26},{2,24},{4,30},{6,28},{8,18},{10,16},{12,22},{14,20},{16,10}... | collective-permute-start | bytes 786440 | tf_op jit(solution)/shard_map/ppermute | solution.py:380
  79.7 36.0 %collective-permute-start.12 = (bf16[256,512]{1,0:T(8,128)(2,1)S(1)}, bf16[256,512]{1,0:T(8,128)(2,1)S(1)}, u32[]{:S(2)}, u32[]{:S(2)}) collective-permute-start(bf16[256,512]{1,0:T(8,128)(2,1)S(1)} %get-tuple-element.45), channel_id=1, source_target_pairs={{0,20},{2,22},{4,16},{6,18},{8,28},{10,30},{12,24},{14,26},{16,4},... | collective-permute-start | bytes 786440 | tf_op jit(solution)/shard_map/ppermute | solution.py:380
  98.3 17.4 %collective-permute-start.13 = (bf16[256,512]{1,0:T(8,128)(2,1)S(1)}, bf16[256,512]{1,0:T(8,128)(2,1)S(1)}, u32[]{:S(2)}, u32[]{:S(2)}) collective-permute-start(bf16[256,512]{1,0:T(8,128)(2,1)S(1)} %get-tuple-element.46), channel_id=1, source_target_pairs={{0,28},{2,30},{4,24},{6,26},{8,20},{10,22},{12,16},{14,18},{16,12}... | collective-permute-start | bytes 786440 | tf_op jit(solution)/shard_map/ppermute | solution.py:380
  98.6 17.1 %collective-permute-start.14 = (bf16[256,512]{1,0:T(8,128)(2,1)S(1)}, bf16[256,512]{1,0:T(8,128)(2,1)S(1)}, u32[]{:S(2)}, u32[]{:S(2)}) collective-permute-start(bf16[256,512]{1,0:T(8,128)(2,1)S(1)} %get-tuple-element.47), channel_id=1, source_target_pairs={{0,22},{2,20},{4,18},{6,16},{8,30},{10,28},{12,26},{14,24},{16,6},... | collective-permute-start | bytes 786440 | tf_op jit(solution)/shard_map/ppermute | solution.py:380
  115.8 12.3 %collective-permute-start.15 = (bf16[256,512]{1,0:T(8,128)(2,1)S(1)}, bf16[256,512]{1,0:T(8,128)(2,1)S(1)}, u32[]{:S(2)}, u32[]{:S(2)}) collective-permute-start(bf16[256,512]{1,0:T(8,128)(2,1)S(1)} %get-tuple-element.48), channel_id=1, source_target_pairs={{0,30},{2,28},{4,26},{6,24},{8,22},{10,20},{12,18},{14,16},{16,14}... | collective-permute-start | bytes 786440 | tf_op jit(solution)/shard_map/ppermute | solution.py:380
  130.4 3.5 %collective-permute-start.16 = (bf16[3,64,4096]{2,1,0:T(8,128)(2,1)S(1)}, bf16[3,64,4096]{2,1,0:T(8,128)(2,1)S(1)}, u32[]{:S(2)}, u32[]{:S(2)}) collective-permute-start(bf16[3,64,4096]{2,1,0:T(8,128)(2,1)S(1)} %get-tuple-element.49), channel_id=1, source_target_pairs={{0,1},{1,0},{2,3},{3,2},{4,5},{5,4},{6,7},{7,6},{8,9},{9,8},{10,11... | collective-permute-start | bytes 4718600 | tf_op jit(solution)/shard_map/ppermute | solution.py:443

commit v4 on v3

--- a/solution.py
+++ b/solution.py
@@ -31,7 +31,7 @@
 
 def sending_order(peers):
     half = peers // 2
-    return [k for i in range(half) for k in (i, half + i)]
+    return [0, 1, *range(half, peers), *range(2, half)]
 
 
 def multiply_kernel(chunks, proj_ref, grad_ref, marks_ref, *refs):

time: 137 us -> 139 us (1.015)
  waiting for transfers between devices: 82.7 us -> 84.7 us
    ppermute x7, waiting for transfers between devices: 31.7 us -> 39.1 us  [swap(): lax.ppermute(array, 'ctx', [(i, i ^ k) for i in range(peers)])]
    ppermute x8, waiting for transfers between devices: 48 us -> 42.6 us  [swap_to_previous(): return lax.ppermute(array, ('pipe', 'ctx'), pairs)]
    ppermute x7, starting transfers between devices: 18.9 us -> 15.3 us  [swap(): lax.ppermute(array, 'ctx', [(i, i ^ k) for i in range(peers)])]
    ppermute x1, starting transfers between devices: 0.49 us -> 1.99 us  [shards(): held.append(lax.ppermute(cross, 'tp', [(0, 1), (1, 0)]))]
    ppermute x8, starting transfers between devices: 5.99 us -> 7.38 us  [swap_to_previous(): return lax.ppermute(array, ('pipe', 'ctx'), pairs)]
  transfers between devices with their start and end apart: 17 -> 17, of which waited for: 8 -> 12; matrix products, arithmetic and copies ran while one was open for 1% -> 1% of each run, Pallas kernels for 11% -> 11%
where the time goes in v4:
time: 139 us; the launch traced here: 137 us
  waiting for transfers between devices  84.7 us (61%)
  starting transfers between devices  26 us (19%)
  Pallas kernels  24.3 us (17%)
    ppermute x8, waiting for transfers between devices, swap_to_previous(): return lax.ppermute(array, ('pipe', 'ctx'), pairs)  42.6 us
    ppermute x7, waiting for transfers between devices, swap(): lax.ppermute(array, 'ctx', [(i, i ^ k) for i in range(peers)])  39.1 us
    ppermute x7, starting transfers between devices, swap(): lax.ppermute(array, 'ctx', [(i, i ^ k) for i in range(peers)])  15.3 us
    pallas_call x1, Pallas kernels, convolve(): pl.pallas_call(functools.partial(conv_kernel, group_size, me_at, peers),...  13.4 us
    ppermute x8, starting transfers between devices, swap_to_previous(): return lax.ppermute(array, ('pipe', 'ctx'), pairs)  7.38 us
    pallas_call x1, Pallas kernels, multiply(): pl.pallas_call(functools.partial(multiply_kernel, chunks), out_shape=[jax...  5.34 us
    ppermute x1, waiting for transfers between devices, shards(): held.append(lax.ppermute(cross, 'tp', [(0, 1), (1, 0)]))  3.04 us
  transfers between devices with their start and end apart: 17, of which 12 were waited for; matrix products, arithmetic and copies ran while one was open for 1% of the time, Pallas kernels for 11%

profile of v4, /device:TPU:21, one launch (start us, length us, event | category | flops | bytes accessed | tf_op | source)
XLA Modules:
  0.0 136.9 jit_solution(983659134775647810)
XLA Ops:
  0.0 0.0 copy-start
  0.0 5.3 %multiply.1 = (bf16[272,512]{1,0:T(8,128)(2,1)}, bf16[272,512]{1,0:T(8,128)(2,1)}, bf16[272,512]{1,0:T(8,128)(2,1)}, bf16[272,512]{1,0:T(8,128)(2,1)}, bf16[272,...) custom-call(bf16[1,3,128,4096]{3,2,1,0:T(8,128)(2,1)} %proj_ref.1, ...), custom_call_target="tpu_custom_call" | custom-call | flops 1048576 | bytes 9437184 | tf_op jit(solution)/shard_map/multiply/pallas_call | solution.py:97
  5.3 0.0 copy-start.2
  5.4 1.3 collective-permute-start.7
  6.6 0.2 collective-permute-start
  6.9 0.1 collective-permute-start.1
  6.9 3.3 %collective-permute-start.2 = (bf16[272,512]{1,0:T(8,128)(2,1)}, bf16[272,512]{1,0:T(8,128)(2,1)}, u32[]{:S(2)}, u32[]{:S(2)}) collective-permute-start(bf16[272,512]{1,0:T(8,128)(2,1)} %get-tuple-element.31), channel_id=1, source_target_pairs={{0,10},{2,8},{4,14},{6,12},{8,2},{10,0},{12,6},{14,4},{1,11},{3,9}... | collective-permute-start | bytes 835592 | tf_op jit(solution)/shard_map/ppermute | solution.py:369
  10.2 0.2 collective-permute-start.3
  10.4 0.0 copy-done
  10.4 0.7 convert_bitcast_fusion
  11.1 3.1 %collective-permute-done.refs_1_ = bf16[272,512]{1,0:T(8,128)(2,1)} collective-permute-done((bf16[272,512]{1,0:T(8,128)(2,1)}, bf16[272,512]{1,0:T(8,128)(2,1)}, u32[]{:S(2)}, u32[]{:S(2)}) %collective-permute-start) | collective-permute-done | bytes 278560 | tf_op jit(solution)/shard_map/ppermute | solution.py:369
  14.2 0.1 collective-permute-start.4
  14.3 22.1 %collective-permute-done.1.refs_2_ = bf16[272,512]{1,0:T(8,128)(2,1)} collective-permute-done((bf16[272,512]{1,0:T(8,128)(2,1)}, bf16[272,512]{1,0:T(8,128)(2,1)}, u32[]{:S(2)}, u32[]{:S(2)}) %collective-permute-start.1) | collective-permute-done | bytes 278560 | tf_op jit(solution)/shard_map/ppermute | solution.py:369
  36.4 5.3 %collective-permute-start.5 = (bf16[272,512]{1,0:T(8,128)(2,1)}, bf16[272,512]{1,0:T(8,128)(2,1)}, u32[]{:S(2)}, u32[]{:S(2)}) collective-permute-start(bf16[272,512]{1,0:T(8,128)(2,1)} %get-tuple-element.34), channel_id=1, source_target_pairs={{0,4},{2,6},{4,0},{6,2},{8,12},{10,14},{12,8},{14,10},{1,5},{3,7},... | collective-permute-start | bytes 835592 | tf_op jit(solution)/shard_map/ppermute | solution.py:369
  41.7 0.7 collective-permute-done.2.refs_3_
  42.4 6.2 %collective-permute-start.6 = (bf16[272,512]{1,0:T(8,128)(2,1)}, bf16[272,512]{1,0:T(8,128)(2,1)}, u32[]{:S(2)}, u32[]{:S(2)}) collective-permute-start(bf16[272,512]{1,0:T(8,128)(2,1)} %get-tuple-element.35), channel_id=1, source_target_pairs={{0,6},{2,4},{4,2},{6,0},{8,14},{10,12},{12,10},{14,8},{1,7},{3,5},... | collective-permute-start | bytes 835592 | tf_op jit(solution)/shard_map/ppermute | solution.py:369
  48.6 0.1 pad_add_fusion.meta_ref
  48.7 0.1 rev.3
  48.8 0.1 pad_bitcast_fusion
  48.9 3.6 %collective-permute-done.3.refs_4_ = bf16[272,512]{1,0:T(8,128)(2,1)} collective-permute-done((bf16[272,512]{1,0:T(8,128)(2,1)}, bf16[272,512]{1,0:T(8,128)(2,1)}, u32[]{:S(2)}, u32[]{:S(2)}) %collective-permute-start.3) | collective-permute-done | bytes 278560 | tf_op jit(solution)/shard_map/ppermute | solution.py:369
  52.5 9.5 %collective-permute-done.4.refs_5_ = bf16[272,512]{1,0:T(8,128)(2,1)} collective-permute-done((bf16[272,512]{1,0:T(8,128)(2,1)}, bf16[272,512]{1,0:T(8,128)(2,1)}, u32[]{:S(2)}, u32[]{:S(2)}) %collective-permute-start.4) | collective-permute-done | bytes 278560 | tf_op jit(solution)/shard_map/ppermute | solution.py:369
  62.0 0.0 collective-permute-done.5.refs_6_
  62.0 0.0 collective-permute-done.6.refs_7_
  62.0 1.0 copy-done.1
  62.9 1.4 %masks.1.mask_ref = bf16[8,2,128,256]{3,2,1,0:T(8,128)(2,1)S(1)} custom-call(s32[66]{0:T(128)S(1)} %pad_add_fusion.meta_ref, bf16[272,512]{1,0:T(8,128)(2,1)S(1)} %copy-done.1, bf16[272,512]{1,0:T(8,128)(2,1)} %collective-permute-done.refs_1_, bf16[272,512]{1,0:T(8,128)(2,1)} %collective-permute-done.1.refs_2_, ...), custom_call_target="tpu_custom_call" | custom-call | flops 1048576 | bytes 1048576 | tf_op jit(solution)/shard_map/masks/pallas_call | solution.py:170
  64.4 0.0 copy-done.2
  64.4 13.4 %convolve.1 = (bf16[256,512]{1,0:T(8,128)(2,1)S(1)}, bf16[256,512]{1,0:T(8,128)(2,1)S(1)}, bf16[256,512]{1,0:T(8,128)(2,1)S(1)}, bf16[256,512]{1,0:T(8,128)(2,1)...) custom-call(s32[66]{0:T(128)S(1)} %pad_add_fusion.meta_ref, ...), custom_call_target="tpu_custom_call" | custom-call | flops 4294967296 | bytes 4718592 | tf_op jit(solution)/shard_map/convolve/pallas_call | solution.py:255
  77.8 0.3 collective-permute-start.8
  78.2 2.2 %collective-permute-start.9 = (bf16[256,512]{1,0:T(8,128)(2,1)S(1)}, bf16[256,512]{1,0:T(8,128)(2,1)S(1)}, u32[]{:S(2)}, u32[]{:S(2)}) collective-permute-start(bf16[256,512]{1,0:T(8,128)(2,1)S(1)} %get-tuple-element.42), channel_id=1, source_target_pairs={{0,18},{2,16},{4,22},{6,20},{8,26},{10,24},{12,30},{14,28},{16,2},... | collective-permute-start | bytes 786440 | tf_op jit(solution)/shard_map/ppermute | solution.py:380
  80.3 0.0 collective-permute-start.10
  80.3 3.2 %collective-permute-start.11 = (bf16[256,512]{1,0:T(8,128)(2,1)S(1)}, bf16[256,512]{1,0:T(8,128)(2,1)S(1)}, u32[]{:S(2)}, u32[]{:S(2)}) collective-permute-start(bf16[256,512]{1,0:T(8,128)(2,1)S(1)} %get-tuple-element.44), channel_id=1, source_target_pairs={{0,26},{2,24},{4,30},{6,28},{8,18},{10,16},{12,22},{14,20},{16,10}... | collective-permute-start | bytes 786440 | tf_op jit(solution)/shard_map/ppermute | solution.py:380
  83.5 0.0 collective-permute-done.7.side_ref
  83.5 0.0 collective-permute-start.12
  83.5 11.6 %collective-permute-done.8.refs_0_ = bf16[256,512]{1,0:T(8,128)(2,1)S(1)} collective-permute-done((bf16[256,512]{1,0:T(8,128)(2,1)S(1)}, bf16[256,512]{1,0:T(8,128)(2,1)S(1)}, u32[]{:S(2)}, u32[]{:S(2)}) %collective-permute-start.8) | collective-permute-done | bytes 262176 | tf_op jit(solution)/shard_map/ppermute | solution.py:380
  95.1 0.0 collective-permute-start.13
  95.2 7.9 %collective-permute-done.9.refs_1_ = bf16[256,512]{1,0:T(8,128)(2,1)S(1)} collective-permute-done((bf16[256,512]{1,0:T(8,128)(2,1)S(1)}, bf16[256,512]{1,0:T(8,128)(2,1)S(1)}, u32[]{:S(2)}, u32[]{:S(2)}) %collective-permute-start.9) | collective-permute-done | bytes 262176 | tf_op jit(solution)/shard_map/ppermute | solution.py:380
  103.0 0.0 collective-permute-start.14
  103.0 5.0 %collective-permute-done.10.refs_2_ = bf16[256,512]{1,0:T(8,128)(2,1)S(1)} collective-permute-done((bf16[256,512]{1,0:T(8,128)(2,1)S(1)}, bf16[256,512]{1,0:T(8,128)(2,1)S(1)}, u32[]{:S(2)}, u32[]{:S(2)}) %collective-permute-start.10) | collective-permute-done | bytes 262176 | tf_op jit(solution)/shard_map/ppermute | solution.py:380
  108.0 1.7 %collective-permute-start.15 = (bf16[256,512]{1,0:T(8,128)(2,1)S(1)}, bf16[256,512]{1,0:T(8,128)(2,1)S(1)}, u32[]{:S(2)}, u32[]{:S(2)}) collective-permute-start(bf16[256,512]{1,0:T(8,128)(2,1)S(1)} %get-tuple-element.48), channel_id=1, source_target_pairs={{0,22},{2,20},{4,18},{6,16},{8,30},{10,28},{12,26},{14,24},{16,6},... | collective-permute-start | bytes 786440 | tf_op jit(solution)/shard_map/ppermute | solution.py:380
  109.7 3.9 %collective-permute-done.11.refs_3_ = bf16[256,512]{1,0:T(8,128)(2,1)S(1)} collective-permute-done((bf16[256,512]{1,0:T(8,128)(2,1)S(1)}, bf16[256,512]{1,0:T(8,128)(2,1)S(1)}, u32[]{:S(2)}, u32[]{:S(2)}) %collective-permute-start.11) | collective-permute-done | bytes 262176 | tf_op jit(solution)/shard_map/ppermute | solution.py:380
  113.7 8.5 %collective-permute-done.12.refs_4_ = bf16[256,512]{1,0:T(8,128)(2,1)S(1)} collective-permute-done((bf16[256,512]{1,0:T(8,128)(2,1)S(1)}, bf16[256,512]{1,0:T(8,128)(2,1)S(1)}, u32[]{:S(2)}, u32[]{:S(2)}) %collective-permute-start.12) | collective-permute-done | bytes 262176 | tf_op jit(solution)/shard_map/ppermute | solution.py:380
  122.2 5.6 %collective-permute-done.13.refs_5_ = bf16[256,512]{1,0:T(8,128)(2,1)S(1)} collective-permute-done((bf16[256,512]{1,0:T(8,128)(2,1)S(1)}, bf16[256,512]{1,0:T(8,128)(2,1)S(1)}, u32[]{:S(2)}, u32[]{:S(2)}) %collective-permute-start.13) | collective-permute-done | bytes 262176 | tf_op jit(solution)/shard_map/ppermute | solution.py:380
  127.8 0.0 collective-permute-done.14.refs_6_
  127.8 0.0 collective-permute-done.15.refs_7_
  127.8 2.3 %gradients.1 = (bf16[1,3,64,8192]{3,2,1,0:T(8,128)(2,1)}, bf16[3,64,4096]{2,1,0:T(8,128)(2,1)S(1)}) custom-call(s32[66]{0:T(128)S(1)} %pad_add_fusion.meta_ref, bf16[3,128,4096]{2,1,0:T(8,128)(2,1)S(1)} %collective-permute-done.7.side_ref, bf16[256,512]{1,0:T(8,128)(2,1)S(1)} %collective-permute-done.8.refs_0_, ...), custom_call_target="tpu_custom_call" | custom-call | flops 1572864 | bytes 8388608 | tf_op jit(solution)/shard_map/gradients/pallas_call | solution.py:326
  130.1 2.0 %collective-permute-start.16 = (bf16[3,64,4096]{2,1,0:T(8,128)(2,1)S(1)}, bf16[3,64,4096]{2,1,0:T(8,128)(2,1)S(1)}, u32[]{:S(2)}, u32[]{:S(2)}) collective-permute-start(bf16[3,64,4096]{2,1,0:T(8,128)(2,1)S(1)} %get-tuple-element.49), channel_id=1, source_target_pairs={{0,1},{1,0},{2,3},{3,2},{4,5},{5,4},{6,7},{7,6},{8,9},{9,8},{10,11... | collective-permute-start | bytes 4718600 | tf_op jit(solution)/shard_map/ppermute | solution.py:443
  132.1 3.0 %collective-permute-done.16.cross_ref = bf16[3,64,4096]{2,1,0:T(8,128)(2,1)S(1)} collective-permute-done((bf16[3,64,4096]{2,1,0:T(8,128)(2,1)S(1)}, bf16[3,64,4096]{2,1,0:T(8,128)(2,1)S(1)}, u32[]{:S(2)}, u32[]{:S(2)}) %collective-permute-start.16) | collective-permute-done | bytes 1572896 | tf_op jit(solution)/shard_map/ppermute | solution.py:443
  135.2 1.8 %place.1 = bf16[1,3,64,8192]{3,2,1,0:T(8,128)(2,1)} custom-call(s32[66]{0:T(128)S(1)} %pad_add_fusion.meta_ref, bf16[3,64,4096]{2,1,0:T(8,128)(2,1)S(1)} %collective-permute-done.16.cross_ref, bf16[1,3,64,8192]{3,2,1,0:T(8,128)(2,1)} %get-tuple-element.50.held_ref), custom_call_target="tpu_custom_call", output_to_operand_aliasing={{}: (2, {})} | custom-call | bytes 3145728 | tf_op jit(solution)/shard_map/place/pallas_call | solution.py:349
  (3 shorter events, 0.0 us)
Async XLA Ops:
  0.0 10.4 %copy-start = (s32[2,64]{1,0:T(2,128)S(1)}, s32[2,64]{1,0:T(2,128)}, u32[]{:S(2)}) copy-start(s32[2,64]{1,0:T(2,128)} %param.7) | copy-start | bytes 1540
  5.3 59.0 %copy-start.2 = (bf16[272,512]{1,0:T(8,128)(2,1)S(1)}, bf16[272,512]{1,0:T(8,128)(2,1)}, u32[]{:S(2)}) copy-start(bf16[272,512]{1,0:T(8,128)(2,1)} %get-tuple-element.28.refs_0_) | copy-start | bytes 835588
  5.4 78.2 %collective-permute-start.7 = (bf16[3,128,4096]{2,1,0:T(8,128)(2,1)}, bf16[3,128,4096]{2,1,0:T(8,128)(2,1)S(1)}, u32[]{:S(2)}, u32[]{:S(2)}) collective-permute-start(bf16[3,128,4096]{2,1,0:T(8,128)(2,1)} %get-tuple-element.39), channel_id=1, source_target_pairs={{0,16},{16,0},{1,17},{17,1},{2,18},{18,2},{3,19},{19,3},{4,20},{20... | collective-permute-start | bytes 9437192 | tf_op jit(solution)/shard_map/ppermute | solution.py:415
  6.6 7.5 %collective-permute-start = (bf16[272,512]{1,0:T(8,128)(2,1)}, bf16[272,512]{1,0:T(8,128)(2,1)}, u32[]{:S(2)}, u32[]{:S(2)}) collective-permute-start(bf16[272,512]{1,0:T(8,128)(2,1)} %get-tuple-element.29), channel_id=1, source_target_pairs={{0,2},{2,0},{4,6},{6,4},{8,10},{10,8},{12,14},{14,12},{1,3},{3,1},... | collective-permute-start | bytes 835592 | tf_op jit(solution)/shard_map/ppermute | solution.py:369
  6.9 29.5 %collective-permute-start.1 = (bf16[272,512]{1,0:T(8,128)(2,1)}, bf16[272,512]{1,0:T(8,128)(2,1)}, u32[]{:S(2)}, u32[]{:S(2)}) collective-permute-start(bf16[272,512]{1,0:T(8,128)(2,1)} %get-tuple-element.30), channel_id=1, source_target_pairs={{0,8},{2,10},{4,12},{6,14},{8,0},{10,2},{12,4},{14,6},{1,9},{3,11}... | collective-permute-start | bytes 835592 | tf_op jit(solution)/shard_map/ppermute | solution.py:369
  6.9 35.5 %collective-permute-start.2 = (bf16[272,512]{1,0:T(8,128)(2,1)}, bf16[272,512]{1,0:T(8,128)(2,1)}, u32[]{:S(2)}, u32[]{:S(2)}) collective-permute-start(bf16[272,512]{1,0:T(8,128)(2,1)} %get-tuple-element.31), channel_id=1, source_target_pairs={{0,10},{2,8},{4,14},{6,12},{8,2},{10,0},{12,6},{14,4},{1,11},{3,9}... | collective-permute-start | bytes 835592 | tf_op jit(solution)/shard_map/ppermute | solution.py:369
  10.2 42.3 %collective-permute-start.3 = (bf16[272,512]{1,0:T(8,128)(2,1)}, bf16[272,512]{1,0:T(8,128)(2,1)}, u32[]{:S(2)}, u32[]{:S(2)}) collective-permute-start(bf16[272,512]{1,0:T(8,128)(2,1)} %get-tuple-element.32), channel_id=1, source_target_pairs={{0,12},{2,14},{4,8},{6,10},{8,4},{10,6},{12,0},{14,2},{1,13},{3,15... | collective-permute-start | bytes 835592 | tf_op jit(solution)/shard_map/ppermute | solution.py:369
  14.2 47.8 %collective-permute-start.4 = (bf16[272,512]{1,0:T(8,128)(2,1)}, bf16[272,512]{1,0:T(8,128)(2,1)}, u32[]{:S(2)}, u32[]{:S(2)}) collective-permute-start(bf16[272,512]{1,0:T(8,128)(2,1)} %get-tuple-element.33), channel_id=1, source_target_pairs={{0,14},{2,12},{4,10},{6,8},{8,6},{10,4},{12,2},{14,0},{1,15},{3,13... | collective-permute-start | bytes 835592 | tf_op jit(solution)/shard_map/ppermute | solution.py:369
  36.4 25.6 %collective-permute-start.5 = (bf16[272,512]{1,0:T(8,128)(2,1)}, bf16[272,512]{1,0:T(8,128)(2,1)}, u32[]{:S(2)}, u32[]{:S(2)}) collective-permute-start(bf16[272,512]{1,0:T(8,128)(2,1)} %get-tuple-element.34), channel_id=1, source_target_pairs={{0,4},{2,6},{4,0},{6,2},{8,12},{10,14},{12,8},{14,10},{1,5},{3,7},... | collective-permute-start | bytes 835592 | tf_op jit(solution)/shard_map/ppermute | solution.py:369
  42.4 19.6 %collective-permute-start.6 = (bf16[272,512]{1,0:T(8,128)(2,1)}, bf16[272,512]{1,0:T(8,128)(2,1)}, u32[]{:S(2)}, u32[]{:S(2)}) collective-permute-start(bf16[272,512]{1,0:T(8,128)(2,1)} %get-tuple-element.35), channel_id=1, source_target_pairs={{0,6},{2,4},{4,2},{6,0},{8,14},{10,12},{12,10},{14,8},{1,7},{3,5},... | collective-permute-start | bytes 835592 | tf_op jit(solution)/shard_map/ppermute | solution.py:369
  62.0 1.0 copy-start.1
  77.8 17.3 %collective-permute-start.8 = (bf16[256,512]{1,0:T(8,128)(2,1)S(1)}, bf16[256,512]{1,0:T(8,128)(2,1)S(1)}, u32[]{:S(2)}, u32[]{:S(2)}) collective-permute-start(bf16[256,512]{1,0:T(8,128)(2,1)S(1)} %get-tuple-element.41), channel_id=1, source_target_pairs={{0,16},{2,18},{4,20},{6,22},{8,24},{10,26},{12,28},{14,30},{16,0},... | collective-permute-start | bytes 786440 | tf_op jit(solution)/shard_map/ppermute | solution.py:380
  78.2 24.9 %collective-permute-start.9 = (bf16[256,512]{1,0:T(8,128)(2,1)S(1)}, bf16[256,512]{1,0:T(8,128)(2,1)S(1)}, u32[]{:S(2)}, u32[]{:S(2)}) collective-permute-start(bf16[256,512]{1,0:T(8,128)(2,1)S(1)} %get-tuple-element.42), channel_id=1, source_target_pairs={{0,18},{2,16},{4,22},{6,20},{8,26},{10,24},{12,30},{14,28},{16,2},... | collective-permute-start | bytes 786440 | tf_op jit(solution)/shard_map/ppermute | solution.py:380
  80.3 27.7 %collective-permute-start.10 = (bf16[256,512]{1,0:T(8,128)(2,1)S(1)}, bf16[256,512]{1,0:T(8,128)(2,1)S(1)}, u32[]{:S(2)}, u32[]{:S(2)}) collective-permute-start(bf16[256,512]{1,0:T(8,128)(2,1)S(1)} %get-tuple-element.43), channel_id=1, source_target_pairs={{0,24},{2,26},{4,28},{6,30},{8,16},{10,18},{12,20},{14,22},{16,8},... | collective-permute-start | bytes 786440 | tf_op jit(solution)/shard_map/ppermute | solution.py:380
  80.3 33.3 %collective-permute-start.11 = (bf16[256,512]{1,0:T(8,128)(2,1)S(1)}, bf16[256,512]{1,0:T(8,128)(2,1)S(1)}, u32[]{:S(2)}, u32[]{:S(2)}) collective-permute-start(bf16[256,512]{1,0:T(8,128)(2,1)S(1)} %get-tuple-element.44), channel_id=1, source_target_pairs={{0,26},{2,24},{4,30},{6,28},{8,18},{10,16},{12,22},{14,20},{16,10}... | collective-permute-start | bytes 786440 | tf_op jit(solution)/shard_map/ppermute | solution.py:380
  83.5 38.7 %collective-permute-start.12 = (bf16[256,512]{1,0:T(8,128)(2,1)S(1)}, bf16[256,512]{1,0:T(8,128)(2,1)S(1)}, u32[]{:S(2)}, u32[]{:S(2)}) collective-permute-start(bf16[256,512]{1,0:T(8,128)(2,1)S(1)} %get-tuple-element.45), channel_id=1, source_target_pairs={{0,28},{2,30},{4,24},{6,26},{8,20},{10,22},{12,16},{14,18},{16,12}... | collective-permute-start | bytes 786440 | tf_op jit(solution)/shard_map/ppermute | solution.py:380
  95.1 32.7 %collective-permute-start.13 = (bf16[256,512]{1,0:T(8,128)(2,1)S(1)}, bf16[256,512]{1,0:T(8,128)(2,1)S(1)}, u32[]{:S(2)}, u32[]{:S(2)}) collective-permute-start(bf16[256,512]{1,0:T(8,128)(2,1)S(1)} %get-tuple-element.46), channel_id=1, source_target_pairs={{0,30},{2,28},{4,26},{6,24},{8,22},{10,20},{12,18},{14,16},{16,14}... | collective-permute-start | bytes 786440 | tf_op jit(solution)/shard_map/ppermute | solution.py:380
  103.0 24.8 %collective-permute-start.14 = (bf16[256,512]{1,0:T(8,128)(2,1)S(1)}, bf16[256,512]{1,0:T(8,128)(2,1)S(1)}, u32[]{:S(2)}, u32[]{:S(2)}) collective-permute-start(bf16[256,512]{1,0:T(8,128)(2,1)S(1)} %get-tuple-element.47), channel_id=1, source_target_pairs={{0,20},{2,22},{4,16},{6,18},{8,28},{10,30},{12,24},{14,26},{16,4},... | collective-permute-start | bytes 786440 | tf_op jit(solution)/shard_map/ppermute | solution.py:380
  108.0 19.8 %collective-permute-start.15 = (bf16[256,512]{1,0:T(8,128)(2,1)S(1)}, bf16[256,512]{1,0:T(8,128)(2,1)S(1)}, u32[]{:S(2)}, u32[]{:S(2)}) collective-permute-start(bf16[256,512]{1,0:T(8,128)(2,1)S(1)} %get-tuple-element.48), channel_id=1, source_target_pairs={{0,22},{2,20},{4,18},{6,16},{8,30},{10,28},{12,26},{14,24},{16,6},... | collective-permute-start | bytes 786440 | tf_op jit(solution)/shard_map/ppermute | solution.py:380
  130.1 5.0 %collective-permute-start.16 = (bf16[3,64,4096]{2,1,0:T(8,128)(2,1)S(1)}, bf16[3,64,4096]{2,1,0:T(8,128)(2,1)S(1)}, u32[]{:S(2)}, u32[]{:S(2)}) collective-permute-start(bf16[3,64,4096]{2,1,0:T(8,128)(2,1)S(1)} %get-tuple-element.49), channel_id=1, source_target_pairs={{0,1},{1,0},{2,3},{3,2},{4,5},{5,4},{6,7},{7,6},{8,9},{9,8},{10,11... | collective-permute-start | bytes 4718600 | tf_op jit(solution)/shard_map/ppermute | solution.py:443

commit v5 on v3

--- a/solution.py
+++ b/solution.py
@@ -40,7 +40,7 @@
     outs = refs[:-6]
     peers = len(outs) // chunks
     rows = grad_ref.shape[1]
-    width = outs[0].shape[1]
+    width = outs[-1].shape[0] // (2 * rows) * LANES
     span = peers * width
     me = lax.axis_index("ctx")
     loads, stores = [], []
@@ -65,13 +65,14 @@
             query, key_rows, value, grad_in = [
                 arrived[array, :, pl.ds(first, width)].astype(F32) for array in range(4)
             ]
-            made[at, :rows, :] = (key_rows * value).astype(BF16)
-            made[at, rows : 2 * rows, :] = (grad_in * query).astype(BF16)
+            for sub in range(width // LANES):
+                lanes = slice(sub * LANES, (sub + 1) * LANES)
+                top = 2 * rows * sub
+                made[at, top : top + rows, :] = (key_rows * value)[:, lanes].astype(BF16)
+                made[at, top + rows : top + 2 * rows, :] = (grad_in * query)[:, lanes].astype(BF16)
             if chunk == 0:
-                made[at, 2 * rows :, :LANES] = marks
-                if width > LANES:
-                    made[at, 2 * rows :, LANES:] = jnp.zeros((MARK_ROWS, width - LANES), BF16)
-            source = made.at[at] if chunk == 0 else made.at[at, : 2 * rows]
+                made[at, made.shape[1] - MARK_ROWS :, :] = marks
+            source = made.at[at] if chunk == 0 else made.at[at, : made.shape[1] - MARK_ROWS]
             stores.append(pltpu.make_async_copy(source, outs[at], out_sems.at[at]))
             stores[-1].start()
         lanes = pl.ds(chunk * span, span)
@@ -91,8 +92,9 @@
 def multiply(chunks, width, peers, qkv_proj, cotangent, marks):
     _, rows, channels = cotangent.shape
     anywhere = pl.BlockSpec(memory_space=pl.ANY)
-    tall = 2 * rows + MARK_ROWS
-    shapes = [(tall if chunk == 0 else 2 * rows, width) for chunk in range(chunks)]
+    plain = 2 * rows * (width // LANES)
+    tall = plain + MARK_ROWS
+    shapes = [(tall if chunk == 0 else plain, LANES) for chunk in range(chunks)]
     shapes = [shape for shape in shapes for _ in range(peers)] + [(3, rows, channels)]
     made = pl.pallas_call(
         functools.partial(multiply_kernel, chunks),
@@ -101,7 +103,7 @@
         out_specs=[anywhere] * len(shapes),
         scratch_shapes=[
             pltpu.VMEM((4, rows, channels), BF16),
-            pltpu.VMEM((chunks * peers, tall, width), BF16),
+            pltpu.VMEM((chunks * peers, tall, LANES), BF16),
             pltpu.SemaphoreType.DMA((chunks, 4)),
             pltpu.SemaphoreType.DMA((chunks * peers,)),
             pltpu.SemaphoreType.DMA((chunks, 3)),
@@ -185,35 +187,60 @@
     )(meta, *received)
 
 
-def conv_kernel(group_size, me_at, peers, meta_ref, mask_ref, base_ref, *refs):
-    rows32, rows16, toep = refs[-3:]
+def toeplitz_kernel(base_ref, out_ref):
+    _, groups, tile, span = out_ref.shape
+    for group in range(groups):
+        base = jnp.broadcast_to(base_ref[0, group : group + 1, :], (tile, span))
+        out_ref[0, group] = pltpu.roll(base, 0, 1, stride=1, stride_axis=0).astype(BF16)
+
+
+def toeplitz_of(bases):
+    two, groups, span = bases.shape
+    out = (two, groups, span // 2, span)
+    return pl.pallas_call(
+        toeplitz_kernel,
+        out_shape=jax.ShapeDtypeStruct(out, BF16),
+        in_specs=[pl.BlockSpec((1, groups, span), lambda i: (i, 0, 0))],
+        out_specs=pl.BlockSpec((1,) + out[1:], lambda i: (i, 0, 0, 0)),
+        compiler_params=params(24),
+        cost_estimate=pl.CostEstimate(
+            flops=two * groups * span * span, bytes_accessed=2 * math.prod(out), transcendentals=0
+        ),
+        grid=(two,),
+        name="toeplitz",
+    )(bases)
+
+
+def conv_kernel(group_size, me_at, peers, meta_ref, mask_ref, toep_ref, *refs):
+    rows32, rows16, toep, sem = refs[-4:]
     recv = refs[:peers]
     outs = refs[peers : 2 * peers]
     me = meta_ref[me_at]
     arrivals = [(me ^ k, recv_ref) for k, recv_ref in zip(sending_order(peers), recv)]
     tile = LANES
     width = outs[0].shape[1]
-    groups = base_ref.shape[1]
     block_rows = tile // peers
     rows16[0, :tile, :] = jnp.zeros((tile, width), BF16)
     rows16[1, peers * tile :, :] = jnp.zeros((tile, width), BF16)
 
-    for half in range(2):
-        for group in range(groups):
-            base = jnp.broadcast_to(base_ref[half, group : group + 1, :], (tile, 2 * tile))
-            toep[half, group] = pltpu.roll(base, 0, 1, stride=1, stride_axis=0).astype(BF16)
+    load = pltpu.make_async_copy(toep_ref, toep, sem)
+    load.start()
 
     for source, recv_ref in arrivals:
         firsts = [first_row(meta_ref, peers, source, block) for block in range(peers)]
         for half in range(2):
-            arrived = recv_ref[half * tile : (half + 1) * tile, :].astype(F32)
-            for block in range(peers):
-                rows32[half, pl.ds(firsts[block], block_rows), :] = arrived[
-                    block * block_rows : (block + 1) * block_rows
-                ]
+            for sub in range(width // tile):
+                top = (2 * sub + half) * tile
+                lanes = slice(sub * tile, (sub + 1) * tile)
+                arrived = recv_ref[top : top + tile, :].astype(F32)
+                for block in range(peers):
+                    rows32[half, pl.ds(firsts[block], block_rows), lanes] = arrived[
+                        block * block_rows : (block + 1) * block_rows
+                    ]
     rows16[0, tile:, :] = rows32[0].astype(BF16)
     rows16[1, : peers * tile, :] = rows32[1].astype(BF16)
 
+    load.wait()
     tile_groups = tile // group_size
     lane_group = lax.broadcasted_iota(jnp.int32, (tile, tile), 1) // group_size
 
@@ -246,22 +273,23 @@
             )
 
 
-def convolve(group_size, me_at, meta, received, masks, bases):
+def convolve(group_size, me_at, meta, received, masks, toeplitz):
     peers = masks.shape[0]
     tile = LANES
-    width = received[0].shape[-1]
-    groups = bases.shape[1]
+    groups = toeplitz.shape[1]
+    width = groups * group_size
     out = (2 * tile, width)
     outs = pl.pallas_call(
         functools.partial(conv_kernel, group_size, me_at, peers),
         out_shape=[jax.ShapeDtypeStruct(out, BF16)] * peers,
-        in_specs=[smem(), whole_block(*masks.shape), whole_block(*bases.shape)]
+        in_specs=[smem(), whole_block(*masks.shape), pl.BlockSpec(memory_space=pl.ANY)]
         + [whole_block(*r.shape) for r in received],
         out_specs=[whole_block(*out)] * peers,
         scratch_shapes=[
             pltpu.VMEM((2, peers * tile, width), F32),
             pltpu.VMEM((2, (peers + 1) * tile, width), BF16),
             pltpu.VMEM((2, groups, tile, 2 * tile), BF16),
+            pltpu.SemaphoreType.DMA,
         ],
         compiler_params=params(40),
         cost_estimate=pl.CostEstimate(
@@ -271,7 +299,7 @@
         ),
         grid=(1,),
         name="convolve",
-    )(meta, masks, bases, *received)
+    )(meta, masks, toeplitz, *received)
     return list(outs)
 
 
@@ -411,6 +439,7 @@
     to_previous = [(pipe, (pipe - 1) % pipes) for pipe in range(pipes)]
     order = sending_order(peers)
     products, side = multiply(chunks, width, peers, qkv_proj, cotangent, doc_start)
+    toeplitz = [toeplitz_of(bases[chunk]) for chunk in range(chunks)]
     received = [swap(array, k) for array, k in zip(products[0], order)]
     side = lax.ppermute(side, "pipe", to_previous)
 
@@ -419,7 +448,7 @@
     backs, late = [], []
     for chunk in range(chunks):
         coming = products[chunk + 1] if chunk + 1 < chunks else []
-        convolved = convolve(group_size, me_at, meta, received, masks, bases[chunk])
+        convolved = convolve(group_size, me_at, meta, received, masks, toeplitz[chunk])
         convolved, waited, late = lax.optimization_barrier((convolved, coming[first_out:], late))
         received = [swap(array, k) for array, k in zip(coming[:first_out] + waited, order)]
         if chunk:

time: 137 us -> 138 us (level)
  starting transfers between devices: 26.7 us -> 37.8 us
  waiting for transfers between devices: 82.7 us -> 73.4 us
    ppermute x8, starting transfers between devices: 5.99 us -> 15.6 us  [swap_to_previous(): return lax.ppermute(array, ('pipe', 'ctx'), pairs)]
    ppermute x8, waiting for transfers between devices: 48 us -> 41.6 us  [swap_to_previous(): return lax.ppermute(array, ('pipe', 'ctx'), pairs)]
    ppermute x7, waiting for transfers between devices: 31.7 us -> 28.7 us  [swap(): lax.ppermute(array, 'ctx', [(i, i ^ k) for i in range(peers)])]
    ppermute x1, starting transfers between devices: 0.49 us -> 2.46 us  [shards(): held.append(lax.ppermute(cross, 'tp', [(0, 1), (1, 0)]))]
where the time goes in v5:
time: 138 us; the launch traced here: 137 us
  waiting for transfers between devices  73.4 us (53%)
  starting transfers between devices  37.8 us (27%)
  Pallas kernels  24.8 us (18%)
    ppermute x8, waiting for transfers between devices, swap_to_previous(): return lax.ppermute(array, ('pipe', 'ctx'), pairs)  41.6 us
    ppermute x7, waiting for transfers between devices, swap(): lax.ppermute(array, 'ctx', [(i, i ^ k) for i in range(peers)])  28.7 us
    ppermute x7, starting transfers between devices, swap(): lax.ppermute(array, 'ctx', [(i, i ^ k) for i in range(peers)])  18.5 us
    ppermute x8, starting transfers between devices, swap_to_previous(): return lax.ppermute(array, ('pipe', 'ctx'), pairs)  15.6 us
    pallas_call x1, Pallas kernels, convolve(): pl.pallas_call(functools.partial(conv_kernel, group_size, me_at, peers),...  12.7 us
    pallas_call x1, Pallas kernels, multiply(): pl.pallas_call(functools.partial(multiply_kernel, chunks), out_shape=[jax...  5.31 us
    ppermute x1, waiting for transfers between devices, shards(): held.append(lax.ppermute(cross, 'tp', [(0, 1), (1, 0)]))  3.04 us
  transfers between devices with their start and end apart: 17, of which 8 were waited for; matrix products, arithmetic and copies ran while one was open for 1% of the time, Pallas kernels for 11%

profile of v5, /device:TPU:21, one launch (start us, length us, event | category | flops | bytes accessed | tf_op | source)
XLA Modules:
  0.0 137.1 jit_solution(5689585789695434686)
XLA Ops:
  0.0 0.0 copy-start
  0.0 5.3 %multiply.1 = (bf16[1040,128]{1,0:T(8,128)(2,1)}, bf16[1040,128]{1,0:T(8,128)(2,1)}, bf16[1040,128]{1,0:T(8,128)(2,1)}, bf16[1040,128]{1,0:T(8,128)(2,1)}, bf16[...) custom-call(bf16[1,3,128,4096]{3,2,1,0:T(8,128)(2,1)} %proj_ref.1, ...), custom_call_target="tpu_custom_call" | custom-call | flops 1048576 | bytes 9437184 | tf_op jit(solution)/shard_map/multiply/pallas_call | solution.py:99
  5.3 0.0 copy-start.1
  5.3 1.3 collective-permute-start.7
  6.6 0.1 collective-permute-start
  6.7 0.2 collective-permute-start.1
  6.9 3.3 %collective-permute-start.2 = (bf16[1040,128]{1,0:T(8,128)(2,1)}, bf16[1040,128]{1,0:T(8,128)(2,1)}, u32[]{:S(2)}, u32[]{:S(2)}) collective-permute-start(bf16[1040,128]{1,0:T(8,128)(2,1)} %get-tuple-element.31), channel_id=1, source_target_pairs={{0,10},{2,8},{4,14},{6,12},{8,2},{10,0},{12,6},{14,4},{1,11},{3,9}... | collective-permute-start | bytes 798728 | tf_op jit(solution)/shard_map/ppermute | solution.py:397
  10.2 1.3 collective-permute-start.3
  11.5 0.7 convert_bitcast_fusion
  12.2 0.1 rev.3
  12.2 0.1 pad_bitcast_fusion
  12.3 11.1 %collective-permute-done.refs_1_ = bf16[1040,128]{1,0:T(8,128)(2,1)} collective-permute-done((bf16[1040,128]{1,0:T(8,128)(2,1)}, bf16[1040,128]{1,0:T(8,128)(2,1)}, u32[]{:S(2)}, u32[]{:S(2)}) %collective-permute-start) | collective-permute-done | bytes 266272 | tf_op jit(solution)/shard_map/ppermute | solution.py:397
  23.4 3.4 %collective-permute-start.4 = (bf16[1040,128]{1,0:T(8,128)(2,1)}, bf16[1040,128]{1,0:T(8,128)(2,1)}, u32[]{:S(2)}, u32[]{:S(2)}) collective-permute-start(bf16[1040,128]{1,0:T(8,128)(2,1)} %get-tuple-element.33), channel_id=1, source_target_pairs={{0,12},{2,14},{4,8},{6,10},{8,4},{10,6},{12,0},{14,2},{1,13},{3,15... | collective-permute-start | bytes 798728 | tf_op jit(solution)/shard_map/ppermute | solution.py:397
  26.8 0.0 collective-permute-done.1.refs_2_
  26.8 1.9 %collective-permute-start.5 = (bf16[1040,128]{1,0:T(8,128)(2,1)}, bf16[1040,128]{1,0:T(8,128)(2,1)}, u32[]{:S(2)}, u32[]{:S(2)}) collective-permute-start(bf16[1040,128]{1,0:T(8,128)(2,1)} %get-tuple-element.34), channel_id=1, source_target_pairs={{0,6},{2,4},{4,2},{6,0},{8,14},{10,12},{12,10},{14,8},{1,7},{3,5},... | collective-permute-start | bytes 798728 | tf_op jit(solution)/shard_map/ppermute | solution.py:397
  28.7 0.5 collective-permute-done.2.refs_3_
  29.1 8.4 %collective-permute-start.6 = (bf16[1040,128]{1,0:T(8,128)(2,1)}, bf16[1040,128]{1,0:T(8,128)(2,1)}, u32[]{:S(2)}, u32[]{:S(2)}) collective-permute-start(bf16[1040,128]{1,0:T(8,128)(2,1)} %get-tuple-element.35), channel_id=1, source_target_pairs={{0,14},{2,12},{4,10},{6,8},{8,6},{10,4},{12,2},{14,0},{1,15},{3,13... | collective-permute-start | bytes 798728 | tf_op jit(solution)/shard_map/ppermute | solution.py:397
  37.6 1.2 toeplitz.1.toep_ref
  38.8 0.0 copy-done
  38.8 0.1 pad_add_fusion.meta_ref
  38.9 0.0 collective-permute-done.3.refs_4_
  38.9 11.5 %collective-permute-done.4.refs_5_ = bf16[1040,128]{1,0:T(8,128)(2,1)} collective-permute-done((bf16[1040,128]{1,0:T(8,128)(2,1)}, bf16[1040,128]{1,0:T(8,128)(2,1)}, u32[]{:S(2)}, u32[]{:S(2)}) %collective-permute-start.4) | collective-permute-done | bytes 266272 | tf_op jit(solution)/shard_map/ppermute | solution.py:397
  50.4 0.0 collective-permute-done.5.refs_6_
  50.4 5.6 %collective-permute-done.6.refs_7_ = bf16[1040,128]{1,0:T(8,128)(2,1)} collective-permute-done((bf16[1040,128]{1,0:T(8,128)(2,1)}, bf16[1040,128]{1,0:T(8,128)(2,1)}, u32[]{:S(2)}, u32[]{:S(2)}) %collective-permute-start.6) | collective-permute-done | bytes 266272 | tf_op jit(solution)/shard_map/ppermute | solution.py:397
  56.1 0.0 copy-done.1
  56.1 1.5 %masks.1.mask_ref = bf16[8,2,128,256]{3,2,1,0:T(8,128)(2,1)S(1)} custom-call(s32[66]{0:T(128)S(1)} %pad_add_fusion.meta_ref, bf16[1040,128]{1,0:T(8,128)(2,1)S(1)} %copy-done.1, bf16[1040,128]{1,0:T(8,128)(2,1)} %collective-permute-done.refs_1_, bf16[1040,128]{1,0:T(8,128)(2,1)} %collective-permute-done.1.refs_2_, ...), custom_call_target="tpu_custom_call" | custom-call | flops 1048576 | bytes 1048576 | tf_op jit(solution)/shard_map/masks/pallas_call | solution.py:172
  57.5 12.7 %convolve.1 = (bf16[256,512]{1,0:T(8,128)(2,1)S(1)}, bf16[256,512]{1,0:T(8,128)(2,1)S(1)}, bf16[256,512]{1,0:T(8,128)(2,1)S(1)}, bf16[256,512]{1,0:T(8,128)(2,1)...) custom-call(s32[66]{0:T(128)S(1)} %pad_add_fusion.meta_ref, ...), custom_call_target="tpu_custom_call" | custom-call | flops 4294967296 | bytes 4718592 | tf_op jit(solution)/shard_map/convolve/pallas_call | solution.py:282
  70.2 0.3 collective-permute-start.8
  70.5 0.0 collective-permute-start.9
  70.5 2.2 %collective-permute-start.10 = (bf16[256,512]{1,0:T(8,128)(2,1)S(1)}, bf16[256,512]{1,0:T(8,128)(2,1)S(1)}, u32[]{:S(2)}, u32[]{:S(2)}) collective-permute-start(bf16[256,512]{1,0:T(8,128)(2,1)S(1)} %get-tuple-element.43), channel_id=1, source_target_pairs={{0,18},{2,16},{4,22},{6,20},{8,26},{10,24},{12,30},{14,28},{16,2},... | collective-permute-start | bytes 786440 | tf_op jit(solution)/shard_map/ppermute | solution.py:408
  72.7 3.2 %collective-permute-start.11 = (bf16[256,512]{1,0:T(8,128)(2,1)S(1)}, bf16[256,512]{1,0:T(8,128)(2,1)S(1)}, u32[]{:S(2)}, u32[]{:S(2)}) collective-permute-start(bf16[256,512]{1,0:T(8,128)(2,1)S(1)} %get-tuple-element.44), channel_id=1, source_target_pairs={{0,26},{2,24},{4,30},{6,28},{8,18},{10,16},{12,22},{14,20},{16,10}... | collective-permute-start | bytes 786440 | tf_op jit(solution)/shard_map/ppermute | solution.py:408
  75.9 0.0 collective-permute-done.7.side_ref
  75.9 4.9 %collective-permute-start.12 = (bf16[256,512]{1,0:T(8,128)(2,1)S(1)}, bf16[256,512]{1,0:T(8,128)(2,1)S(1)}, u32[]{:S(2)}, u32[]{:S(2)}) collective-permute-start(bf16[256,512]{1,0:T(8,128)(2,1)S(1)} %get-tuple-element.45), channel_id=1, source_target_pairs={{0,20},{2,22},{4,16},{6,18},{8,28},{10,30},{12,24},{14,26},{16,4},... | collective-permute-start | bytes 786440 | tf_op jit(solution)/shard_map/ppermute | solution.py:408
  80.9 13.4 %collective-permute-done.8.refs_0_ = bf16[256,512]{1,0:T(8,128)(2,1)S(1)} collective-permute-done((bf16[256,512]{1,0:T(8,128)(2,1)S(1)}, bf16[256,512]{1,0:T(8,128)(2,1)S(1)}, u32[]{:S(2)}, u32[]{:S(2)}) %collective-permute-start.8) | collective-permute-done | bytes 262176 | tf_op jit(solution)/shard_map/ppermute | solution.py:408
  94.2 3.9 %collective-permute-start.13 = (bf16[256,512]{1,0:T(8,128)(2,1)S(1)}, bf16[256,512]{1,0:T(8,128)(2,1)S(1)}, u32[]{:S(2)}, u32[]{:S(2)}) collective-permute-start(bf16[256,512]{1,0:T(8,128)(2,1)S(1)} %get-tuple-element.46), channel_id=1, source_target_pairs={{0,28},{2,30},{4,24},{6,26},{8,20},{10,22},{12,16},{14,18},{16,12}... | collective-permute-start | bytes 786440 | tf_op jit(solution)/shard_map/ppermute | solution.py:408
  98.1 0.0 collective-permute-done.9.refs_1_
  98.1 1.1 collective-permute-start.14
  99.2 14.6 %collective-permute-done.10.refs_2_ = bf16[256,512]{1,0:T(8,128)(2,1)S(1)} collective-permute-done((bf16[256,512]{1,0:T(8,128)(2,1)S(1)}, bf16[256,512]{1,0:T(8,128)(2,1)S(1)}, u32[]{:S(2)}, u32[]{:S(2)}) %collective-permute-start.10) | collective-permute-done | bytes 262176 | tf_op jit(solution)/shard_map/ppermute | solution.py:408
  113.8 0.0 collective-permute-start.15
  113.8 0.0 collective-permute-done.11.refs_3_
  113.8 0.0 collective-permute-done.12.refs_4_
  113.9 0.0 collective-permute-done.13.refs_5_
  113.9 0.0 collective-permute-done.14.refs_6_
  113.9 13.6 %collective-permute-done.15.refs_7_ = bf16[256,512]{1,0:T(8,128)(2,1)S(1)} collective-permute-done((bf16[256,512]{1,0:T(8,128)(2,1)S(1)}, bf16[256,512]{1,0:T(8,128)(2,1)S(1)}, u32[]{:S(2)}, u32[]{:S(2)}) %collective-permute-start.15) | collective-permute-done | bytes 262176 | tf_op jit(solution)/shard_map/ppermute | solution.py:408
  127.5 2.3 %gradients.1 = (bf16[1,3,64,8192]{3,2,1,0:T(8,128)(2,1)}, bf16[3,64,4096]{2,1,0:T(8,128)(2,1)S(1)}) custom-call(s32[66]{0:T(128)S(1)} %pad_add_fusion.meta_ref, bf16[3,128,4096]{2,1,0:T(8,128)(2,1)S(1)} %collective-permute-done.7.side_ref, bf16[256,512]{1,0:T(8,128)(2,1)S(1)} %collective-permute-done.8.refs_0_, ...), custom_call_target="tpu_custom_call" | custom-call | flops 1572864 | bytes 8388608 | tf_op jit(solution)/shard_map/gradients/pallas_call | solution.py:354
  129.8 2.5 %collective-permute-start.16 = (bf16[3,64,4096]{2,1,0:T(8,128)(2,1)S(1)}, bf16[3,64,4096]{2,1,0:T(8,128)(2,1)S(1)}, u32[]{:S(2)}, u32[]{:S(2)}) collective-permute-start(bf16[3,64,4096]{2,1,0:T(8,128)(2,1)S(1)} %get-tuple-element.49), channel_id=1, source_target_pairs={{0,1},{1,0},{2,3},{3,2},{4,5},{5,4},{6,7},{7,6},{8,9},{9,8},{10,11... | collective-permute-start | bytes 4718600 | tf_op jit(solution)/shard_map/ppermute | solution.py:472
  132.3 3.0 %collective-permute-done.16.cross_ref = bf16[3,64,4096]{2,1,0:T(8,128)(2,1)S(1)} collective-permute-done((bf16[3,64,4096]{2,1,0:T(8,128)(2,1)S(1)}, bf16[3,64,4096]{2,1,0:T(8,128)(2,1)S(1)}, u32[]{:S(2)}, u32[]{:S(2)}) %collective-permute-start.16) | collective-permute-done | bytes 1572896 | tf_op jit(solution)/shard_map/ppermute | solution.py:472
  135.3 1.8 %place.1 = bf16[1,3,64,8192]{3,2,1,0:T(8,128)(2,1)} custom-call(s32[66]{0:T(128)S(1)} %pad_add_fusion.meta_ref, bf16[3,64,4096]{2,1,0:T(8,128)(2,1)S(1)} %collective-permute-done.16.cross_ref, bf16[1,3,64,8192]{3,2,1,0:T(8,128)(2,1)} %get-tuple-element.50.held_ref), custom_call_target="tpu_custom_call", output_to_operand_aliasing={{}: (2, {})} | custom-call | bytes 3145728 | tf_op jit(solution)/shard_map/place/pallas_call | solution.py:377
  (2 shorter events, 0.0 us)
Async XLA Ops:
  0.0 38.8 %copy-start = (s32[2,64]{1,0:T(2,128)S(1)}, s32[2,64]{1,0:T(2,128)}, u32[]{:S(2)}) copy-start(s32[2,64]{1,0:T(2,128)} %param.7) | copy-start | bytes 1540
  5.3 50.7 %copy-start.1 = (bf16[1040,128]{1,0:T(8,128)(2,1)S(1)}, bf16[1040,128]{1,0:T(8,128)(2,1)}, u32[]{:S(2)}) copy-start(bf16[1040,128]{1,0:T(8,128)(2,1)} %get-tuple-element.28.refs_0_) | copy-start | bytes 798724
  5.3 70.6 %collective-permute-start.7 = (bf16[3,128,4096]{2,1,0:T(8,128)(2,1)}, bf16[3,128,4096]{2,1,0:T(8,128)(2,1)S(1)}, u32[]{:S(2)}, u32[]{:S(2)}) collective-permute-start(bf16[3,128,4096]{2,1,0:T(8,128)(2,1)} %get-tuple-element.39), channel_id=1, source_target_pairs={{0,16},{16,0},{1,17},{17,1},{2,18},{18,2},{3,19},{19,3},{4,20},{20... | collective-permute-start | bytes 9437192 | tf_op jit(solution)/shard_map/ppermute | solution.py:444
  6.6 16.8 %collective-permute-start = (bf16[1040,128]{1,0:T(8,128)(2,1)}, bf16[1040,128]{1,0:T(8,128)(2,1)}, u32[]{:S(2)}, u32[]{:S(2)}) collective-permute-start(bf16[1040,128]{1,0:T(8,128)(2,1)} %get-tuple-element.29), channel_id=1, source_target_pairs={{0,8},{2,10},{4,12},{6,14},{8,0},{10,2},{12,4},{14,6},{1,9},{3,11}... | collective-permute-start | bytes 798728 | tf_op jit(solution)/shard_map/ppermute | solution.py:397
  6.7 20.2 %collective-permute-start.1 = (bf16[1040,128]{1,0:T(8,128)(2,1)}, bf16[1040,128]{1,0:T(8,128)(2,1)}, u32[]{:S(2)}, u32[]{:S(2)}) collective-permute-start(bf16[1040,128]{1,0:T(8,128)(2,1)} %get-tuple-element.30), channel_id=1, source_target_pairs={{0,2},{2,0},{4,6},{6,4},{8,10},{10,8},{12,14},{14,12},{1,3},{3,1},... | collective-permute-start | bytes 798728 | tf_op jit(solution)/shard_map/ppermute | solution.py:397
  6.9 22.3 %collective-permute-start.2 = (bf16[1040,128]{1,0:T(8,128)(2,1)}, bf16[1040,128]{1,0:T(8,128)(2,1)}, u32[]{:S(2)}, u32[]{:S(2)}) collective-permute-start(bf16[1040,128]{1,0:T(8,128)(2,1)} %get-tuple-element.31), channel_id=1, source_target_pairs={{0,10},{2,8},{4,14},{6,12},{8,2},{10,0},{12,6},{14,4},{1,11},{3,9}... | collective-permute-start | bytes 798728 | tf_op jit(solution)/shard_map/ppermute | solution.py:397
  10.2 28.8 %collective-permute-start.3 = (bf16[1040,128]{1,0:T(8,128)(2,1)}, bf16[1040,128]{1,0:T(8,128)(2,1)}, u32[]{:S(2)}, u32[]{:S(2)}) collective-permute-start(bf16[1040,128]{1,0:T(8,128)(2,1)} %get-tuple-element.32), channel_id=1, source_target_pairs={{0,4},{2,6},{4,0},{6,2},{8,12},{10,14},{12,8},{14,10},{1,5},{3,7},... | collective-permute-start | bytes 798728 | tf_op jit(solution)/shard_map/ppermute | solution.py:397
  23.4 27.0 %collective-permute-start.4 = (bf16[1040,128]{1,0:T(8,128)(2,1)}, bf16[1040,128]{1,0:T(8,128)(2,1)}, u32[]{:S(2)}, u32[]{:S(2)}) collective-permute-start(bf16[1040,128]{1,0:T(8,128)(2,1)} %get-tuple-element.33), channel_id=1, source_target_pairs={{0,12},{2,14},{4,8},{6,10},{8,4},{10,6},{12,0},{14,2},{1,13},{3,15... | collective-permute-start | bytes 798728 | tf_op jit(solution)/shard_map/ppermute | solution.py:397
  26.8 23.6 %collective-permute-start.5 = (bf16[1040,128]{1,0:T(8,128)(2,1)}, bf16[1040,128]{1,0:T(8,128)(2,1)}, u32[]{:S(2)}, u32[]{:S(2)}) collective-permute-start(bf16[1040,128]{1,0:T(8,128)(2,1)} %get-tuple-element.34), channel_id=1, source_target_pairs={{0,6},{2,4},{4,2},{6,0},{8,14},{10,12},{12,10},{14,8},{1,7},{3,5},... | collective-permute-start | bytes 798728 | tf_op jit(solution)/shard_map/ppermute | solution.py:397
  29.1 26.9 %collective-permute-start.6 = (bf16[1040,128]{1,0:T(8,128)(2,1)}, bf16[1040,128]{1,0:T(8,128)(2,1)}, u32[]{:S(2)}, u32[]{:S(2)}) collective-permute-start(bf16[1040,128]{1,0:T(8,128)(2,1)} %get-tuple-element.35), channel_id=1, source_target_pairs={{0,14},{2,12},{4,10},{6,8},{8,6},{10,4},{12,2},{14,0},{1,15},{3,13... | collective-permute-start | bytes 798728 | tf_op jit(solution)/shard_map/ppermute | solution.py:397
  70.2 24.0 %collective-permute-start.8 = (bf16[256,512]{1,0:T(8,128)(2,1)S(1)}, bf16[256,512]{1,0:T(8,128)(2,1)S(1)}, u32[]{:S(2)}, u32[]{:S(2)}) collective-permute-start(bf16[256,512]{1,0:T(8,128)(2,1)S(1)} %get-tuple-element.41), channel_id=1, source_target_pairs={{0,16},{2,18},{4,20},{6,22},{8,24},{10,26},{12,28},{14,30},{16,0},... | collective-permute-start | bytes 786440 | tf_op jit(solution)/shard_map/ppermute | solution.py:408
  70.5 27.6 %collective-permute-start.9 = (bf16[256,512]{1,0:T(8,128)(2,1)S(1)}, bf16[256,512]{1,0:T(8,128)(2,1)S(1)}, u32[]{:S(2)}, u32[]{:S(2)}) collective-permute-start(bf16[256,512]{1,0:T(8,128)(2,1)S(1)} %get-tuple-element.42), channel_id=1, source_target_pairs={{0,24},{2,26},{4,28},{6,30},{8,16},{10,18},{12,20},{14,22},{16,8},... | collective-permute-start | bytes 786440 | tf_op jit(solution)/shard_map/ppermute | solution.py:408
  70.5 43.3 %collective-permute-start.10 = (bf16[256,512]{1,0:T(8,128)(2,1)S(1)}, bf16[256,512]{1,0:T(8,128)(2,1)S(1)}, u32[]{:S(2)}, u32[]{:S(2)}) collective-permute-start(bf16[256,512]{1,0:T(8,128)(2,1)S(1)} %get-tuple-element.43), channel_id=1, source_target_pairs={{0,18},{2,16},{4,22},{6,20},{8,26},{10,24},{12,30},{14,28},{16,2},... | collective-permute-start | bytes 786440 | tf_op jit(solution)/shard_map/ppermute | solution.py:408
  72.7 41.1 %collective-permute-start.11 = (bf16[256,512]{1,0:T(8,128)(2,1)S(1)}, bf16[256,512]{1,0:T(8,128)(2,1)S(1)}, u32[]{:S(2)}, u32[]{:S(2)}) collective-permute-start(bf16[256,512]{1,0:T(8,128)(2,1)S(1)} %get-tuple-element.44), channel_id=1, source_target_pairs={{0,26},{2,24},{4,30},{6,28},{8,18},{10,16},{12,22},{14,20},{16,10}... | collective-permute-start | bytes 786440 | tf_op jit(solution)/shard_map/ppermute | solution.py:408
  75.9 37.9 %collective-permute-start.12 = (bf16[256,512]{1,0:T(8,128)(2,1)S(1)}, bf16[256,512]{1,0:T(8,128)(2,1)S(1)}, u32[]{:S(2)}, u32[]{:S(2)}) collective-permute-start(bf16[256,512]{1,0:T(8,128)(2,1)S(1)} %get-tuple-element.45), channel_id=1, source_target_pairs={{0,20},{2,22},{4,16},{6,18},{8,28},{10,30},{12,24},{14,26},{16,4},... | collective-permute-start | bytes 786440 | tf_op jit(solution)/shard_map/ppermute | solution.py:408
  94.2 19.6 %collective-permute-start.13 = (bf16[256,512]{1,0:T(8,128)(2,1)S(1)}, bf16[256,512]{1,0:T(8,128)(2,1)S(1)}, u32[]{:S(2)}, u32[]{:S(2)}) collective-permute-start(bf16[256,512]{1,0:T(8,128)(2,1)S(1)} %get-tuple-element.46), channel_id=1, source_target_pairs={{0,28},{2,30},{4,24},{6,26},{8,20},{10,22},{12,16},{14,18},{16,12}... | collective-permute-start | bytes 786440 | tf_op jit(solution)/shard_map/ppermute | solution.py:408
  98.1 15.7 %collective-permute-start.14 = (bf16[256,512]{1,0:T(8,128)(2,1)S(1)}, bf16[256,512]{1,0:T(8,128)(2,1)S(1)}, u32[]{:S(2)}, u32[]{:S(2)}) collective-permute-start(bf16[256,512]{1,0:T(8,128)(2,1)S(1)} %get-tuple-element.47), channel_id=1, source_target_pairs={{0,22},{2,20},{4,18},{6,16},{8,30},{10,28},{12,26},{14,24},{16,6},... | collective-permute-start | bytes 786440 | tf_op jit(solution)/shard_map/ppermute | solution.py:408
  113.8 13.7 %collective-permute-start.15 = (bf16[256,512]{1,0:T(8,128)(2,1)S(1)}, bf16[256,512]{1,0:T(8,128)(2,1)S(1)}, u32[]{:S(2)}, u32[]{:S(2)}) collective-permute-start(bf16[256,512]{1,0:T(8,128)(2,1)S(1)} %get-tuple-element.48), channel_id=1, source_target_pairs={{0,30},{2,28},{4,26},{6,24},{8,22},{10,20},{12,18},{14,16},{16,14}... | collective-permute-start | bytes 786440 | tf_op jit(solution)/shard_map/ppermute | solution.py:408
  129.8 5.5 %collective-permute-start.16 = (bf16[3,64,4096]{2,1,0:T(8,128)(2,1)S(1)}, bf16[3,64,4096]{2,1,0:T(8,128)(2,1)S(1)}, u32[]{:S(2)}, u32[]{:S(2)}) collective-permute-start(bf16[3,64,4096]{2,1,0:T(8,128)(2,1)S(1)} %get-tuple-element.49), channel_id=1, source_target_pairs={{0,1},{1,0},{2,3},{3,2},{4,5},{5,4},{6,7},{7,6},{8,9},{9,8},{10,11... | collective-permute-start | bytes 4718600 | tf_op jit(solution)/shard_map/ppermute | solution.py:472

commit v6 on v5

--- a/solution.py
+++ b/solution.py
@@ -35,9 +35,8 @@
 
 
 def multiply_kernel(chunks, proj_ref, grad_ref, marks_ref, *refs):
-    arrived, made, in_sems, out_sems, side_sems = refs[-5:]
-    side_ref = refs[-6]
-    outs = refs[:-6]
+    arrived, made, in_sems, out_sems = refs[-4:]
+    outs = refs[:-4]
     peers = len(outs) // chunks
     rows = grad_ref.shape[1]
     width = outs[-1].shape[0] // (2 * rows) * LANES
@@ -75,16 +74,6 @@
             source = made.at[at] if chunk == 0 else made.at[at, : made.shape[1] - MARK_ROWS]
             stores.append(pltpu.make_async_copy(source, outs[at], out_sems.at[at]))
             stores[-1].start()
-        lanes = pl.ds(chunk * span, span)
-        for array in range(3):
-            stores.append(
-                pltpu.make_async_copy(
-                    arrived.at[array + 1, :, lanes],
-                    side_ref.at[array, :, lanes],
-                    side_sems.at[chunk, array],
-                )
-            )
-            stores[-1].start()
     for store in stores:
         store.wait()
 
@@ -95,7 +84,7 @@
     plain = 2 * rows * (width // LANES)
     tall = plain + MARK_ROWS
     shapes = [(tall if chunk == 0 else plain, LANES) for chunk in range(chunks)]
-    shapes = [shape for shape in shapes for _ in range(peers)] + [(3, rows, channels)]
+    shapes = [shape for shape in shapes for _ in range(peers)]
     made = pl.pallas_call(
         functools.partial(multiply_kernel, chunks),
         out_shape=[jax.ShapeDtypeStruct(shape, BF16) for shape in shapes],
@@ -106,15 +95,58 @@
             pltpu.VMEM((chunks * peers, tall, LANES), BF16),
             pltpu.SemaphoreType.DMA((chunks, 4)),
             pltpu.SemaphoreType.DMA((chunks * peers,)),
-            pltpu.SemaphoreType.DMA((chunks, 3)),
         ],
         compiler_params=params(60),
         cost_estimate=pl.CostEstimate(
-            flops=2 * rows * channels, bytes_accessed=18 * rows * channels, transcendentals=0
+            flops=2 * rows * channels, bytes_accessed=12 * rows * channels, transcendentals=0
         ),
         name="multiply",
     )(qkv_proj, cotangent, marks)
-    return [list(made[c * peers : (c + 1) * peers]) for c in range(chunks)], made[-1]
+    return [list(made[c * peers : (c + 1) * peers]) for c in range(chunks)]
+
+
+def side_kernel(proj_ref, grad_ref, side_ref, arrived, in_sems, out_sems):
+    sources = (proj_ref.at[0, 1], proj_ref.at[0, 2], grad_ref.at[0])
+    rows = grad_ref.shape[1]
+    parts = in_sems.shape[1]
+    loads, stores = [], []
+    for i, source in enumerate(sources):
+        for part in range(parts):
+            at = pl.ds(part * (rows // parts), rows // parts)
+            loads.append(
+                pltpu.make_async_copy(source.at[at], arrived.at[i, at], in_sems.at[i, part])
+            )
+            stores.append(
+                pltpu.make_async_copy(arrived.at[i, at], side_ref.at[i, at], out_sems.at[i, part])
+            )
+    for load in loads:
+        load.start()
+    for load, store in zip(loads, stores):
+        load.wait()
+        store.start()
+    for store in stores:
+        store.wait()
+
+
+def side_of(qkv_proj, cotangent):
+    _, rows, channels = cotangent.shape
+    anywhere = pl.BlockSpec(memory_space=pl.ANY)
+    return pl.pallas_call(
+        side_kernel,
+        out_shape=jax.ShapeDtypeStruct((3, rows, channels), BF16),
+        in_specs=[anywhere, anywhere],
+        out_specs=anywhere,
+        scratch_shapes=[
+            pltpu.VMEM((3, rows, channels), BF16),
+            pltpu.SemaphoreType.DMA((3, 2)),
+            pltpu.SemaphoreType.DMA((3, 2)),
+        ],
+        compiler_params=params(60),
+        cost_estimate=pl.CostEstimate(
+            flops=0, bytes_accessed=12 * rows * channels, transcendentals=0
+        ),
+        name="side",
+    )(qkv_proj, cotangent)
 
 
 def first_row(meta_ref, peers, source, block):
@@ -438,10 +470,10 @@
 
     to_previous = [(pipe, (pipe - 1) % pipes) for pipe in range(pipes)]
     order = sending_order(peers)
-    products, side = multiply(chunks, width, peers, qkv_proj, cotangent, doc_start)
+    products = multiply(chunks, width, peers, qkv_proj, cotangent, doc_start)
     toeplitz = [toeplitz_of(bases[chunk]) for chunk in range(chunks)]
     received = [swap(array, k) for array, k in zip(products[0], order)]
-    side = lax.ppermute(side, "pipe", to_previous)
+    side = lax.ppermute(side_of(qkv_proj, cotangent), "pipe", to_previous)
 
     first_out, first_back = OUT_FIRST * peers // 8, BACK_FIRST * peers // 8
     masks = document_masks(me_at, meta, received, MARK_ROWS)

time: 138 us -> 131 us (0.949)
  starting transfers between devices: 37.8 us -> 32.7 us
  waiting for transfers between devices: 73.4 us -> 70 us
  Pallas kernels: 24.8 us -> 26.7 us
    ppermute x8, starting transfers between devices: 15.6 us -> 11 us  [swap_to_previous(): return lax.ppermute(array, ('pipe', 'ctx'), pairs)]
    ppermute x8, waiting for transfers between devices: 41.6 us -> 38.2 us  [swap_to_previous(): return lax.ppermute(array, ('pipe', 'ctx'), pairs)]
    pallas_call x0 -> x1, Pallas kernels: none -> 2.81 us  [side_of(): pl.pallas_call(side_kernel, out_shape=jax.ShapeDtypeStruct((3, rows, chan...]
  transfers between devices with their start and end apart: 17 -> 17, of which waited for: 8 -> 9; matrix products, arithmetic and copies ran while one was open for 1% -> 1% of each run, Pallas kernels for 11% -> 15%
where the time goes in v6:
time: 131 us; the launch traced here: 130 us
  waiting for transfers between devices  70 us (53%)
  starting transfers between devices  32.7 us (25%)
  Pallas kernels  26.7 us (20%)
    ppermute x8, waiting for transfers between devices, swap_to_previous(): return lax.ppermute(array, ('pipe', 'ctx'), pairs)  38.2 us
    ppermute x7, waiting for transfers between devices, swap(): lax.ppermute(array, 'ctx', [(i, i ^ k) for i in range(peers)])  28.7 us
    ppermute x7, starting transfers between devices, swap(): lax.ppermute(array, 'ctx', [(i, i ^ k) for i in range(peers)])  18.6 us
    pallas_call x1, Pallas kernels, convolve(): pl.pallas_call(functools.partial(conv_kernel, group_size, me_at, peers),...  12.7 us
    ppermute x8, starting transfers between devices, swap_to_previous(): return lax.ppermute(array, ('pipe', 'ctx'), pairs)  11 us
    pallas_call x1, Pallas kernels, multiply(): pl.pallas_call(functools.partial(multiply_kernel, chunks), out_shape=[jax...  4.36 us
    ppermute x1, waiting for transfers between devices, shards(): held.append(lax.ppermute(cross, 'tp', [(0, 1), (1, 0)]))  3.04 us
    pallas_call x1, Pallas kernels, side_of(): pl.pallas_call(side_kernel, out_shape=jax.ShapeDtypeStruct((3, rows, chan...  2.81 us
  transfers between devices with their start and end apart: 17, of which 9 were waited for; matrix products, arithmetic and copies ran while one was open for 1% of the time, Pallas kernels for 15%

profile of v6, /device:TPU:21, one launch (start us, length us, event | category | flops | bytes accessed | tf_op | source)
XLA Modules:
  0.0 130.4 jit_solution(9416969292279615601)
XLA Ops:
  0.0 0.0 copy-start
  0.0 2.8 %side.1 = bf16[3,128,4096]{2,1,0:T(8,128)(2,1)} custom-call(bf16[1,3,128,4096]{3,2,1,0:T(8,128)(2,1)} %proj_ref.3, bf16[1,128,4096]{2,1,0:T(8,128)(2,1)} %grad_ref.3), custom_call_target="tpu_custom_call" | custom-call | bytes 6291456 | tf_op jit(solution)/shard_map/side/pallas_call | solution.py:134
  2.8 1.3 collective-permute-start.7
  4.1 4.4 %multiply.1 = (bf16[1040,128]{1,0:T(8,128)(2,1)}, bf16[1040,128]{1,0:T(8,128)(2,1)}, bf16[1040,128]{1,0:T(8,128)(2,1)}, bf16[1040,128]{1,0:T(8,128)(2,1)}, bf16[...) custom-call(bf16[1,3,128,4096]{3,2,1,0:T(8,128)(2,1)} %proj_ref.3, ...), custom_call_target="tpu_custom_call" | custom-call | flops 1048576 | bytes 6291456 | tf_op jit(solution)/shard_map/multiply/pallas_call | solution.py:88
  8.5 0.0 copy-start.1
  8.5 0.1 collective-permute-start
  8.6 0.2 collective-permute-start.1
  8.9 3.2 %collective-permute-start.2 = (bf16[1040,128]{1,0:T(8,128)(2,1)}, bf16[1040,128]{1,0:T(8,128)(2,1)}, u32[]{:S(2)}, u32[]{:S(2)}) collective-permute-start(bf16[1040,128]{1,0:T(8,128)(2,1)} %get-tuple-element.30), channel_id=1, source_target_pairs={{0,10},{2,8},{4,14},{6,12},{8,2},{10,0},{12,6},{14,4},{1,11},{3,9}... | collective-permute-start | bytes 798728 | tf_op jit(solution)/shard_map/ppermute | solution.py:429
  12.1 1.3 collective-permute-start.3
  13.4 0.7 convert_bitcast_fusion
  14.1 0.1 rev.3
  14.2 0.1 pad_bitcast_fusion
  14.2 11.1 %collective-permute-done.refs_1_ = bf16[1040,128]{1,0:T(8,128)(2,1)} collective-permute-done((bf16[1040,128]{1,0:T(8,128)(2,1)}, bf16[1040,128]{1,0:T(8,128)(2,1)}, u32[]{:S(2)}, u32[]{:S(2)}) %collective-permute-start) | collective-permute-done | bytes 266272 | tf_op jit(solution)/shard_map/ppermute | solution.py:429
  25.4 3.4 %collective-permute-start.4 = (bf16[1040,128]{1,0:T(8,128)(2,1)}, bf16[1040,128]{1,0:T(8,128)(2,1)}, u32[]{:S(2)}, u32[]{:S(2)}) collective-permute-start(bf16[1040,128]{1,0:T(8,128)(2,1)} %get-tuple-element.32), channel_id=1, source_target_pairs={{0,12},{2,14},{4,8},{6,10},{8,4},{10,6},{12,0},{14,2},{1,13},{3,15... | collective-permute-start | bytes 798728 | tf_op jit(solution)/shard_map/ppermute | solution.py:429
  28.8 0.0 collective-permute-done.1.refs_2_
  28.8 1.9 %collective-permute-start.5 = (bf16[1040,128]{1,0:T(8,128)(2,1)}, bf16[1040,128]{1,0:T(8,128)(2,1)}, u32[]{:S(2)}, u32[]{:S(2)}) collective-permute-start(bf16[1040,128]{1,0:T(8,128)(2,1)} %get-tuple-element.33), channel_id=1, source_target_pairs={{0,6},{2,4},{4,2},{6,0},{8,14},{10,12},{12,10},{14,8},{1,7},{3,5},... | collective-permute-start | bytes 798728 | tf_op jit(solution)/shard_map/ppermute | solution.py:429
  30.6 0.5 collective-permute-done.2.refs_3_
  31.1 8.4 %collective-permute-start.6 = (bf16[1040,128]{1,0:T(8,128)(2,1)}, bf16[1040,128]{1,0:T(8,128)(2,1)}, u32[]{:S(2)}, u32[]{:S(2)}) collective-permute-start(bf16[1040,128]{1,0:T(8,128)(2,1)} %get-tuple-element.34), channel_id=1, source_target_pairs={{0,14},{2,12},{4,10},{6,8},{8,6},{10,4},{12,2},{14,0},{1,15},{3,13... | collective-permute-start | bytes 798728 | tf_op jit(solution)/shard_map/ppermute | solution.py:429
  39.5 1.2 toeplitz.1.toep_ref
  40.8 0.1 pad_add_fusion.meta_ref
  40.8 0.0 collective-permute-done.3.refs_4_
  40.8 11.5 %collective-permute-done.4.refs_5_ = bf16[1040,128]{1,0:T(8,128)(2,1)} collective-permute-done((bf16[1040,128]{1,0:T(8,128)(2,1)}, bf16[1040,128]{1,0:T(8,128)(2,1)}, u32[]{:S(2)}, u32[]{:S(2)}) %collective-permute-start.4) | collective-permute-done | bytes 266272 | tf_op jit(solution)/shard_map/ppermute | solution.py:429
  52.4 0.0 collective-permute-done.5.refs_6_
  52.4 5.6 %collective-permute-done.6.refs_7_ = bf16[1040,128]{1,0:T(8,128)(2,1)} collective-permute-done((bf16[1040,128]{1,0:T(8,128)(2,1)}, bf16[1040,128]{1,0:T(8,128)(2,1)}, u32[]{:S(2)}, u32[]{:S(2)}) %collective-permute-start.6) | collective-permute-done | bytes 266272 | tf_op jit(solution)/shard_map/ppermute | solution.py:429
  58.0 0.0 copy-done.1
  58.0 1.5 %masks.1.mask_ref = bf16[8,2,128,256]{3,2,1,0:T(8,128)(2,1)S(1)} custom-call(s32[66]{0:T(128)S(1)} %pad_add_fusion.meta_ref, bf16[1040,128]{1,0:T(8,128)(2,1)S(1)} %copy-done.1, bf16[1040,128]{1,0:T(8,128)(2,1)} %collective-permute-done.refs_1_, bf16[1040,128]{1,0:T(8,128)(2,1)} %collective-permute-done.1.refs_2_, ...), custom_call_target="tpu_custom_call" | custom-call | flops 1048576 | bytes 1048576 | tf_op jit(solution)/shard_map/masks/pallas_call | solution.py:204
  59.5 12.7 %convolve.1 = (bf16[256,512]{1,0:T(8,128)(2,1)S(1)}, bf16[256,512]{1,0:T(8,128)(2,1)S(1)}, bf16[256,512]{1,0:T(8,128)(2,1)S(1)}, bf16[256,512]{1,0:T(8,128)(2,1)...) custom-call(s32[66]{0:T(128)S(1)} %pad_add_fusion.meta_ref, ...), custom_call_target="tpu_custom_call" | custom-call | flops 4294967296 | bytes 4718592 | tf_op jit(solution)/shard_map/convolve/pallas_call | solution.py:314
  72.2 1.3 collective-permute-start.10
  73.4 0.0 collective-permute-start.11
  73.4 1.3 %collective-permute-start.12 = (bf16[256,512]{1,0:T(8,128)(2,1)S(1)}, bf16[256,512]{1,0:T(8,128)(2,1)S(1)}, u32[]{:S(2)}, u32[]{:S(2)}) collective-permute-start(bf16[256,512]{1,0:T(8,128)(2,1)S(1)} %get-tuple-element.43), channel_id=1, source_target_pairs={{0,20},{2,22},{4,16},{6,18},{8,28},{10,30},{12,24},{14,26},{16,4},... | collective-permute-start | bytes 786440 | tf_op jit(solution)/shard_map/ppermute | solution.py:440
  74.8 1.2 collective-permute-start.8
  76.0 0.0 collective-permute-done.7.side_ref
  76.0 1.9 %collective-permute-start.9 = (bf16[256,512]{1,0:T(8,128)(2,1)S(1)}, bf16[256,512]{1,0:T(8,128)(2,1)S(1)}, u32[]{:S(2)}, u32[]{:S(2)}) collective-permute-start(bf16[256,512]{1,0:T(8,128)(2,1)S(1)} %get-tuple-element.40), channel_id=1, source_target_pairs={{0,24},{2,26},{4,28},{6,30},{8,16},{10,18},{12,20},{14,22},{16,8},... | collective-permute-start | bytes 786440 | tf_op jit(solution)/shard_map/ppermute | solution.py:440
  77.9 17.6 %collective-permute-done.10.refs_2_ = bf16[256,512]{1,0:T(8,128)(2,1)S(1)} collective-permute-done((bf16[256,512]{1,0:T(8,128)(2,1)S(1)}, bf16[256,512]{1,0:T(8,128)(2,1)S(1)}, u32[]{:S(2)}, u32[]{:S(2)}) %collective-permute-start.10) | collective-permute-done | bytes 262176 | tf_op jit(solution)/shard_map/ppermute | solution.py:440
  95.5 0.0 collective-permute-start.13
  95.5 0.0 collective-permute-done.11.refs_3_
  95.5 0.0 collective-permute-start.14
  95.5 0.0 collective-permute-done.12.refs_4_
  95.5 5.3 %collective-permute-start.15 = (bf16[256,512]{1,0:T(8,128)(2,1)S(1)}, bf16[256,512]{1,0:T(8,128)(2,1)S(1)}, u32[]{:S(2)}, u32[]{:S(2)}) collective-permute-start(bf16[256,512]{1,0:T(8,128)(2,1)S(1)} %get-tuple-element.46), channel_id=1, source_target_pairs={{0,30},{2,28},{4,26},{6,24},{8,22},{10,20},{12,18},{14,16},{16,14}... | collective-permute-start | bytes 786440 | tf_op jit(solution)/shard_map/ppermute | solution.py:440
  100.8 12.7 %collective-permute-done.8.refs_0_ = bf16[256,512]{1,0:T(8,128)(2,1)S(1)} collective-permute-done((bf16[256,512]{1,0:T(8,128)(2,1)S(1)}, bf16[256,512]{1,0:T(8,128)(2,1)S(1)}, u32[]{:S(2)}, u32[]{:S(2)}) %collective-permute-start.8) | collective-permute-done | bytes 262176 | tf_op jit(solution)/shard_map/ppermute | solution.py:440
  113.5 0.0 collective-permute-done.9.refs_1_
  113.5 1.5 %collective-permute-done.13.refs_5_ = bf16[256,512]{1,0:T(8,128)(2,1)S(1)} collective-permute-done((bf16[256,512]{1,0:T(8,128)(2,1)S(1)}, bf16[256,512]{1,0:T(8,128)(2,1)S(1)}, u32[]{:S(2)}, u32[]{:S(2)}) %collective-permute-start.13) | collective-permute-done | bytes 262176 | tf_op jit(solution)/shard_map/ppermute | solution.py:440
  115.0 0.0 collective-permute-done.14.refs_6_
  115.0 6.3 %collective-permute-done.15.refs_7_ = bf16[256,512]{1,0:T(8,128)(2,1)S(1)} collective-permute-done((bf16[256,512]{1,0:T(8,128)(2,1)S(1)}, bf16[256,512]{1,0:T(8,128)(2,1)S(1)}, u32[]{:S(2)}, u32[]{:S(2)}) %collective-permute-start.15) | collective-permute-done | bytes 262176 | tf_op jit(solution)/shard_map/ppermute | solution.py:440
  121.4 2.3 %gradients.1 = (bf16[1,3,64,8192]{3,2,1,0:T(8,128)(2,1)}, bf16[3,64,4096]{2,1,0:T(8,128)(2,1)S(1)}) custom-call(s32[66]{0:T(128)S(1)} %pad_add_fusion.meta_ref, bf16[3,128,4096]{2,1,0:T(8,128)(2,1)S(1)} %collective-permute-done.7.side_ref, bf16[256,512]{1,0:T(8,128)(2,1)S(1)} %collective-permute-done.8.refs_0_, ...), custom_call_target="tpu_custom_call" | custom-call | flops 1572864 | bytes 8388608 | tf_op jit(solution)/shard_map/gradients/pallas_call | solution.py:386
  123.7 1.9 %collective-permute-start.16 = (bf16[3,64,4096]{2,1,0:T(8,128)(2,1)S(1)}, bf16[3,64,4096]{2,1,0:T(8,128)(2,1)S(1)}, u32[]{:S(2)}, u32[]{:S(2)}) collective-permute-start(bf16[3,64,4096]{2,1,0:T(8,128)(2,1)S(1)} %get-tuple-element.47), channel_id=1, source_target_pairs={{0,1},{1,0},{2,3},{3,2},{4,5},{5,4},{6,7},{7,6},{8,9},{9,8},{10,11... | collective-permute-start | bytes 4718600 | tf_op jit(solution)/shard_map/ppermute | solution.py:504
  125.6 3.0 %collective-permute-done.16.cross_ref = bf16[3,64,4096]{2,1,0:T(8,128)(2,1)S(1)} collective-permute-done((bf16[3,64,4096]{2,1,0:T(8,128)(2,1)S(1)}, bf16[3,64,4096]{2,1,0:T(8,128)(2,1)S(1)}, u32[]{:S(2)}, u32[]{:S(2)}) %collective-permute-start.16) | collective-permute-done | bytes 1572896 | tf_op jit(solution)/shard_map/ppermute | solution.py:504
  128.6 1.8 %place.1 = bf16[1,3,64,8192]{3,2,1,0:T(8,128)(2,1)} custom-call(s32[66]{0:T(128)S(1)} %pad_add_fusion.meta_ref, bf16[3,64,4096]{2,1,0:T(8,128)(2,1)S(1)} %collective-permute-done.16.cross_ref, bf16[1,3,64,8192]{3,2,1,0:T(8,128)(2,1)} %get-tuple-element.48.held_ref), custom_call_target="tpu_custom_call", output_to_operand_aliasing={{}: (2, {})} | custom-call | bytes 3145728 | tf_op jit(solution)/shard_map/place/pallas_call | solution.py:409
  (3 shorter events, 0.0 us)
Async XLA Ops:
  0.0 40.7 %copy-start = (s32[2,64]{1,0:T(2,128)S(1)}, s32[2,64]{1,0:T(2,128)}, u32[]{:S(2)}) copy-start(s32[2,64]{1,0:T(2,128)} %param.7) | copy-start | bytes 1540
  2.8 73.2 %collective-permute-start.7 = (bf16[3,128,4096]{2,1,0:T(8,128)(2,1)}, bf16[3,128,4096]{2,1,0:T(8,128)(2,1)S(1)}, u32[]{:S(2)}, u32[]{:S(2)}) collective-permute-start(bf16[3,128,4096]{2,1,0:T(8,128)(2,1)} %side.1), channel_id=1, source_target_pairs={{0,16},{16,0},{1,17},{17,1},{2,18},{18,2},{3,19},{19,3},{4,20},{20... | collective-permute-start | bytes 9437192 | tf_op jit(solution)/shard_map/ppermute | solution.py:476
  8.5 49.5 %copy-start.1 = (bf16[1040,128]{1,0:T(8,128)(2,1)S(1)}, bf16[1040,128]{1,0:T(8,128)(2,1)}, u32[]{:S(2)}) copy-start(bf16[1040,128]{1,0:T(8,128)(2,1)} %get-tuple-element.27.refs_0_) | copy-start | bytes 798724
  8.5 16.9 %collective-permute-start = (bf16[1040,128]{1,0:T(8,128)(2,1)}, bf16[1040,128]{1,0:T(8,128)(2,1)}, u32[]{:S(2)}, u32[]{:S(2)}) collective-permute-start(bf16[1040,128]{1,0:T(8,128)(2,1)} %get-tuple-element.28), channel_id=1, source_target_pairs={{0,8},{2,10},{4,12},{6,14},{8,0},{10,2},{12,4},{14,6},{1,9},{3,11}... | collective-permute-start | bytes 798728 | tf_op jit(solution)/shard_map/ppermute | solution.py:429
  8.6 20.2 %collective-permute-start.1 = (bf16[1040,128]{1,0:T(8,128)(2,1)}, bf16[1040,128]{1,0:T(8,128)(2,1)}, u32[]{:S(2)}, u32[]{:S(2)}) collective-permute-start(bf16[1040,128]{1,0:T(8,128)(2,1)} %get-tuple-element.29), channel_id=1, source_target_pairs={{0,2},{2,0},{4,6},{6,4},{8,10},{10,8},{12,14},{14,12},{1,3},{3,1},... | collective-permute-start | bytes 798728 | tf_op jit(solution)/shard_map/ppermute | solution.py:429
  8.9 22.2 %collective-permute-start.2 = (bf16[1040,128]{1,0:T(8,128)(2,1)}, bf16[1040,128]{1,0:T(8,128)(2,1)}, u32[]{:S(2)}, u32[]{:S(2)}) collective-permute-start(bf16[1040,128]{1,0:T(8,128)(2,1)} %get-tuple-element.30), channel_id=1, source_target_pairs={{0,10},{2,8},{4,14},{6,12},{8,2},{10,0},{12,6},{14,4},{1,11},{3,9}... | collective-permute-start | bytes 798728 | tf_op jit(solution)/shard_map/ppermute | solution.py:429
  12.1 28.8 %collective-permute-start.3 = (bf16[1040,128]{1,0:T(8,128)(2,1)}, bf16[1040,128]{1,0:T(8,128)(2,1)}, u32[]{:S(2)}, u32[]{:S(2)}) collective-permute-start(bf16[1040,128]{1,0:T(8,128)(2,1)} %get-tuple-element.31), channel_id=1, source_target_pairs={{0,4},{2,6},{4,0},{6,2},{8,12},{10,14},{12,8},{14,10},{1,5},{3,7},... | collective-permute-start | bytes 798728 | tf_op jit(solution)/shard_map/ppermute | solution.py:429
  25.4 27.0 %collective-permute-start.4 = (bf16[1040,128]{1,0:T(8,128)(2,1)}, bf16[1040,128]{1,0:T(8,128)(2,1)}, u32[]{:S(2)}, u32[]{:S(2)}) collective-permute-start(bf16[1040,128]{1,0:T(8,128)(2,1)} %get-tuple-element.32), channel_id=1, source_target_pairs={{0,12},{2,14},{4,8},{6,10},{8,4},{10,6},{12,0},{14,2},{1,13},{3,15... | collective-permute-start | bytes 798728 | tf_op jit(solution)/shard_map/ppermute | solution.py:429
  28.8 23.6 %collective-permute-start.5 = (bf16[1040,128]{1,0:T(8,128)(2,1)}, bf16[1040,128]{1,0:T(8,128)(2,1)}, u32[]{:S(2)}, u32[]{:S(2)}) collective-permute-start(bf16[1040,128]{1,0:T(8,128)(2,1)} %get-tuple-element.33), channel_id=1, source_target_pairs={{0,6},{2,4},{4,2},{6,0},{8,14},{10,12},{12,10},{14,8},{1,7},{3,5},... | collective-permute-start | bytes 798728 | tf_op jit(solution)/shard_map/ppermute | solution.py:429
  31.1 26.9 %collective-permute-start.6 = (bf16[1040,128]{1,0:T(8,128)(2,1)}, bf16[1040,128]{1,0:T(8,128)(2,1)}, u32[]{:S(2)}, u32[]{:S(2)}) collective-permute-start(bf16[1040,128]{1,0:T(8,128)(2,1)} %get-tuple-element.34), channel_id=1, source_target_pairs={{0,14},{2,12},{4,10},{6,8},{8,6},{10,4},{12,2},{14,0},{1,15},{3,13... | collective-permute-start | bytes 798728 | tf_op jit(solution)/shard_map/ppermute | solution.py:429
  72.2 23.3 %collective-permute-start.10 = (bf16[256,512]{1,0:T(8,128)(2,1)S(1)}, bf16[256,512]{1,0:T(8,128)(2,1)S(1)}, u32[]{:S(2)}, u32[]{:S(2)}) collective-permute-start(bf16[256,512]{1,0:T(8,128)(2,1)S(1)} %get-tuple-element.41), channel_id=1, source_target_pairs={{0,18},{2,16},{4,22},{6,20},{8,26},{10,24},{12,30},{14,28},{16,2},... | collective-permute-start | bytes 786440 | tf_op jit(solution)/shard_map/ppermute | solution.py:440
  73.4 22.0 %collective-permute-start.11 = (bf16[256,512]{1,0:T(8,128)(2,1)S(1)}, bf16[256,512]{1,0:T(8,128)(2,1)S(1)}, u32[]{:S(2)}, u32[]{:S(2)}) collective-permute-start(bf16[256,512]{1,0:T(8,128)(2,1)S(1)} %get-tuple-element.42), channel_id=1, source_target_pairs={{0,26},{2,24},{4,30},{6,28},{8,18},{10,16},{12,22},{14,20},{16,10}... | collective-permute-start | bytes 786440 | tf_op jit(solution)/shard_map/ppermute | solution.py:440
  73.4 22.0 %collective-permute-start.12 = (bf16[256,512]{1,0:T(8,128)(2,1)S(1)}, bf16[256,512]{1,0:T(8,128)(2,1)S(1)}, u32[]{:S(2)}, u32[]{:S(2)}) collective-permute-start(bf16[256,512]{1,0:T(8,128)(2,1)S(1)} %get-tuple-element.43), channel_id=1, source_target_pairs={{0,20},{2,22},{4,16},{6,18},{8,28},{10,30},{12,24},{14,26},{16,4},... | collective-permute-start | bytes 786440 | tf_op jit(solution)/shard_map/ppermute | solution.py:440
  74.8 38.7 %collective-permute-start.8 = (bf16[256,512]{1,0:T(8,128)(2,1)S(1)}, bf16[256,512]{1,0:T(8,128)(2,1)S(1)}, u32[]{:S(2)}, u32[]{:S(2)}) collective-permute-start(bf16[256,512]{1,0:T(8,128)(2,1)S(1)} %get-tuple-element.39), channel_id=1, source_target_pairs={{0,16},{2,18},{4,20},{6,22},{8,24},{10,26},{12,28},{14,30},{16,0},... | collective-permute-start | bytes 786440 | tf_op jit(solution)/shard_map/ppermute | solution.py:440
  76.0 37.5 %collective-permute-start.9 = (bf16[256,512]{1,0:T(8,128)(2,1)S(1)}, bf16[256,512]{1,0:T(8,128)(2,1)S(1)}, u32[]{:S(2)}, u32[]{:S(2)}) collective-permute-start(bf16[256,512]{1,0:T(8,128)(2,1)S(1)} %get-tuple-element.40), channel_id=1, source_target_pairs={{0,24},{2,26},{4,28},{6,30},{8,16},{10,18},{12,20},{14,22},{16,8},... | collective-permute-start | bytes 786440 | tf_op jit(solution)/shard_map/ppermute | solution.py:440
  95.5 19.6 %collective-permute-start.13 = (bf16[256,512]{1,0:T(8,128)(2,1)S(1)}, bf16[256,512]{1,0:T(8,128)(2,1)S(1)}, u32[]{:S(2)}, u32[]{:S(2)}) collective-permute-start(bf16[256,512]{1,0:T(8,128)(2,1)S(1)} %get-tuple-element.44), channel_id=1, source_target_pairs={{0,28},{2,30},{4,24},{6,26},{8,20},{10,22},{12,16},{14,18},{16,12}... | collective-permute-start | bytes 786440 | tf_op jit(solution)/shard_map/ppermute | solution.py:440
  95.5 19.6 %collective-permute-start.14 = (bf16[256,512]{1,0:T(8,128)(2,1)S(1)}, bf16[256,512]{1,0:T(8,128)(2,1)S(1)}, u32[]{:S(2)}, u32[]{:S(2)}) collective-permute-start(bf16[256,512]{1,0:T(8,128)(2,1)S(1)} %get-tuple-element.45), channel_id=1, source_target_pairs={{0,22},{2,20},{4,18},{6,16},{8,30},{10,28},{12,26},{14,24},{16,6},... | collective-permute-start | bytes 786440 | tf_op jit(solution)/shard_map/ppermute | solution.py:440
  95.5 25.9 %collective-permute-start.15 = (bf16[256,512]{1,0:T(8,128)(2,1)S(1)}, bf16[256,512]{1,0:T(8,128)(2,1)S(1)}, u32[]{:S(2)}, u32[]{:S(2)}) collective-permute-start(bf16[256,512]{1,0:T(8,128)(2,1)S(1)} %get-tuple-element.46), channel_id=1, source_target_pairs={{0,30},{2,28},{4,26},{6,24},{8,22},{10,20},{12,18},{14,16},{16,14}... | collective-permute-start | bytes 786440 | tf_op jit(solution)/shard_map/ppermute | solution.py:440
  123.7 5.0 %collective-permute-start.16 = (bf16[3,64,4096]{2,1,0:T(8,128)(2,1)S(1)}, bf16[3,64,4096]{2,1,0:T(8,128)(2,1)S(1)}, u32[]{:S(2)}, u32[]{:S(2)}) collective-permute-start(bf16[3,64,4096]{2,1,0:T(8,128)(2,1)S(1)} %get-tuple-element.47), channel_id=1, source_target_pairs={{0,1},{1,0},{2,3},{3,2},{4,5},{5,4},{6,7},{7,6},{8,9},{9,8},{10,11... | collective-permute-start | bytes 4718600 | tf_op jit(solution)/shard_map/ppermute | solution.py:504

commit v7 on v6

--- a/solution.py
+++ b/solution.py
@@ -105,7 +105,7 @@
     return [list(made[c * peers : (c + 1) * peers]) for c in range(chunks)]
 
 
-def side_kernel(proj_ref, grad_ref, side_ref, arrived, in_sems, out_sems):
+def side_kernel(proj_ref, grad_ref, side_ref, copy_ref, arrived, in_sems, out_sems):
     sources = (proj_ref.at[0, 1], proj_ref.at[0, 2], grad_ref.at[0])
     rows = grad_ref.shape[1]
     parts = in_sems.shape[1]
@@ -116,9 +116,8 @@
             loads.append(
                 pltpu.make_async_copy(source.at[at], arrived.at[i, at], in_sems.at[i, part])
             )
-            stores.append(
-                pltpu.make_async_copy(arrived.at[i, at], side_ref.at[i, at], out_sems.at[i, part])
-            )
+            target = copy_ref.at[0, at] if i == 2 else side_ref.at[i, at]
+            stores.append(pltpu.make_async_copy(arrived.at[i, at], target, out_sems.at[i, part]))
     for load in loads:
         load.start()
     for load, store in zip(loads, stores):
@@ -133,9 +132,9 @@
     anywhere = pl.BlockSpec(memory_space=pl.ANY)
     return pl.pallas_call(
         side_kernel,
-        out_shape=jax.ShapeDtypeStruct((3, rows, channels), BF16),
+        out_shape=[jax.ShapeDtypeStruct((n, rows, channels), BF16) for n in (2, 1)],
         in_specs=[anywhere, anywhere],
-        out_specs=anywhere,
+        out_specs=[anywhere] * 2,
         scratch_shapes=[
             pltpu.VMEM((3, rows, channels), BF16),
             pltpu.SemaphoreType.DMA((3, 2)),
@@ -335,7 +334,7 @@
     return list(outs)
 
 
-def gradients_kernel(me_at, tp_at, peers, meta_ref, side_ref, *refs):
+def gradients_kernel(me_at, tp_at, peers, meta_ref, side_ref, grad_ref, *refs):
     result_ref, cross_ref = refs[-2:]
     rows = side_ref.shape[1]
     width = side_ref.shape[2] // peers
@@ -352,7 +351,7 @@
             mixed_grad = back_ref[later, :].astype(F32)
             key_rows = side_ref[0, at, lanes].astype(F32)
             value = side_ref[1, at, lanes].astype(F32)
-            grad_in = side_ref[2, at, lanes].astype(F32)
+            grad_in = grad_ref[0, at, lanes].astype(F32)
             out_ref[0, :, lanes] = (grad_in * medium).astype(BF16)
             out_ref[1, :, lanes] = (mixed_grad * value).astype(BF16)
             out_ref[2, :, lanes] = (mixed_grad * key_rows).astype(BF16)
@@ -370,15 +369,18 @@
     return pl.BlockSpec((1,) + shape, place)
 
 
-def gradients(chunk, chunks, me_at, tp_at, tp_count, meta, backs, side, others):
+def gradients(chunk, chunks, me_at, tp_at, tp_count, meta, backs, side, grad_in, others):
     peers = len(backs)
     _, rows, channels = side.shape
     span = channels // chunks
     out = (3, rows // tp_count, span)
     whole = (1, 3, rows // tp_count, channels * tp_count)
-    in_specs = [pl.BlockSpec((3, rows, span), lambda _, meta_ref: (0, 0, chunk))]
+    in_specs = [
+        pl.BlockSpec((2, rows, span), lambda _, meta_ref: (0, 0, chunk)),
+        pl.BlockSpec((1, rows, span), lambda _, meta_ref: (0, 0, chunk)),
+    ]
     in_specs += [fixed(backs[0].shape)] * peers
-    args = [meta, side, *backs]
+    args = [meta, side, grad_in, *backs]
     aliases = {} if chunk == 0 else {len(args): 0}
     for other in others:
         args.append(other)
@@ -473,7 +475,9 @@
     products = multiply(chunks, width, peers, qkv_proj, cotangent, doc_start)
     toeplitz = [toeplitz_of(bases[chunk]) for chunk in range(chunks)]
     received = [swap(array, k) for array, k in zip(products[0], order)]
-    side = lax.ppermute(side_of(qkv_proj, cotangent), "pipe", to_previous)
+    side, grad_in = [
+        lax.ppermute(array, "pipe", to_previous) for array in side_of(qkv_proj, cotangent)
+    ]
 
     first_out, first_back = OUT_FIRST * peers // 8, BACK_FIRST * peers // 8
     masks = document_masks(me_at, meta, received, MARK_ROWS)
@@ -490,7 +494,7 @@
         if coming:
             late = convolved[first_back:]
         else:
-            last, side = lax.optimization_barrier((convolved[first_back:], side))
+            last, side, grad_in = lax.optimization_barrier((convolved[first_back:], side, grad_in))
             convolved = convolved[:first_back] + last
         now = first_back if coming else peers
         backs.append([swap_to_previous(array, k) for array, k in zip(convolved[:now], order)])
@@ -499,7 +503,7 @@
     for chunk in range(chunks):
         others = [result] if chunk else [array for back in backs[1:] for array in back]
         result, cross = gradients(
-            chunk, chunks, me_at, tp_at, tp_count, meta, backs[chunk], side, others
+            chunk, chunks, me_at, tp_at, tp_count, meta, backs[chunk], side, grad_in, others
         )
         held.append(lax.ppermute(cross, "tp", [(0, 1), (1, 0)]))
     for chunk in range(chunks):

time: 131 us -> 132 us (level); the launches traced: 130 us -> 129 us
  waiting for transfers between devices: 70 us -> 67.7 us
    ppermute x8, waiting for transfers between devices: 38.2 us -> 32.9 us  [swap_to_previous(): return lax.ppermute(array, ('pipe', 'ctx'), pairs)]
    ppermute x7, starting transfers between devices: 18.6 us -> 14.5 us  [swap(): lax.ppermute(array, 'ctx', [(i, i ^ k) for i in range(peers)])]
    ppermute x7, waiting for transfers between devices: 28.7 us -> 31.8 us  [swap(): lax.ppermute(array, 'ctx', [(i, i ^ k) for i in range(peers)])]
    ppermute x8, starting transfers between devices: 11 us -> 13.5 us  [swap_to_previous(): return lax.ppermute(array, ('pipe', 'ctx'), pairs)]
    ppermute x1, starting transfers between devices: 1.93 us -> 3.57 us  [shards(): held.append(lax.ppermute(cross, 'tp', [(0, 1), (1, 0)]))]
  transfers between devices with their start and end apart: 17 -> 18, of which waited for: 9 -> 8; matrix products, arithmetic and copies ran while one was open for 1% -> 1% of each run, Pallas kernels for 15% -> 15%
where the time goes in v7:
time: 132 us; the launch traced here: 129 us
  waiting for transfers between devices  67.7 us (51%)
  starting transfers between devices  33.1 us (25%)
  Pallas kernels  26.5 us (20%)
    ppermute x8, waiting for transfers between devices, swap_to_previous(): return lax.ppermute(array, ('pipe', 'ctx'), pairs)  32.9 us
    ppermute x7, waiting for transfers between devices, swap(): lax.ppermute(array, 'ctx', [(i, i ^ k) for i in range(peers)])  31.8 us
    ppermute x7, starting transfers between devices, swap(): lax.ppermute(array, 'ctx', [(i, i ^ k) for i in range(peers)])  14.5 us
    ppermute x8, starting transfers between devices, swap_to_previous(): return lax.ppermute(array, ('pipe', 'ctx'), pairs)  13.5 us
    pallas_call x1, Pallas kernels, convolve(): pl.pallas_call(functools.partial(conv_kernel, group_size, me_at, peers),...  12.5 us
    pallas_call x1, Pallas kernels, multiply(): pl.pallas_call(functools.partial(multiply_kernel, chunks), out_shape=[jax...  4.36 us
    ppermute x1, starting transfers between devices, shards(): held.append(lax.ppermute(cross, 'tp', [(0, 1), (1, 0)]))  3.57 us
    ppermute x1, waiting for transfers between devices, shards(): held.append(lax.ppermute(cross, 'tp', [(0, 1), (1, 0)]))  3.04 us
  transfers between devices with their start and end apart: 18, of which 8 were waited for; matrix products, arithmetic and copies ran while one was open for 1% of the time, Pallas kernels for 15%

profile of v7, /device:TPU:21, one launch (start us, length us, event | category | flops | bytes accessed | tf_op | source)
XLA Modules:
  0.0 129.2 jit_solution(721472428229734392)
XLA Ops:
  0.0 2.8 %side.1 = (bf16[2,128,4096]{2,1,0:T(8,128)(2,1)}, bf16[1,128,4096]{2,1,0:T(8,128)(2,1)}) custom-call(bf16[1,3,128,4096]{3,2,1,0:T(8,128)(2,1)} %proj_ref.3, bf16[1,128,4096]{2,1,0:T(8,128)(2,1)} %grad_ref.3), custom_call_target="tpu_custom_call" | custom-call | bytes 6291456 | tf_op jit(solution)/shard_map/side/pallas_call | solution.py:133
  2.8 1.3 collective-permute-start.7
  4.1 4.4 %multiply.1 = (bf16[1040,128]{1,0:T(8,128)(2,1)}, bf16[1040,128]{1,0:T(8,128)(2,1)}, bf16[1040,128]{1,0:T(8,128)(2,1)}, bf16[1040,128]{1,0:T(8,128)(2,1)}, bf16[...) custom-call(bf16[1,3,128,4096]{3,2,1,0:T(8,128)(2,1)} %proj_ref.3, ...), custom_call_target="tpu_custom_call" | custom-call | flops 1048576 | bytes 6291456 | tf_op jit(solution)/shard_map/multiply/pallas_call | solution.py:88
  8.5 0.1 collective-permute-start
  8.6 0.2 collective-permute-start.1
  8.9 3.2 %collective-permute-start.2 = (bf16[1040,128]{1,0:T(8,128)(2,1)}, bf16[1040,128]{1,0:T(8,128)(2,1)}, u32[]{:S(2)}, u32[]{:S(2)}) collective-permute-start(bf16[1040,128]{1,0:T(8,128)(2,1)} %get-tuple-element.33), channel_id=1, source_target_pairs={{0,10},{2,8},{4,14},{6,12},{8,2},{10,0},{12,6},{14,4},{1,11},{3,9}... | collective-permute-start | bytes 798728 | tf_op jit(solution)/shard_map/ppermute | solution.py:431
  12.1 1.3 %collective-permute-start.3 = (bf16[1040,128]{1,0:T(8,128)(2,1)}, bf16[1040,128]{1,0:T(8,128)(2,1)}, u32[]{:S(2)}, u32[]{:S(2)}) collective-permute-start(bf16[1040,128]{1,0:T(8,128)(2,1)} %get-tuple-element.34), channel_id=1, source_target_pairs={{0,4},{2,6},{4,0},{6,2},{8,12},{10,14},{12,8},{14,10},{1,5},{3,7},... | collective-permute-start | bytes 798728 | tf_op jit(solution)/shard_map/ppermute | solution.py:431
  13.4 0.7 convert_bitcast_fusion
  14.1 0.1 rev.3
  14.2 11.2 %collective-permute-done.refs_1_ = bf16[1040,128]{1,0:T(8,128)(2,1)S(1)} collective-permute-done((bf16[1040,128]{1,0:T(8,128)(2,1)}, bf16[1040,128]{1,0:T(8,128)(2,1)S(1)}, u32[]{:S(2)}, u32[]{:S(2)}) %collective-permute-start) | collective-permute-done | bytes 266272 | tf_op jit(solution)/shard_map/ppermute | solution.py:431
  25.4 0.7 copy-done.2
  26.1 0.3 collective-permute-start.8
  26.3 0.1 pad_bitcast_fusion
  26.4 0.0 collective-permute-done.1.refs_2_
  26.4 3.4 %collective-permute-start.4 = (bf16[1040,128]{1,0:T(8,128)(2,1)}, bf16[1040,128]{1,0:T(8,128)(2,1)}, u32[]{:S(2)}, u32[]{:S(2)}) collective-permute-start(bf16[1040,128]{1,0:T(8,128)(2,1)} %get-tuple-element.35), channel_id=1, source_target_pairs={{0,12},{2,14},{4,8},{6,10},{8,4},{10,6},{12,0},{14,2},{1,13},{3,15... | collective-permute-start | bytes 798728 | tf_op jit(solution)/shard_map/ppermute | solution.py:431
  29.8 1.3 collective-permute-done.2.refs_3_
  31.1 6.2 %collective-permute-start.5 = (bf16[1040,128]{1,0:T(8,128)(2,1)}, bf16[1040,128]{1,0:T(8,128)(2,1)}, u32[]{:S(2)}, u32[]{:S(2)}) collective-permute-start(bf16[1040,128]{1,0:T(8,128)(2,1)} %get-tuple-element.36), channel_id=1, source_target_pairs={{0,6},{2,4},{4,2},{6,0},{8,14},{10,12},{12,10},{14,8},{1,7},{3,5},... | collective-permute-start | bytes 798728 | tf_op jit(solution)/shard_map/ppermute | solution.py:431
  37.3 0.0 collective-permute-done.3.refs_4_
  37.3 0.0 collective-permute-start.6
  37.3 1.3 toeplitz.1.toep_ref
  38.6 0.1 pad_add_fusion.meta_ref
  38.7 10.8 %collective-permute-done.4.refs_5_ = bf16[1040,128]{1,0:T(8,128)(2,1)} collective-permute-done((bf16[1040,128]{1,0:T(8,128)(2,1)}, bf16[1040,128]{1,0:T(8,128)(2,1)}, u32[]{:S(2)}, u32[]{:S(2)}) %collective-permute-start.4) | collective-permute-done | bytes 266272 | tf_op jit(solution)/shard_map/ppermute | solution.py:431
  49.5 0.0 collective-permute-done.5.refs_6_
  49.5 8.5 %collective-permute-done.6.refs_7_ = bf16[1040,128]{1,0:T(8,128)(2,1)} collective-permute-done((bf16[1040,128]{1,0:T(8,128)(2,1)}, bf16[1040,128]{1,0:T(8,128)(2,1)}, u32[]{:S(2)}, u32[]{:S(2)}) %collective-permute-start.6) | collective-permute-done | bytes 266272 | tf_op jit(solution)/shard_map/ppermute | solution.py:431
  58.0 1.4 %masks.1.mask_ref = bf16[8,2,128,256]{3,2,1,0:T(8,128)(2,1)S(1)} custom-call(s32[66]{0:T(128)S(1)} %pad_add_fusion.meta_ref, bf16[1040,128]{1,0:T(8,128)(2,1)S(1)} %copy-done.1, bf16[1040,128]{1,0:T(8,128)(2,1)S(1)} %copy-done.3, bf16[1040,128]{1,0:T(8,128)(2,1)} %collective-permute-done.1.refs_2_, bf16[1040,128]{1,0:T(8,128)(2,1)} %collective-permute-done.2.refs_3_, ...), custom_call_target="tpu_custom_call" | custom-call | flops 1048576 | bytes 1048576 | tf_op jit(solution)/shard_map/masks/pallas_call | solution.py:203
  59.4 12.5 %convolve.1 = (bf16[256,512]{1,0:T(8,128)(2,1)S(1)}, bf16[256,512]{1,0:T(8,128)(2,1)S(1)}, bf16[256,512]{1,0:T(8,128)(2,1)S(1)}, bf16[256,512]{1,0:T(8,128)(2,1)...) custom-call(s32[66]{0:T(128)S(1)} %pad_add_fusion.meta_ref, ...), custom_call_target="tpu_custom_call" | custom-call | flops 4294967296 | bytes 4718592 | tf_op jit(solution)/shard_map/convolve/pallas_call | solution.py:313
  71.9 0.1 collective-permute-start.10
  72.0 1.3 collective-permute-start.11
  73.3 3.1 %collective-permute-start.12 = (bf16[256,512]{1,0:T(8,128)(2,1)S(1)}, bf16[256,512]{1,0:T(8,128)(2,1)S(1)}, u32[]{:S(2)}, u32[]{:S(2)}) collective-permute-start(bf16[256,512]{1,0:T(8,128)(2,1)S(1)} %get-tuple-element.48), channel_id=1, source_target_pairs={{0,26},{2,24},{4,30},{6,28},{8,18},{10,16},{12,22},{14,20},{16,10}... | collective-permute-start | bytes 786440 | tf_op jit(solution)/shard_map/ppermute | solution.py:442
  76.4 0.0 collective-permute-done.8.grad_ref
  76.4 0.0 collective-permute-start.13
  76.4 0.0 collective-permute-done.7.side_ref
  76.4 1.3 collective-permute-start.9
  77.7 11.4 %collective-permute-done.10.refs_1_ = bf16[256,512]{1,0:T(8,128)(2,1)S(1)} collective-permute-done((bf16[256,512]{1,0:T(8,128)(2,1)S(1)}, bf16[256,512]{1,0:T(8,128)(2,1)S(1)}, u32[]{:S(2)}, u32[]{:S(2)}) %collective-permute-start.10) | collective-permute-done | bytes 262176 | tf_op jit(solution)/shard_map/ppermute | solution.py:442
  89.1 0.0 collective-permute-start.14
  89.1 8.6 %collective-permute-done.11.refs_2_ = bf16[256,512]{1,0:T(8,128)(2,1)S(1)} collective-permute-done((bf16[256,512]{1,0:T(8,128)(2,1)S(1)}, bf16[256,512]{1,0:T(8,128)(2,1)S(1)}, u32[]{:S(2)}, u32[]{:S(2)}) %collective-permute-start.11) | collective-permute-done | bytes 262176 | tf_op jit(solution)/shard_map/ppermute | solution.py:442
  97.7 5.7 %collective-permute-start.15 = (bf16[256,512]{1,0:T(8,128)(2,1)S(1)}, bf16[256,512]{1,0:T(8,128)(2,1)S(1)}, u32[]{:S(2)}, u32[]{:S(2)}) collective-permute-start(bf16[256,512]{1,0:T(8,128)(2,1)S(1)} %get-tuple-element.51), channel_id=1, source_target_pairs={{0,22},{2,20},{4,18},{6,16},{8,30},{10,28},{12,26},{14,24},{16,6},... | collective-permute-start | bytes 786440 | tf_op jit(solution)/shard_map/ppermute | solution.py:442
  103.4 0.0 collective-permute-done.12.refs_3_
  103.4 2.1 %collective-permute-start.16 = (bf16[256,512]{1,0:T(8,128)(2,1)S(1)}, bf16[256,512]{1,0:T(8,128)(2,1)S(1)}, u32[]{:S(2)}, u32[]{:S(2)}) collective-permute-start(bf16[256,512]{1,0:T(8,128)(2,1)S(1)} %get-tuple-element.52), channel_id=1, source_target_pairs={{0,30},{2,28},{4,26},{6,24},{8,22},{10,20},{12,18},{14,16},{16,14}... | collective-permute-start | bytes 786440 | tf_op jit(solution)/shard_map/ppermute | solution.py:442
  105.5 0.0 collective-permute-done.13.refs_4_
  105.5 12.9 %collective-permute-done.9.refs_0_ = bf16[256,512]{1,0:T(8,128)(2,1)S(1)} collective-permute-done((bf16[256,512]{1,0:T(8,128)(2,1)S(1)}, bf16[256,512]{1,0:T(8,128)(2,1)S(1)}, u32[]{:S(2)}, u32[]{:S(2)}) %collective-permute-start.9) | collective-permute-done | bytes 262176 | tf_op jit(solution)/shard_map/ppermute | solution.py:442
  118.4 0.0 collective-permute-done.14.refs_5_
  118.4 0.0 collective-permute-done.15.refs_6_
  118.4 0.0 collective-permute-done.16.refs_7_
  118.4 2.4 %gradients.1 = (bf16[1,3,64,8192]{3,2,1,0:T(8,128)(2,1)}, bf16[3,64,4096]{2,1,0:T(8,128)(2,1)S(1)}) custom-call(s32[66]{0:T(128)S(1)} %pad_add_fusion.meta_ref, bf16[2,128,4096]{2,1,0:T(8,128)(2,1)S(1)} %collective-permute-done.7.side_ref, bf16[1,128,4096]{2,1,0:T(8,128)(2,1)S(1)} %collective-permute-done.8.grad_ref, ...), custom_call_target="tpu_custom_call" | custom-call | flops 1572864 | bytes 8388608 | tf_op jit(solution)/shard_map/gradients/pallas_call | solution.py:388
  120.8 3.6 %collective-permute-start.17 = (bf16[3,64,4096]{2,1,0:T(8,128)(2,1)S(1)}, bf16[3,64,4096]{2,1,0:T(8,128)(2,1)S(1)}, u32[]{:S(2)}, u32[]{:S(2)}) collective-permute-start(bf16[3,64,4096]{2,1,0:T(8,128)(2,1)S(1)} %get-tuple-element.53), channel_id=1, source_target_pairs={{0,1},{1,0},{2,3},{3,2},{4,5},{5,4},{6,7},{7,6},{8,9},{9,8},{10,11... | collective-permute-start | bytes 4718600 | tf_op jit(solution)/shard_map/ppermute | solution.py:508
  124.4 3.0 %collective-permute-done.17.cross_ref = bf16[3,64,4096]{2,1,0:T(8,128)(2,1)S(1)} collective-permute-done((bf16[3,64,4096]{2,1,0:T(8,128)(2,1)S(1)}, bf16[3,64,4096]{2,1,0:T(8,128)(2,1)S(1)}, u32[]{:S(2)}, u32[]{:S(2)}) %collective-permute-start.17) | collective-permute-done | bytes 1572896 | tf_op jit(solution)/shard_map/ppermute | solution.py:508
  127.4 1.8 %place.1 = bf16[1,3,64,8192]{3,2,1,0:T(8,128)(2,1)} custom-call(s32[66]{0:T(128)S(1)} %pad_add_fusion.meta_ref, bf16[3,64,4096]{2,1,0:T(8,128)(2,1)S(1)} %collective-permute-done.17.cross_ref, bf16[1,3,64,8192]{3,2,1,0:T(8,128)(2,1)} %get-tuple-element.54.held_ref), custom_call_target="tpu_custom_call", output_to_operand_aliasing={{}: (2, {})} | custom-call | bytes 3145728 | tf_op jit(solution)/shard_map/place/pallas_call | solution.py:411
  (9 shorter events, 0.0 us)
Async XLA Ops:
  0.0 38.6 %copy-start = (s32[2,64]{1,0:T(2,128)S(1)}, s32[2,64]{1,0:T(2,128)}, u32[]{:S(2)}) copy-start(s32[2,64]{1,0:T(2,128)} %param.7) | copy-start | bytes 1540
  2.8 73.6 %collective-permute-start.7 = (bf16[2,128,4096]{2,1,0:T(8,128)(2,1)}, bf16[2,128,4096]{2,1,0:T(8,128)(2,1)S(1)}, u32[]{:S(2)}, u32[]{:S(2)}) collective-permute-start(bf16[2,128,4096]{2,1,0:T(8,128)(2,1)} %get-tuple-element.41), channel_id=1, source_target_pairs={{0,16},{16,0},{1,17},{17,1},{2,18},{18,2},{3,19},{19,3},{4,20},{20... | collective-permute-start | bytes 6291464 | tf_op jit(solution)/shard_map/ppermute | solution.py:479
  8.5 49.5 %copy-start.1 = (bf16[1040,128]{1,0:T(8,128)(2,1)S(1)}, bf16[1040,128]{1,0:T(8,128)(2,1)}, u32[]{:S(2)}) copy-start(bf16[1040,128]{1,0:T(8,128)(2,1)} %get-tuple-element.30.refs_0_) | copy-start | bytes 798724
  8.5 16.9 %collective-permute-start = (bf16[1040,128]{1,0:T(8,128)(2,1)}, bf16[1040,128]{1,0:T(8,128)(2,1)S(1)}, u32[]{:S(2)}, u32[]{:S(2)}) collective-permute-start(bf16[1040,128]{1,0:T(8,128)(2,1)} %get-tuple-element.31), channel_id=1, source_target_pairs={{0,8},{2,10},{4,12},{6,14},{8,0},{10,2},{12,4},{14,6},{1,9},{3,11}... | collective-permute-start | bytes 798728 | tf_op jit(solution)/shard_map/ppermute | solution.py:431
  8.6 17.8 %collective-permute-start.1 = (bf16[1040,128]{1,0:T(8,128)(2,1)}, bf16[1040,128]{1,0:T(8,128)(2,1)}, u32[]{:S(2)}, u32[]{:S(2)}) collective-permute-start(bf16[1040,128]{1,0:T(8,128)(2,1)} %get-tuple-element.32), channel_id=1, source_target_pairs={{0,2},{2,0},{4,6},{6,4},{8,10},{10,8},{12,14},{14,12},{1,3},{3,1},... | collective-permute-start | bytes 798728 | tf_op jit(solution)/shard_map/ppermute | solution.py:431
  8.9 22.2 %collective-permute-start.2 = (bf16[1040,128]{1,0:T(8,128)(2,1)}, bf16[1040,128]{1,0:T(8,128)(2,1)}, u32[]{:S(2)}, u32[]{:S(2)}) collective-permute-start(bf16[1040,128]{1,0:T(8,128)(2,1)} %get-tuple-element.33), channel_id=1, source_target_pairs={{0,10},{2,8},{4,14},{6,12},{8,2},{10,0},{12,6},{14,4},{1,11},{3,9}... | collective-permute-start | bytes 798728 | tf_op jit(solution)/shard_map/ppermute | solution.py:431
  12.1 25.2 %collective-permute-start.3 = (bf16[1040,128]{1,0:T(8,128)(2,1)}, bf16[1040,128]{1,0:T(8,128)(2,1)}, u32[]{:S(2)}, u32[]{:S(2)}) collective-permute-start(bf16[1040,128]{1,0:T(8,128)(2,1)} %get-tuple-element.34), channel_id=1, source_target_pairs={{0,4},{2,6},{4,0},{6,2},{8,12},{10,14},{12,8},{14,10},{1,5},{3,7},... | collective-permute-start | bytes 798728 | tf_op jit(solution)/shard_map/ppermute | solution.py:431
  25.4 0.7 copy-start.2
  26.1 50.3 %collective-permute-start.8 = (bf16[1,128,4096]{2,1,0:T(8,128)(2,1)}, bf16[1,128,4096]{2,1,0:T(8,128)(2,1)S(1)}, u32[]{:S(2)}, u32[]{:S(2)}) collective-permute-start(bf16[1,128,4096]{2,1,0:T(8,128)(2,1)} %get-tuple-element.42), channel_id=1, source_target_pairs={{0,16},{16,0},{1,17},{17,1},{2,18},{18,2},{3,19},{19,3},{4,20},{20... | collective-permute-start | bytes 3145736 | tf_op jit(solution)/shard_map/ppermute | solution.py:479
  26.4 23.1 %collective-permute-start.4 = (bf16[1040,128]{1,0:T(8,128)(2,1)}, bf16[1040,128]{1,0:T(8,128)(2,1)}, u32[]{:S(2)}, u32[]{:S(2)}) collective-permute-start(bf16[1040,128]{1,0:T(8,128)(2,1)} %get-tuple-element.35), channel_id=1, source_target_pairs={{0,12},{2,14},{4,8},{6,10},{8,4},{10,6},{12,0},{14,2},{1,13},{3,15... | collective-permute-start | bytes 798728 | tf_op jit(solution)/shard_map/ppermute | solution.py:431
  31.1 18.4 %collective-permute-start.5 = (bf16[1040,128]{1,0:T(8,128)(2,1)}, bf16[1040,128]{1,0:T(8,128)(2,1)}, u32[]{:S(2)}, u32[]{:S(2)}) collective-permute-start(bf16[1040,128]{1,0:T(8,128)(2,1)} %get-tuple-element.36), channel_id=1, source_target_pairs={{0,6},{2,4},{4,2},{6,0},{8,14},{10,12},{12,10},{14,8},{1,7},{3,5},... | collective-permute-start | bytes 798728 | tf_op jit(solution)/shard_map/ppermute | solution.py:431
  37.3 20.7 %collective-permute-start.6 = (bf16[1040,128]{1,0:T(8,128)(2,1)}, bf16[1040,128]{1,0:T(8,128)(2,1)}, u32[]{:S(2)}, u32[]{:S(2)}) collective-permute-start(bf16[1040,128]{1,0:T(8,128)(2,1)} %get-tuple-element.37), channel_id=1, source_target_pairs={{0,14},{2,12},{4,10},{6,8},{8,6},{10,4},{12,2},{14,0},{1,15},{3,13... | collective-permute-start | bytes 798728 | tf_op jit(solution)/shard_map/ppermute | solution.py:431
  37.3 20.7 %copy-start.3 = (bf16[1040,128]{1,0:T(8,128)(2,1)S(1)}, bf16[1040,128]{1,0:T(8,128)(2,1)}, u32[]{:S(2)}) copy-start(bf16[1040,128]{1,0:T(8,128)(2,1)} %copy-done.2) | copy-start | bytes 798724
  71.9 17.1 %collective-permute-start.10 = (bf16[256,512]{1,0:T(8,128)(2,1)S(1)}, bf16[256,512]{1,0:T(8,128)(2,1)S(1)}, u32[]{:S(2)}, u32[]{:S(2)}) collective-permute-start(bf16[256,512]{1,0:T(8,128)(2,1)S(1)} %get-tuple-element.46), channel_id=1, source_target_pairs={{0,24},{2,26},{4,28},{6,30},{8,16},{10,18},{12,20},{14,22},{16,8},... | collective-permute-start | bytes 786440 | tf_op jit(solution)/shard_map/ppermute | solution.py:442
  72.0 25.7 %collective-permute-start.11 = (bf16[256,512]{1,0:T(8,128)(2,1)S(1)}, bf16[256,512]{1,0:T(8,128)(2,1)S(1)}, u32[]{:S(2)}, u32[]{:S(2)}) collective-permute-start(bf16[256,512]{1,0:T(8,128)(2,1)S(1)} %get-tuple-element.47), channel_id=1, source_target_pairs={{0,18},{2,16},{4,22},{6,20},{8,26},{10,24},{12,30},{14,28},{16,2},... | collective-permute-start | bytes 786440 | tf_op jit(solution)/shard_map/ppermute | solution.py:442
  73.3 30.1 %collective-permute-start.12 = (bf16[256,512]{1,0:T(8,128)(2,1)S(1)}, bf16[256,512]{1,0:T(8,128)(2,1)S(1)}, u32[]{:S(2)}, u32[]{:S(2)}) collective-permute-start(bf16[256,512]{1,0:T(8,128)(2,1)S(1)} %get-tuple-element.48), channel_id=1, source_target_pairs={{0,26},{2,24},{4,30},{6,28},{8,18},{10,16},{12,22},{14,20},{16,10}... | collective-permute-start | bytes 786440 | tf_op jit(solution)/shard_map/ppermute | solution.py:442
  76.4 29.1 %collective-permute-start.13 = (bf16[256,512]{1,0:T(8,128)(2,1)S(1)}, bf16[256,512]{1,0:T(8,128)(2,1)S(1)}, u32[]{:S(2)}, u32[]{:S(2)}) collective-permute-start(bf16[256,512]{1,0:T(8,128)(2,1)S(1)} %get-tuple-element.49), channel_id=1, source_target_pairs={{0,20},{2,22},{4,16},{6,18},{8,28},{10,30},{12,24},{14,26},{16,4},... | collective-permute-start | bytes 786440 | tf_op jit(solution)/shard_map/ppermute | solution.py:442
  76.4 42.0 %collective-permute-start.9 = (bf16[256,512]{1,0:T(8,128)(2,1)S(1)}, bf16[256,512]{1,0:T(8,128)(2,1)S(1)}, u32[]{:S(2)}, u32[]{:S(2)}) collective-permute-start(bf16[256,512]{1,0:T(8,128)(2,1)S(1)} %get-tuple-element.45), channel_id=1, source_target_pairs={{0,16},{2,18},{4,20},{6,22},{8,24},{10,26},{12,28},{14,30},{16,0},... | collective-permute-start | bytes 786440 | tf_op jit(solution)/shard_map/ppermute | solution.py:442
  89.1 29.4 %collective-permute-start.14 = (bf16[256,512]{1,0:T(8,128)(2,1)S(1)}, bf16[256,512]{1,0:T(8,128)(2,1)S(1)}, u32[]{:S(2)}, u32[]{:S(2)}) collective-permute-start(bf16[256,512]{1,0:T(8,128)(2,1)S(1)} %get-tuple-element.50), channel_id=1, source_target_pairs={{0,28},{2,30},{4,24},{6,26},{8,20},{10,22},{12,16},{14,18},{16,12}... | collective-permute-start | bytes 786440 | tf_op jit(solution)/shard_map/ppermute | solution.py:442
  97.7 20.7 %collective-permute-start.15 = (bf16[256,512]{1,0:T(8,128)(2,1)S(1)}, bf16[256,512]{1,0:T(8,128)(2,1)S(1)}, u32[]{:S(2)}, u32[]{:S(2)}) collective-permute-start(bf16[256,512]{1,0:T(8,128)(2,1)S(1)} %get-tuple-element.51), channel_id=1, source_target_pairs={{0,22},{2,20},{4,18},{6,16},{8,30},{10,28},{12,26},{14,24},{16,6},... | collective-permute-start | bytes 786440 | tf_op jit(solution)/shard_map/ppermute | solution.py:442
  103.4 15.1 %collective-permute-start.16 = (bf16[256,512]{1,0:T(8,128)(2,1)S(1)}, bf16[256,512]{1,0:T(8,128)(2,1)S(1)}, u32[]{:S(2)}, u32[]{:S(2)}) collective-permute-start(bf16[256,512]{1,0:T(8,128)(2,1)S(1)} %get-tuple-element.52), channel_id=1, source_target_pairs={{0,30},{2,28},{4,26},{6,24},{8,22},{10,20},{12,18},{14,16},{16,14}... | collective-permute-start | bytes 786440 | tf_op jit(solution)/shard_map/ppermute | solution.py:442
  120.8 6.6 %collective-permute-start.17 = (bf16[3,64,4096]{2,1,0:T(8,128)(2,1)S(1)}, bf16[3,64,4096]{2,1,0:T(8,128)(2,1)S(1)}, u32[]{:S(2)}, u32[]{:S(2)}) collective-permute-start(bf16[3,64,4096]{2,1,0:T(8,128)(2,1)S(1)} %get-tuple-element.53), channel_id=1, source_target_pairs={{0,1},{1,0},{2,3},{3,2},{4,5},{5,4},{6,7},{7,6},{8,9},{9,8},{10,11... | collective-permute-start | bytes 4718600 | tf_op jit(solution)/shard_map/ppermute | solution.py:508

commit v8 on v6

--- a/solution.py
+++ b/solution.py
@@ -138,8 +138,8 @@
         out_specs=anywhere,
         scratch_shapes=[
             pltpu.VMEM((3, rows, channels), BF16),
-            pltpu.SemaphoreType.DMA((3, 2)),
-            pltpu.SemaphoreType.DMA((3, 2)),
+            pltpu.SemaphoreType.DMA((3, 4)),
+            pltpu.SemaphoreType.DMA((3, 4)),
         ],
         compiler_params=params(60),
         cost_estimate=pl.CostEstimate(
@@ -406,6 +406,68 @@
 
 
 def place(chunk, chunks, tp_at, meta, cross, result):
+    three, part, span = cross.shape
+
+    def other(i, meta_ref):
+        return (0, i, 0, (1 - meta_ref[tp_at]) * chunks + chunk)
+
+    return pl.pallas_call(
+        place_kernel,
+        out_shape=jax.ShapeDtypeStruct(result.shape, BF16),
+        grid_spec=pltpu.PrefetchScalarGridSpec(
+            num_scalar_prefetch=1,
+            grid=(three,),
+            in_specs=[
+                pl.BlockSpec((1, part, span), lambda i, _: (i, 0, 0)),
+                pl.BlockSpec(memory_space=pl.ANY),
+            ],
+            out_specs=pl.BlockSpec((1, 1, part, span), other),
+        ),
+        input_output_aliases={2: 0},
+        compiler_params=params(24),
+        cost_estimate=pl.CostEstimate(
+            flops=0, bytes_accessed=4 * math.prod(cross.shape), transcendentals=0
+        ),
+        name="place",
+    )(meta, cross, result)
+
+
+def gradients(chunk, chunks, me_at, tp_at, tp_count, meta, backs, side, others):
+    peers = len(backs)
+    _, rows, channels = side.shape
+    span = channels // chunks
+    out = (3, rows // tp_count, span)
+    whole = (1, 3, rows // tp_count, channels * tp_count)
+    in_specs = [pl.BlockSpec((3, rows, span), lambda _, meta_ref: (0, 0, chunk))]
+    in_specs += [fixed(backs[0].shape)] * peers
+    args = [meta, side, *backs]
+    aliases = {} if chunk == 0 else {len(args): 0}
+    for other in others:
+        args.append(other)
+        in_specs.append(pl.BlockSpec(memory_space=pl.ANY))
+    return pl.pallas_call(
+        functools.partial(gradients_kernel, me_at, tp_at, peers),
+        out_shape=[jax.ShapeDtypeStruct(whole, BF16), jax.ShapeDtypeStruct(out, BF16)],
+        grid_spec=pltpu.PrefetchScalarGridSpec(
+            num_scalar_prefetch=1,
+            grid=(1,),
+            in_specs=in_specs,
+            out_specs=[result_block(out, chunk, chunks, tp_at, True), fixed(out)],
+        ),
+        input_output_aliases=aliases,
+        compiler_params=params(24),
+        cost_estimate=pl.CostEstimate(
+            flops=3 * rows * span, bytes_accessed=16 * rows * span, transcendentals=0
+        ),
+        name="gradients",
+    )(*args)
+
+
+def place_kernel(meta_ref, cross_ref, held_ref, result_ref):
+    result_ref[0] = cross_ref[...]
+
+
+def place(chunk, chunks, tp_at, meta, cross, result):
     return pl.pallas_call(
         place_kernel,
         out_shape=jax.ShapeDtypeStruct(result.shape, BF16),

time: 131 us -> 131 us (level)
  no operation moved by 1% of the time
where the time goes in v8:
time: 131 us; the launch traced here: 130 us
  waiting for transfers between devices  70 us (53%)
  starting transfers between devices  32.7 us (25%)
  Pallas kernels  26.7 us (20%)
    ppermute x8, waiting for transfers between devices, swap_to_previous(): return lax.ppermute(array, ('pipe', 'ctx'), pairs)  38.2 us
    ppermute x7, waiting for transfers between devices, swap(): lax.ppermute(array, 'ctx', [(i, i ^ k) for i in range(peers)])  28.7 us
    ppermute x7, starting transfers between devices, swap(): lax.ppermute(array, 'ctx', [(i, i ^ k) for i in range(peers)])  18.6 us
    pallas_call x1, Pallas kernels, convolve(): pl.pallas_call(functools.partial(conv_kernel, group_size, me_at, peers),...  12.7 us
    ppermute x8, starting transfers between devices, swap_to_previous(): return lax.ppermute(array, ('pipe', 'ctx'), pairs)  11 us
    pallas_call x1, Pallas kernels, multiply(): pl.pallas_call(functools.partial(multiply_kernel, chunks), out_shape=[jax...  4.36 us
    ppermute x1, waiting for transfers between devices, shards(): held.append(lax.ppermute(cross, 'tp', [(0, 1), (1, 0)]))  3.04 us
    pallas_call x1, Pallas kernels, side_of(): pl.pallas_call(side_kernel, out_shape=jax.ShapeDtypeStruct((3, rows, chan...  2.82 us
  transfers between devices with their start and end apart: 17, of which 9 were waited for; matrix products, arithmetic and copies ran while one was open for 1% of the time, Pallas kernels for 15%

profile of v8, /device:TPU:21, one launch (start us, length us, event | category | flops | bytes accessed | tf_op | source)
XLA Modules:
  0.0 130.4 jit_solution(9350318024183459830)
XLA Ops:
  0.0 0.0 copy-start
  0.0 2.8 %side.1 = bf16[3,128,4096]{2,1,0:T(8,128)(2,1)} custom-call(bf16[1,3,128,4096]{3,2,1,0:T(8,128)(2,1)} %proj_ref.3, bf16[1,128,4096]{2,1,0:T(8,128)(2,1)} %grad_ref.3), custom_call_target="tpu_custom_call" | custom-call | bytes 6291456 | tf_op jit(solution)/shard_map/side/pallas_call | solution.py:134
  2.8 1.3 collective-permute-start.7
  4.1 4.4 %multiply.1 = (bf16[1040,128]{1,0:T(8,128)(2,1)}, bf16[1040,128]{1,0:T(8,128)(2,1)}, bf16[1040,128]{1,0:T(8,128)(2,1)}, bf16[1040,128]{1,0:T(8,128)(2,1)}, bf16[...) custom-call(bf16[1,3,128,4096]{3,2,1,0:T(8,128)(2,1)} %proj_ref.3, ...), custom_call_target="tpu_custom_call" | custom-call | flops 1048576 | bytes 6291456 | tf_op jit(solution)/shard_map/multiply/pallas_call | solution.py:88
  8.5 0.0 copy-start.1
  8.5 0.1 collective-permute-start
  8.6 0.2 collective-permute-start.1
  8.9 3.2 %collective-permute-start.2 = (bf16[1040,128]{1,0:T(8,128)(2,1)}, bf16[1040,128]{1,0:T(8,128)(2,1)}, u32[]{:S(2)}, u32[]{:S(2)}) collective-permute-start(bf16[1040,128]{1,0:T(8,128)(2,1)} %get-tuple-element.30), channel_id=1, source_target_pairs={{0,10},{2,8},{4,14},{6,12},{8,2},{10,0},{12,6},{14,4},{1,11},{3,9}... | collective-permute-start | bytes 798728 | tf_op jit(solution)/shard_map/ppermute | solution.py:491
  12.1 1.3 collective-permute-start.3
  13.4 0.7 convert_bitcast_fusion
  14.1 0.1 rev.3
  14.2 0.1 pad_bitcast_fusion
  14.3 11.1 %collective-permute-done.refs_1_ = bf16[1040,128]{1,0:T(8,128)(2,1)} collective-permute-done((bf16[1040,128]{1,0:T(8,128)(2,1)}, bf16[1040,128]{1,0:T(8,128)(2,1)}, u32[]{:S(2)}, u32[]{:S(2)}) %collective-permute-start) | collective-permute-done | bytes 266272 | tf_op jit(solution)/shard_map/ppermute | solution.py:491
  25.4 3.4 %collective-permute-start.4 = (bf16[1040,128]{1,0:T(8,128)(2,1)}, bf16[1040,128]{1,0:T(8,128)(2,1)}, u32[]{:S(2)}, u32[]{:S(2)}) collective-permute-start(bf16[1040,128]{1,0:T(8,128)(2,1)} %get-tuple-element.32), channel_id=1, source_target_pairs={{0,12},{2,14},{4,8},{6,10},{8,4},{10,6},{12,0},{14,2},{1,13},{3,15... | collective-permute-start | bytes 798728 | tf_op jit(solution)/shard_map/ppermute | solution.py:491
  28.8 0.0 collective-permute-done.1.refs_2_
  28.8 1.9 %collective-permute-start.5 = (bf16[1040,128]{1,0:T(8,128)(2,1)}, bf16[1040,128]{1,0:T(8,128)(2,1)}, u32[]{:S(2)}, u32[]{:S(2)}) collective-permute-start(bf16[1040,128]{1,0:T(8,128)(2,1)} %get-tuple-element.33), channel_id=1, source_target_pairs={{0,6},{2,4},{4,2},{6,0},{8,14},{10,12},{12,10},{14,8},{1,7},{3,5},... | collective-permute-start | bytes 798728 | tf_op jit(solution)/shard_map/ppermute | solution.py:491
  30.6 0.5 collective-permute-done.2.refs_3_
  31.1 8.4 %collective-permute-start.6 = (bf16[1040,128]{1,0:T(8,128)(2,1)}, bf16[1040,128]{1,0:T(8,128)(2,1)}, u32[]{:S(2)}, u32[]{:S(2)}) collective-permute-start(bf16[1040,128]{1,0:T(8,128)(2,1)} %get-tuple-element.34), channel_id=1, source_target_pairs={{0,14},{2,12},{4,10},{6,8},{8,6},{10,4},{12,2},{14,0},{1,15},{3,13... | collective-permute-start | bytes 798728 | tf_op jit(solution)/shard_map/ppermute | solution.py:491
  39.5 1.2 toeplitz.1.toep_ref
  40.7 0.0 copy-done
  40.8 0.1 pad_add_fusion.meta_ref
  40.9 0.0 collective-permute-done.3.refs_4_
  40.9 11.5 %collective-permute-done.4.refs_5_ = bf16[1040,128]{1,0:T(8,128)(2,1)} collective-permute-done((bf16[1040,128]{1,0:T(8,128)(2,1)}, bf16[1040,128]{1,0:T(8,128)(2,1)}, u32[]{:S(2)}, u32[]{:S(2)}) %collective-permute-start.4) | collective-permute-done | bytes 266272 | tf_op jit(solution)/shard_map/ppermute | solution.py:491
  52.4 0.0 collective-permute-done.5.refs_6_
  52.4 5.6 %collective-permute-done.6.refs_7_ = bf16[1040,128]{1,0:T(8,128)(2,1)} collective-permute-done((bf16[1040,128]{1,0:T(8,128)(2,1)}, bf16[1040,128]{1,0:T(8,128)(2,1)}, u32[]{:S(2)}, u32[]{:S(2)}) %collective-permute-start.6) | collective-permute-done | bytes 266272 | tf_op jit(solution)/shard_map/ppermute | solution.py:491
  58.0 1.5 %masks.1.mask_ref = bf16[8,2,128,256]{3,2,1,0:T(8,128)(2,1)S(1)} custom-call(s32[66]{0:T(128)S(1)} %pad_add_fusion.meta_ref, bf16[1040,128]{1,0:T(8,128)(2,1)S(1)} %copy-done.1, bf16[1040,128]{1,0:T(8,128)(2,1)} %collective-permute-done.refs_1_, bf16[1040,128]{1,0:T(8,128)(2,1)} %collective-permute-done.1.refs_2_, ...), custom_call_target="tpu_custom_call" | custom-call | flops 1048576 | bytes 1048576 | tf_op jit(solution)/shard_map/masks/pallas_call | solution.py:204
  59.5 12.7 %convolve.1 = (bf16[256,512]{1,0:T(8,128)(2,1)S(1)}, bf16[256,512]{1,0:T(8,128)(2,1)S(1)}, bf16[256,512]{1,0:T(8,128)(2,1)S(1)}, bf16[256,512]{1,0:T(8,128)(2,1)...) custom-call(s32[66]{0:T(128)S(1)} %pad_add_fusion.meta_ref, ...), custom_call_target="tpu_custom_call" | custom-call | flops 4294967296 | bytes 4718592 | tf_op jit(solution)/shard_map/convolve/pallas_call | solution.py:314
  72.2 1.3 collective-permute-start.10
  73.4 0.0 collective-permute-start.11
  73.4 1.3 %collective-permute-start.12 = (bf16[256,512]{1,0:T(8,128)(2,1)S(1)}, bf16[256,512]{1,0:T(8,128)(2,1)S(1)}, u32[]{:S(2)}, u32[]{:S(2)}) collective-permute-start(bf16[256,512]{1,0:T(8,128)(2,1)S(1)} %get-tuple-element.43), channel_id=1, source_target_pairs={{0,20},{2,22},{4,16},{6,18},{8,28},{10,30},{12,24},{14,26},{16,4},... | collective-permute-start | bytes 786440 | tf_op jit(solution)/shard_map/ppermute | solution.py:502
  74.8 1.2 collective-permute-start.8
  76.0 0.0 collective-permute-done.7.side_ref
  76.0 1.9 %collective-permute-start.9 = (bf16[256,512]{1,0:T(8,128)(2,1)S(1)}, bf16[256,512]{1,0:T(8,128)(2,1)S(1)}, u32[]{:S(2)}, u32[]{:S(2)}) collective-permute-start(bf16[256,512]{1,0:T(8,128)(2,1)S(1)} %get-tuple-element.40), channel_id=1, source_target_pairs={{0,24},{2,26},{4,28},{6,30},{8,16},{10,18},{12,20},{14,22},{16,8},... | collective-permute-start | bytes 786440 | tf_op jit(solution)/shard_map/ppermute | solution.py:502
  77.9 17.6 %collective-permute-done.10.refs_2_ = bf16[256,512]{1,0:T(8,128)(2,1)S(1)} collective-permute-done((bf16[256,512]{1,0:T(8,128)(2,1)S(1)}, bf16[256,512]{1,0:T(8,128)(2,1)S(1)}, u32[]{:S(2)}, u32[]{:S(2)}) %collective-permute-start.10) | collective-permute-done | bytes 262176 | tf_op jit(solution)/shard_map/ppermute | solution.py:502
  95.5 0.0 collective-permute-start.13
  95.5 0.0 collective-permute-done.11.refs_3_
  95.5 0.0 collective-permute-start.14
  95.5 0.0 collective-permute-done.12.refs_4_
  95.5 5.3 %collective-permute-start.15 = (bf16[256,512]{1,0:T(8,128)(2,1)S(1)}, bf16[256,512]{1,0:T(8,128)(2,1)S(1)}, u32[]{:S(2)}, u32[]{:S(2)}) collective-permute-start(bf16[256,512]{1,0:T(8,128)(2,1)S(1)} %get-tuple-element.46), channel_id=1, source_target_pairs={{0,30},{2,28},{4,26},{6,24},{8,22},{10,20},{12,18},{14,16},{16,14}... | collective-permute-start | bytes 786440 | tf_op jit(solution)/shard_map/ppermute | solution.py:502
  100.8 12.7 %collective-permute-done.8.refs_0_ = bf16[256,512]{1,0:T(8,128)(2,1)S(1)} collective-permute-done((bf16[256,512]{1,0:T(8,128)(2,1)S(1)}, bf16[256,512]{1,0:T(8,128)(2,1)S(1)}, u32[]{:S(2)}, u32[]{:S(2)}) %collective-permute-start.8) | collective-permute-done | bytes 262176 | tf_op jit(solution)/shard_map/ppermute | solution.py:502
  113.5 0.0 collective-permute-done.9.refs_1_
  113.5 1.5 %collective-permute-done.13.refs_5_ = bf16[256,512]{1,0:T(8,128)(2,1)S(1)} collective-permute-done((bf16[256,512]{1,0:T(8,128)(2,1)S(1)}, bf16[256,512]{1,0:T(8,128)(2,1)S(1)}, u32[]{:S(2)}, u32[]{:S(2)}) %collective-permute-start.13) | collective-permute-done | bytes 262176 | tf_op jit(solution)/shard_map/ppermute | solution.py:502
  115.0 0.0 collective-permute-done.14.refs_6_
  115.0 6.3 %collective-permute-done.15.refs_7_ = bf16[256,512]{1,0:T(8,128)(2,1)S(1)} collective-permute-done((bf16[256,512]{1,0:T(8,128)(2,1)S(1)}, bf16[256,512]{1,0:T(8,128)(2,1)S(1)}, u32[]{:S(2)}, u32[]{:S(2)}) %collective-permute-start.15) | collective-permute-done | bytes 262176 | tf_op jit(solution)/shard_map/ppermute | solution.py:502
  121.4 2.3 %gradients.1 = (bf16[1,3,64,8192]{3,2,1,0:T(8,128)(2,1)}, bf16[3,64,4096]{2,1,0:T(8,128)(2,1)S(1)}) custom-call(s32[66]{0:T(128)S(1)} %pad_add_fusion.meta_ref, bf16[3,128,4096]{2,1,0:T(8,128)(2,1)S(1)} %collective-permute-done.7.side_ref, bf16[256,512]{1,0:T(8,128)(2,1)S(1)} %collective-permute-done.8.refs_0_, ...), custom_call_target="tpu_custom_call" | custom-call | flops 1572864 | bytes 8388608 | tf_op jit(solution)/shard_map/gradients/pallas_call | solution.py:448
  123.7 1.9 %collective-permute-start.16 = (bf16[3,64,4096]{2,1,0:T(8,128)(2,1)S(1)}, bf16[3,64,4096]{2,1,0:T(8,128)(2,1)S(1)}, u32[]{:S(2)}, u32[]{:S(2)}) collective-permute-start(bf16[3,64,4096]{2,1,0:T(8,128)(2,1)S(1)} %get-tuple-element.47), channel_id=1, source_target_pairs={{0,1},{1,0},{2,3},{3,2},{4,5},{5,4},{6,7},{7,6},{8,9},{9,8},{10,11... | collective-permute-start | bytes 4718600 | tf_op jit(solution)/shard_map/ppermute | solution.py:566
  125.6 3.0 %collective-permute-done.16.cross_ref = bf16[3,64,4096]{2,1,0:T(8,128)(2,1)S(1)} collective-permute-done((bf16[3,64,4096]{2,1,0:T(8,128)(2,1)S(1)}, bf16[3,64,4096]{2,1,0:T(8,128)(2,1)S(1)}, u32[]{:S(2)}, u32[]{:S(2)}) %collective-permute-start.16) | collective-permute-done | bytes 1572896 | tf_op jit(solution)/shard_map/ppermute | solution.py:566
  128.7 1.8 %place.1 = bf16[1,3,64,8192]{3,2,1,0:T(8,128)(2,1)} custom-call(s32[66]{0:T(128)S(1)} %pad_add_fusion.meta_ref, bf16[3,64,4096]{2,1,0:T(8,128)(2,1)S(1)} %collective-permute-done.16.cross_ref, bf16[1,3,64,8192]{3,2,1,0:T(8,128)(2,1)} %get-tuple-element.48.held_ref), custom_call_target="tpu_custom_call", output_to_operand_aliasing={{}: (2, {})} | custom-call | bytes 3145728 | tf_op jit(solution)/shard_map/place/pallas_call | solution.py:471
  (3 shorter events, 0.0 us)
Async XLA Ops:
  0.0 40.7 %copy-start = (s32[2,64]{1,0:T(2,128)S(1)}, s32[2,64]{1,0:T(2,128)}, u32[]{:S(2)}) copy-start(s32[2,64]{1,0:T(2,128)} %param.7) | copy-start | bytes 1540
  2.8 73.2 %collective-permute-start.7 = (bf16[3,128,4096]{2,1,0:T(8,128)(2,1)}, bf16[3,128,4096]{2,1,0:T(8,128)(2,1)S(1)}, u32[]{:S(2)}, u32[]{:S(2)}) collective-permute-start(bf16[3,128,4096]{2,1,0:T(8,128)(2,1)} %side.1), channel_id=1, source_target_pairs={{0,16},{16,0},{1,17},{17,1},{2,18},{18,2},{3,19},{19,3},{4,20},{20... | collective-permute-start | bytes 9437192 | tf_op jit(solution)/shard_map/ppermute | solution.py:538
  8.5 49.5 %copy-start.1 = (bf16[1040,128]{1,0:T(8,128)(2,1)S(1)}, bf16[1040,128]{1,0:T(8,128)(2,1)}, u32[]{:S(2)}) copy-start(bf16[1040,128]{1,0:T(8,128)(2,1)} %get-tuple-element.27.refs_0_) | copy-start | bytes 798724
  8.5 16.9 %collective-permute-start = (bf16[1040,128]{1,0:T(8,128)(2,1)}, bf16[1040,128]{1,0:T(8,128)(2,1)}, u32[]{:S(2)}, u32[]{:S(2)}) collective-permute-start(bf16[1040,128]{1,0:T(8,128)(2,1)} %get-tuple-element.28), channel_id=1, source_target_pairs={{0,8},{2,10},{4,12},{6,14},{8,0},{10,2},{12,4},{14,6},{1,9},{3,11}... | collective-permute-start | bytes 798728 | tf_op jit(solution)/shard_map/ppermute | solution.py:491
  8.6 20.2 %collective-permute-start.1 = (bf16[1040,128]{1,0:T(8,128)(2,1)}, bf16[1040,128]{1,0:T(8,128)(2,1)}, u32[]{:S(2)}, u32[]{:S(2)}) collective-permute-start(bf16[1040,128]{1,0:T(8,128)(2,1)} %get-tuple-element.29), channel_id=1, source_target_pairs={{0,2},{2,0},{4,6},{6,4},{8,10},{10,8},{12,14},{14,12},{1,3},{3,1},... | collective-permute-start | bytes 798728 | tf_op jit(solution)/shard_map/ppermute | solution.py:491
  8.9 22.2 %collective-permute-start.2 = (bf16[1040,128]{1,0:T(8,128)(2,1)}, bf16[1040,128]{1,0:T(8,128)(2,1)}, u32[]{:S(2)}, u32[]{:S(2)}) collective-permute-start(bf16[1040,128]{1,0:T(8,128)(2,1)} %get-tuple-element.30), channel_id=1, source_target_pairs={{0,10},{2,8},{4,14},{6,12},{8,2},{10,0},{12,6},{14,4},{1,11},{3,9}... | collective-permute-start | bytes 798728 | tf_op jit(solution)/shard_map/ppermute | solution.py:491
  12.1 28.8 %collective-permute-start.3 = (bf16[1040,128]{1,0:T(8,128)(2,1)}, bf16[1040,128]{1,0:T(8,128)(2,1)}, u32[]{:S(2)}, u32[]{:S(2)}) collective-permute-start(bf16[1040,128]{1,0:T(8,128)(2,1)} %get-tuple-element.31), channel_id=1, source_target_pairs={{0,4},{2,6},{4,0},{6,2},{8,12},{10,14},{12,8},{14,10},{1,5},{3,7},... | collective-permute-start | bytes 798728 | tf_op jit(solution)/shard_map/ppermute | solution.py:491
  25.4 27.0 %collective-permute-start.4 = (bf16[1040,128]{1,0:T(8,128)(2,1)}, bf16[1040,128]{1,0:T(8,128)(2,1)}, u32[]{:S(2)}, u32[]{:S(2)}) collective-permute-start(bf16[1040,128]{1,0:T(8,128)(2,1)} %get-tuple-element.32), channel_id=1, source_target_pairs={{0,12},{2,14},{4,8},{6,10},{8,4},{10,6},{12,0},{14,2},{1,13},{3,15... | collective-permute-start | bytes 798728 | tf_op jit(solution)/shard_map/ppermute | solution.py:491
  28.8 23.6 %collective-permute-start.5 = (bf16[1040,128]{1,0:T(8,128)(2,1)}, bf16[1040,128]{1,0:T(8,128)(2,1)}, u32[]{:S(2)}, u32[]{:S(2)}) collective-permute-start(bf16[1040,128]{1,0:T(8,128)(2,1)} %get-tuple-element.33), channel_id=1, source_target_pairs={{0,6},{2,4},{4,2},{6,0},{8,14},{10,12},{12,10},{14,8},{1,7},{3,5},... | collective-permute-start | bytes 798728 | tf_op jit(solution)/shard_map/ppermute | solution.py:491
  31.1 26.9 %collective-permute-start.6 = (bf16[1040,128]{1,0:T(8,128)(2,1)}, bf16[1040,128]{1,0:T(8,128)(2,1)}, u32[]{:S(2)}, u32[]{:S(2)}) collective-permute-start(bf16[1040,128]{1,0:T(8,128)(2,1)} %get-tuple-element.34), channel_id=1, source_target_pairs={{0,14},{2,12},{4,10},{6,8},{8,6},{10,4},{12,2},{14,0},{1,15},{3,13... | collective-permute-start | bytes 798728 | tf_op jit(solution)/shard_map/ppermute | solution.py:491
  72.2 23.3 %collective-permute-start.10 = (bf16[256,512]{1,0:T(8,128)(2,1)S(1)}, bf16[256,512]{1,0:T(8,128)(2,1)S(1)}, u32[]{:S(2)}, u32[]{:S(2)}) collective-permute-start(bf16[256,512]{1,0:T(8,128)(2,1)S(1)} %get-tuple-element.41), channel_id=1, source_target_pairs={{0,18},{2,16},{4,22},{6,20},{8,26},{10,24},{12,30},{14,28},{16,2},... | collective-permute-start | bytes 786440 | tf_op jit(solution)/shard_map/ppermute | solution.py:502
  73.4 22.0 %collective-permute-start.11 = (bf16[256,512]{1,0:T(8,128)(2,1)S(1)}, bf16[256,512]{1,0:T(8,128)(2,1)S(1)}, u32[]{:S(2)}, u32[]{:S(2)}) collective-permute-start(bf16[256,512]{1,0:T(8,128)(2,1)S(1)} %get-tuple-element.42), channel_id=1, source_target_pairs={{0,26},{2,24},{4,30},{6,28},{8,18},{10,16},{12,22},{14,20},{16,10}... | collective-permute-start | bytes 786440 | tf_op jit(solution)/shard_map/ppermute | solution.py:502
  73.4 22.0 %collective-permute-start.12 = (bf16[256,512]{1,0:T(8,128)(2,1)S(1)}, bf16[256,512]{1,0:T(8,128)(2,1)S(1)}, u32[]{:S(2)}, u32[]{:S(2)}) collective-permute-start(bf16[256,512]{1,0:T(8,128)(2,1)S(1)} %get-tuple-element.43), channel_id=1, source_target_pairs={{0,20},{2,22},{4,16},{6,18},{8,28},{10,30},{12,24},{14,26},{16,4},... | collective-permute-start | bytes 786440 | tf_op jit(solution)/shard_map/ppermute | solution.py:502
  74.8 38.7 %collective-permute-start.8 = (bf16[256,512]{1,0:T(8,128)(2,1)S(1)}, bf16[256,512]{1,0:T(8,128)(2,1)S(1)}, u32[]{:S(2)}, u32[]{:S(2)}) collective-permute-start(bf16[256,512]{1,0:T(8,128)(2,1)S(1)} %get-tuple-element.39), channel_id=1, source_target_pairs={{0,16},{2,18},{4,20},{6,22},{8,24},{10,26},{12,28},{14,30},{16,0},... | collective-permute-start | bytes 786440 | tf_op jit(solution)/shard_map/ppermute | solution.py:502
  76.0 37.5 %collective-permute-start.9 = (bf16[256,512]{1,0:T(8,128)(2,1)S(1)}, bf16[256,512]{1,0:T(8,128)(2,1)S(1)}, u32[]{:S(2)}, u32[]{:S(2)}) collective-permute-start(bf16[256,512]{1,0:T(8,128)(2,1)S(1)} %get-tuple-element.40), channel_id=1, source_target_pairs={{0,24},{2,26},{4,28},{6,30},{8,16},{10,18},{12,20},{14,22},{16,8},... | collective-permute-start | bytes 786440 | tf_op jit(solution)/shard_map/ppermute | solution.py:502
  95.5 19.6 %collective-permute-start.13 = (bf16[256,512]{1,0:T(8,128)(2,1)S(1)}, bf16[256,512]{1,0:T(8,128)(2,1)S(1)}, u32[]{:S(2)}, u32[]{:S(2)}) collective-permute-start(bf16[256,512]{1,0:T(8,128)(2,1)S(1)} %get-tuple-element.44), channel_id=1, source_target_pairs={{0,28},{2,30},{4,24},{6,26},{8,20},{10,22},{12,16},{14,18},{16,12}... | collective-permute-start | bytes 786440 | tf_op jit(solution)/shard_map/ppermute | solution.py:502
  95.5 19.6 %collective-permute-start.14 = (bf16[256,512]{1,0:T(8,128)(2,1)S(1)}, bf16[256,512]{1,0:T(8,128)(2,1)S(1)}, u32[]{:S(2)}, u32[]{:S(2)}) collective-permute-start(bf16[256,512]{1,0:T(8,128)(2,1)S(1)} %get-tuple-element.45), channel_id=1, source_target_pairs={{0,22},{2,20},{4,18},{6,16},{8,30},{10,28},{12,26},{14,24},{16,6},... | collective-permute-start | bytes 786440 | tf_op jit(solution)/shard_map/ppermute | solution.py:502
  95.5 25.9 %collective-permute-start.15 = (bf16[256,512]{1,0:T(8,128)(2,1)S(1)}, bf16[256,512]{1,0:T(8,128)(2,1)S(1)}, u32[]{:S(2)}, u32[]{:S(2)}) collective-permute-start(bf16[256,512]{1,0:T(8,128)(2,1)S(1)} %get-tuple-element.46), channel_id=1, source_target_pairs={{0,30},{2,28},{4,26},{6,24},{8,22},{10,20},{12,18},{14,16},{16,14}... | collective-permute-start | bytes 786440 | tf_op jit(solution)/shard_map/ppermute | solution.py:502
  123.7 5.0 %collective-permute-start.16 = (bf16[3,64,4096]{2,1,0:T(8,128)(2,1)S(1)}, bf16[3,64,4096]{2,1,0:T(8,128)(2,1)S(1)}, u32[]{:S(2)}, u32[]{:S(2)}) collective-permute-start(bf16[3,64,4096]{2,1,0:T(8,128)(2,1)S(1)} %get-tuple-element.47), channel_id=1, source_target_pairs={{0,1},{1,0},{2,3},{3,2},{4,5},{5,4},{6,7},{7,6},{8,9},{9,8},{10,11... | collective-permute-start | bytes 4718600 | tf_op jit(solution)/shard_map/ppermute | solution.py:566
